TPU v7x, 32 devices: a whole 2x2x4 slice. The times are simulated.
32 devices in a mesh: wide: 8 (over z, x), head: 4 (over y, core).
Axes of the slice: x: 2, y: 2, z: 4, core: 2. Of those that a mesh axis runs over, the one named last changes fastest.
Arguments:
- tokens_a: bfloat16 [1024, 768], P(('wide', 'head')), may hold values from -6 to 6
- tokens_b: bfloat16 [2048, 768], P(('wide', 'head')), may hold values from -6 to 6
- tokens_c: bfloat16 [4096, 768], P(('wide', 'head')), may hold values from -6 to 6
- lengths_a: int32 [8], P('wide'), may hold values from 65 to 128, as said below
- lengths_b: int32 [8], P('wide'), may hold values from 129 to 256, as said below
- lengths_c: int32 [8], P('wide'), may hold values from 257 to 512, as said below
- cotan_a: bfloat16 [1024, 768], P(('wide', 'head')), may hold values from -6 to 6
- cotan_b: bfloat16 [2048, 768], P(('wide', 'head')), may hold values from -6 to 6
- cotan_c: bfloat16 [4096, 768], P(('wide', 'head')), may hold values from -6 to 6
- ln_gain: float32 [2, 2, 768], replicated, may hold values from 0.5 to 1.5
- ln_bias: float32 [2, 2, 768], replicated, may hold values from -1.2 to 1.2
- row_bias: float32 [2, 2, 768], replicated, may hold values from -1.2 to 1.2
- out_weight: bfloat16 [2, 768, 768], P(None, ('wide', 'head')), may hold values from -1.75 to 1.75
- up_weight: bfloat16 [2, 3072, 768], P(None, ('wide', 'head')), may hold values from -0.21875 to 0.21875
- up_bias: float32 [2, 3072], P(None, ('wide', 'head')), may hold values from -1.2 to 1.2
- down_weight: bfloat16 [2, 3072, 768], P(None, ('wide', 'head')), may hold values from -0.109375 to 0.109375
- synth_first: bfloat16 [12, 64, 64], P('head'), may hold values from -0.75 to 0.75
- synth_first_bias: float32 [12, 64], P('head'), may hold values from -3 to 3
- synth_second: bfloat16 [12, 64, 512], P('head'), may hold values from -1.5 to 1.5
- synth_second_bias: float32 [12, 512], P('head'), may hold values from -3 to 3
- random_scores: bfloat16 [12, 512, 512], P('head'), may hold values from -9 to 9
- value_weight: bfloat16 [2, 12, 64, 64], P(None, 'head'), may hold values from -0.75 to 0.75
Outputs:
- out_a: bfloat16 [1024, 768], P(('wide', 'head'))
- out_b: bfloat16 [2048, 768], P(('wide', 'head'))
- out_c: bfloat16 [4096, 768], P(('wide', 'head'))
- grad_a: float32 [1024, 768], P(('wide', 'head'))
- grad_b: float32 [2048, 768], P(('wide', 'head'))
- grad_c: float32 [4096, 768], P(('wide', 'head'))
- grad_ln_gain: float32 [2, 2, 768], replicated
- grad_ln_bias: float32 [2, 2, 768], replicated
- grad_row_bias: float32 [2, 2, 768], replicated
- grad_out_weight: float32 [2, 768, 768], P(None, ('wide', 'head'))
- grad_up_weight: float32 [2, 3072, 768], P(None, ('wide', 'head'))
- grad_up_bias: float32 [2, 3072], P(None, ('wide', 'head'))
- grad_down_weight: float32 [2, 3072, 768], P(None, ('wide', 'head'))
- grad_synth_first: float32 [12, 64, 64], P('head', 'wide')
- grad_synth_first_bias: float32 [12, 64], P('head', 'wide')
- grad_synth_second: float32 [12, 64, 512], P('head', 'wide')
- grad_synth_second_bias: float32 [12, 512], P('head', 'wide')
- grad_random_scores: float32 [12, 512, 512], P('head', 'wide')
- grad_value_weight: float32 [2, 12, 64, 64], P(None, 'head', 'wide')
Inputs may be any that keep to these rules, and one draw needn't show every extreme that they name: `lengths_a`: each item's valid length is more than half of its bucket's padded length 128; in each aligned group of 1 items one item has length exactly 128. `lengths_b`: each item's valid length is more than half of 256; in each aligned group of 1 items one item has length exactly 256. `lengths_c`: each item's valid length is more than half of 512; in each aligned group of 1 items one item has length exactly 512.
All inputs are finite; a program needn't handle non-finite values.
Results may differ from a plain program's by a relative error of at most 0.019.
Values may be sent and summed in bfloat16 or wider, within the bound.
No kernel may reach another device: no remote copies, remote signals or barrier semaphores. Data moves between devices by JAX's collectives and lax.ppermute only.
A program may use at most 256 MiB of HBM per device.

v0:
```python
import math

import jax
import jax.numpy as jnp
from jax import lax
from jax.sharding import PartitionSpec as P

HD = 64
LC = 512
LA = 128
LB = 256
LAYERS = 2


EPSILON = 1e-05
MASKED_SCORE = -1e30


def cut_along(shard, dim, size):
    lengths = shard.shape
    tiles = shard.reshape(*lengths[:dim], size, lengths[dim] // size, *lengths[dim + 1 :])
    return jnp.moveaxis(tiles, dim, 0)


def sent_and_summed(shard, axis, dim):
    tiles = cut_along(shard, dim, lax.axis_size(axis))
    arrived = lax.all_to_all(tiles, axis, split_axis=0, concat_axis=0, tiled=True)
    return arrived.astype(jnp.float32).sum(axis=0)


def side_by_side(arrays, axis, dim, along):
    widths = [math.prod(a.shape[along:]) for a in arrays]
    both = jnp.concatenate(
        [a.reshape(*a.shape[:along], w) for a, w in zip(arrays, widths)], axis=along
    )
    result = sent_and_summed(both, axis, dim)
    tiles = jnp.split(result, [sum(widths[:k]) for k in range(1, len(widths))], axis=along)
    return tuple(
        (b.reshape(*result.shape[:along], *a.shape[along:]) for a, b in zip(arrays, tiles))
    )


def normalize(token_rows, gain_row, shift_row):
    middle = jnp.mean(token_rows, axis=-1, keepdims=True)
    centred = token_rows - middle
    spread = jnp.mean(centred * centred, axis=-1, keepdims=True)
    return centred * lax.rsqrt(spread + EPSILON) * gain_row + shift_row


def cut_rows(whole_rows, counts):
    pieces = []
    offset = 0
    for piece_rows in counts:
        pieces.append(whole_rows[offset : offset + piece_rows])
        offset = offset + piece_rows
    return pieces


def to_heads(bucket_parts):
    return [
        lax.all_to_all(segment, "head", split_axis=1, concat_axis=0, tiled=True)
        for segment in bucket_parts
    ]


def to_tokens(head_parts):
    return [
        lax.all_to_all(segment, "head", split_axis=0, concat_axis=1, tiled=True)
        for segment in head_parts
    ]


def score_parts(level_index, head_block, span_len, item_lengths, head_weights):
    first, first_bias, second, second_bias, random_scores, value_weight = head_weights
    item_count = head_block.shape[0] // span_len
    head_grid = head_block.reshape(item_count, span_len, first.shape[0], HD)
    if level_index == 0:
        pre_act = (
            jnp.einsum("ilhd,hde->ilhe", head_grid, first, preferred_element_type=jnp.float32)
            + first_bias[None, None]
        )
        activated = jax.nn.gelu(pre_act).astype(jnp.bfloat16)
        raw_scores = (
            jnp.einsum(
                "ilhe,hej->ihlj",
                activated,
                second[:, :, :span_len],
                preferred_element_type=jnp.float32,
            )
            + second_bias[None, :, None, :span_len]
        )
    else:
        pre_act = None
        activated = None
        raw_scores = random_scores[None, :, :span_len, :span_len].astype(jnp.float32)
    key_mask = (jnp.arange(span_len)[None, :] < item_lengths[:, None])[:, None, None, :]
    masked = jnp.where(key_mask, raw_scores, MASKED_SCORE)
    highest = jnp.max(masked, axis=-1, keepdims=True)
    expanded = jnp.exp(masked - highest)
    softened = expanded / jnp.sum(expanded, axis=-1, keepdims=True)
    values_low = jnp.einsum(
        "ilhd,hde->ilhe", head_grid, value_weight[level_index], preferred_element_type=jnp.float32
    ).astype(jnp.bfloat16)
    return (head_grid, pre_act, activated, softened, values_low)


def synth_forward(level_index, head_block, span_len, item_lengths, head_weights):
    head_grid, pre_act, activated, softened, values_low = score_parts(
        level_index, head_block, span_len, item_lengths, head_weights
    )
    mixed = jnp.einsum(
        "ihlj,ijhe->ilhe",
        softened.astype(jnp.bfloat16),
        values_low,
        preferred_element_type=jnp.float32,
    )
    return mixed.astype(jnp.bfloat16).reshape(head_block.shape[0], -1)


def synth_backward(level_index, head_block, d_mixed, span_len, item_lengths, head_weights):
    first, first_bias, second, second_bias, random_scores, value_weight = head_weights
    head_grid, pre_act, activated, softened, values_low = score_parts(
        level_index, head_block, span_len, item_lengths, head_weights
    )
    d_grid_out = d_mixed.reshape(head_grid.shape)
    d_soft = jnp.einsum(
        "ilhe,ijhe->ihlj", d_grid_out, values_low, preferred_element_type=jnp.float32
    )
    d_values = jnp.einsum(
        "ihlj,ilhe->ijhe",
        softened.astype(jnp.bfloat16),
        d_grid_out,
        preferred_element_type=jnp.float32,
    ).astype(jnp.bfloat16)
    d_scores = softened * (d_soft - jnp.sum(softened * d_soft, axis=-1, keepdims=True))
    grad_value = jnp.einsum(
        "ilhd,ilhe->hde", head_grid, d_values, preferred_element_type=jnp.float32
    )
    d_grid = jnp.einsum(
        "ilhe,hde->ilhd", d_values, value_weight[level_index], preferred_element_type=jnp.float32
    )
    pad_cols = second.shape[2] - span_len
    if level_index == 0:
        d_scores_low = d_scores.astype(jnp.bfloat16)
        grad_second_bias = jnp.pad(
            jnp.einsum("ihlj->hj", d_scores_low, preferred_element_type=jnp.float32),
            ((0, 0), (0, pad_cols)),
        )
        grad_second = jnp.pad(
            jnp.einsum(
                "ilhe,ihlj->hej", activated, d_scores_low, preferred_element_type=jnp.float32
            ),
            ((0, 0), (0, 0), (0, pad_cols)),
        )
        d_activated = jnp.einsum(
            "ihlj,hej->ilhe",
            d_scores_low,
            second[:, :, :span_len],
            preferred_element_type=jnp.float32,
        )
        d_pre = jax.vjp(jax.nn.gelu, pre_act)[1](d_activated)[0].astype(jnp.bfloat16)
        grad_first_bias = jnp.einsum("ilhe->he", d_pre, preferred_element_type=jnp.float32)
        grad_first = jnp.einsum(
            "ilhd,ilhe->hde", head_grid, d_pre, preferred_element_type=jnp.float32
        )
        d_grid = d_grid + jnp.einsum(
            "ilhe,hde->ilhd", d_pre, first, preferred_element_type=jnp.float32
        )
        dense_grads = (grad_first, grad_first_bias, grad_second, grad_second_bias)
        return (d_grid.astype(jnp.bfloat16).reshape(head_block.shape), dense_grads, grad_value)
    grad_random = jnp.pad(jnp.sum(d_scores, axis=0), ((0, 0), (0, pad_cols), (0, pad_cols)))
    return (d_grid.astype(jnp.bfloat16).reshape(head_block.shape), grad_random, grad_value)


def per_device(
    tokens_a,
    tokens_b,
    tokens_c,
    lengths_a,
    lengths_b,
    lengths_c,
    cotan_a,
    cotan_b,
    cotan_c,
    ln_gain,
    ln_bias,
    row_bias,
    out_weight,
    up_weight,
    up_bias,
    down_weight,
    synth_first,
    synth_first_bias,
    synth_second,
    synth_second_bias,
    random_scores,
    value_weight,
):
    spans = (LA, LB, LC)
    bucket_lengths = (lengths_a, lengths_b, lengths_c)
    counts = [tokens_a.shape[0], tokens_b.shape[0], tokens_c.shape[0]]
    head_weights = (
        synth_first,
        synth_first_bias,
        synth_second,
        synth_second_bias,
        random_scores,
        value_weight,
    )
    token_rows = jnp.concatenate([tokens_a, tokens_b, tokens_c], axis=0).astype(jnp.float32)
    stored = []
    for level_index in range(LAYERS):
        w_out, w_up, b_up, w_down = (
            lax.all_gather(out_weight[level_index], ("wide", "head"), axis=0, tiled=True),
            lax.all_gather(up_weight[level_index], ("wide", "head"), axis=0, tiled=True),
            lax.all_gather(
                up_bias[level_index].astype(jnp.bfloat16), ("wide", "head"), axis=0, tiled=True
            ).astype(jnp.float32),
            lax.all_gather(down_weight[level_index], ("wide", "head"), axis=0, tiled=True),
        )
        normed = normalize(token_rows, ln_gain[level_index, 0], ln_bias[level_index, 0]).astype(
            jnp.bfloat16
        )
        head_parts = to_heads(cut_rows(normed, counts))
        mixed_heads = [
            synth_forward(
                level_index,
                head_parts[bucket_index],
                spans[bucket_index],
                bucket_lengths[bucket_index],
                head_weights,
            )
            for bucket_index in range(3)
        ]
        mixed_rows = jnp.concatenate(to_tokens(mixed_heads), axis=0)
        joined = (
            jnp.dot(mixed_rows, w_out, preferred_element_type=jnp.float32)
            + row_bias[level_index, 0]
        )
        resid = token_rows + joined
        normed2 = normalize(resid, ln_gain[level_index, 1], ln_bias[level_index, 1]).astype(
            jnp.bfloat16
        )
        ffn_in = normed2
        pre_ffn = jnp.einsum("rd,fd->rf", ffn_in, w_up, preferred_element_type=jnp.float32) + b_up
        hidden = jax.nn.gelu(pre_ffn).astype(jnp.bfloat16)
        ffn_term = jnp.dot(hidden, w_down, preferred_element_type=jnp.float32)
        new_rows = resid + ffn_term + row_bias[level_index, 1]
        stored.append(
            (
                token_rows,
                head_parts,
                mixed_rows,
                resid,
                ffn_in,
                pre_ffn,
                hidden,
                (w_out, w_up, b_up, w_down),
            )
        )
        token_rows = new_rows
    out_parts = cut_rows(token_rows.astype(jnp.bfloat16), counts)
    grad_rows = jnp.concatenate([cotan_a, cotan_b, cotan_c], axis=0).astype(jnp.float32)
    gain_grads = [None, None]
    shift_grads = [None, None]
    bias_grads = [None, None]
    layer_grads = [None, None]
    value_grads = [None, None]
    dense_totals = None
    random_total = None
    for level_index in (1, 0):
        rows_in, head_parts, mixed_rows, resid, ffn_in, pre_ffn, hidden, layer_weights = stored[
            level_index
        ]
        w_out, w_up, b_up, w_down = layer_weights
        d_ffn = grad_rows.astype(jnp.bfloat16)
        ffn_bias_grad = jnp.einsum("rd->d", d_ffn, preferred_element_type=jnp.float32)
        grad_down = jnp.einsum("rf,rd->fd", hidden, d_ffn, preferred_element_type=jnp.float32)
        d_hidden = jnp.einsum("rd,fd->rf", d_ffn, w_down, preferred_element_type=jnp.float32)
        d_pre_ffn = jax.vjp(jax.nn.gelu, pre_ffn)[1](d_hidden)[0].astype(jnp.bfloat16)
        grad_up_bias = jnp.einsum("rf->f", d_pre_ffn, preferred_element_type=jnp.float32)
        grad_up = jnp.einsum("rf,rd->fd", d_pre_ffn, ffn_in, preferred_element_type=jnp.float32)
        d_normed2 = jnp.dot(d_pre_ffn, w_up, preferred_element_type=jnp.float32)
        norm_pull = jax.vjp(normalize, resid, ln_gain[level_index, 1], ln_bias[level_index, 1])[1]
        d_resid_norm, gain_second, shift_second = norm_pull(d_normed2)
        d_resid = grad_rows + d_resid_norm
        d_join = d_resid.astype(jnp.bfloat16)
        join_bias_grad = jnp.einsum("rd->d", d_join, preferred_element_type=jnp.float32)
        grad_out = jnp.einsum("rd,re->de", mixed_rows, d_join, preferred_element_type=jnp.float32)
        d_mixed = jnp.einsum("re,de->rd", d_join, w_out, preferred_element_type=jnp.float32).astype(
            jnp.bfloat16
        )
        layer_grads[level_index] = (grad_out, grad_up, grad_up_bias, grad_down)
        d_mixed_heads = to_heads(cut_rows(d_mixed, counts))
        d_head_parts = []
        value_total = None
        for bucket_index in range(3):
            d_block, level_grads, grad_value = synth_backward(
                level_index,
                head_parts[bucket_index],
                d_mixed_heads[bucket_index],
                spans[bucket_index],
                bucket_lengths[bucket_index],
                head_weights,
            )
            d_head_parts.append(d_block)
            value_total = grad_value if value_total is None else value_total + grad_value
            if level_index == 0:
                dense_totals = (
                    level_grads
                    if dense_totals is None
                    else tuple(
                        (
                            total_part + grad_part
                            for total_part, grad_part in zip(dense_totals, level_grads)
                        )
                    )
                )
            else:
                random_total = level_grads if random_total is None else random_total + level_grads
        value_grads[level_index] = value_total
        d_normed = jnp.concatenate(to_tokens(d_head_parts), axis=0).astype(jnp.float32)
        norm_pull = jax.vjp(normalize, rows_in, ln_gain[level_index, 0], ln_bias[level_index, 0])[1]
        d_rows_norm, gain_first, shift_first = norm_pull(d_normed)
        grad_rows = d_resid + d_rows_norm
        gain_grads[level_index] = jnp.stack([gain_first, gain_second])
        shift_grads[level_index] = jnp.stack([shift_first, shift_second])
        bias_grads[level_index] = jnp.stack([join_bias_grad, ffn_bias_grad])
    stacked_out = jnp.stack([layer_grads[0][0], layer_grads[1][0]])
    stacked_up = jnp.stack([layer_grads[0][1], layer_grads[1][1]])
    stacked_up_bias = jnp.stack([layer_grads[0][2], layer_grads[1][2]])
    stacked_down = jnp.stack([layer_grads[0][3], layer_grads[1][3]])
    summed_out, summed_up, summed_up_bias, summed_down = (
        lax.psum_scatter(stacked_out, ("wide", "head"), scatter_dimension=1, tiled=True),
        lax.psum_scatter(stacked_up, ("wide", "head"), scatter_dimension=1, tiled=True),
        lax.psum_scatter(stacked_up_bias, ("wide", "head"), scatter_dimension=1, tiled=True),
        lax.psum_scatter(stacked_down, ("wide", "head"), scatter_dimension=1, tiled=True),
    )
    summed_gain, summed_shift, summed_bias = lax.psum(
        (jnp.stack(gain_grads), jnp.stack(shift_grads), jnp.stack(bias_grads)), ("wide", "head")
    )
    head_sums = (
        *side_by_side(
            (
                dense_totals[0].astype(jnp.bfloat16),
                dense_totals[1].astype(jnp.bfloat16),
                dense_totals[2].astype(jnp.bfloat16),
            ),
            "wide",
            1,
            2,
        ),
        *side_by_side(
            (dense_totals[3].astype(jnp.bfloat16), random_total.astype(jnp.bfloat16)), "wide", 1, 2
        ),
        sent_and_summed(jnp.stack(value_grads).astype(jnp.bfloat16), "wide", 2),
    )
    grad_parts = cut_rows(grad_rows, counts)
    return (
        out_parts[0],
        out_parts[1],
        out_parts[2],
        grad_parts[0],
        grad_parts[1],
        grad_parts[2],
        summed_gain,
        summed_shift,
        summed_bias,
        summed_out,
        summed_up,
        summed_up_bias,
        summed_down,
        head_sums[0],
        head_sums[1],
        head_sums[2],
        head_sums[3],
        head_sums[4],
        head_sums[5],
    )


def solution(mesh):
    placed = (
        P(("wide", "head"), None),
        P(("wide", "head"), None),
        P(("wide", "head"), None),
        P("wide"),
        P("wide"),
        P("wide"),
        P(("wide", "head"), None),
        P(("wide", "head"), None),
        P(("wide", "head"), None),
        P(),
        P(),
        P(),
        P(None, ("wide", "head"), None),
        P(None, ("wide", "head"), None),
        P(None, ("wide", "head")),
        P(None, ("wide", "head"), None),
        P("head", None, None),
        P("head", None),
        P("head", None, None),
        P("head", None),
        P("head", None, None),
        P(None, "head", None, None),
    )
    return jax.shard_map(
        per_device,
        mesh=mesh,
        in_specs=placed,
        out_specs=(
            P(("wide", "head"), None),
            P(("wide", "head"), None),
            P(("wide", "head"), None),
            P(("wide", "head"), None),
            P(("wide", "head"), None),
            P(("wide", "head"), None),
            P(),
            P(),
            P(),
            P(None, ("wide", "head"), None),
            P(None, ("wide", "head"), None),
            P(None, ("wide", "head")),
            P(None, ("wide", "head"), None),
            P("head", "wide", None),
            P("head", "wide"),
            P("head", "wide", None),
            P("head", "wide"),
            P("head", "wide", None),
            P(None, "head", "wide", None),
        ),
        check_vma=False,
    )
```

profile of v0, /device:TPU:0, one launch (start us, length us, event | category | flops | bytes accessed | tf_op | source)
XLA Modules:
  0.0 1133.4 jit_solution(1127949113977298311)
XLA Ops:
  19.4 4.2 all-to-all-start
  27.9 3.2 fusion.352
  34.7 3.3 all-to-all-start.2
  43.0 3.4 all-to-all-start.4
  51.7 3.3 all-to-all-start.1
  62.3 3.9 all-to-all-start.3
  66.2 2.7 fusion.118
  72.2 3.4 all-to-all-start.5
  76.1 41.7 %all-reduce.9 = (bf16[3072]{0:T(1024)(128)(2,1)S(1)}, bf16[3072]{0:T(1024)(128)(2,1)S(1)}) all-reduce(bf16[3072]{0:T(1024)(128)(2,1)S(1)} %dynamic-update-slice, bf16[3072]{0:T(1024)(128)(2,1)S(1)} %dynamic-update-slice.1), channel_id=4, replica_groups=mesh['wide'=8,'head'=4] {'wide','head'}, use_global_device_ids=true, to_apply=%add.6 | all-reduce | flops 6144 | bytes 24576
  124.0 10.7 all-gather.17.cloned.1.call-done
  134.7 5.5 fusion.20
  140.3 60.0 %all-gather.19.cloned.1.call-done = bf16[1,3072,768]{2,1,0:T(8,128)(2,1)} async-done(((bf16[1,96,768]{2,1,0:T(8,128)(2,1)}), bf16[1,3072,768]{2,1,0:T(8,128)(2,1)}) %all-gather.19.cloned.1.call-update) | async-done | bytes 4718608 | tf_op jit(solution)/shard_map/all_gather | solution.py:219
  200.3 5.0 fusion.351
  206.6 3.3 all-to-all-start.6
  211.6 2.4 all-to-all-done.6
  214.1 3.3 all-to-all-start.8
  222.0 3.4 all-to-all-start.10
  226.6 2.5 fusion.140
  231.2 3.3 all-to-all-start.7
  235.0 3.6 all-to-all-done.7
  238.6 3.3 all-to-all-start.9
  242.0 2.8 fusion.113
  245.5 2.3 all-to-all-done.9
  247.8 3.8 all-to-all-start.11
  252.0 4.6 all-gather.21.cloned.1.call-done
  259.4 62.5 %all-gather.23.cloned.1.call-done = bf16[1,3072,768]{2,1,0:T(8,128)(2,1)} async-done(((bf16[1,96,768]{2,1,0:T(8,128)(2,1)}), bf16[1,3072,768]{2,1,0:T(8,128)(2,1)}) %all-gather.23.cloned.1.call-update) | async-done | bytes 4718608 | tf_op jit(solution)/shard_map/all_gather | solution.py:215
  321.9 5.5 fusion.23
  327.4 60.2 %all-gather.25.cloned.1.call-done = bf16[1,3072,768]{2,1,0:T(8,128)(2,1)} async-done(((bf16[1,96,768]{2,1,0:T(8,128)(2,1)}), bf16[1,3072,768]{2,1,0:T(8,128)(2,1)}) %all-gather.25.cloned.1.call-update) | async-done | bytes 4718608 | tf_op jit(solution)/shard_map/all_gather | solution.py:219
  387.6 7.2 convert_reduce_fusion.2
  402.2 3.9 all-to-all-start.12
  410.9 3.3 all-to-all-start.14
  419.3 3.4 all-to-all-start.16
  425.3 2.5 fusion.141
  432.0 3.9 all-to-all-start.13
  438.5 3.2 fusion.114
  441.7 3.3 all-to-all-start.15
  450.1 4.0 all-to-all-start.17
  454.3 3.0 convolution_bitcast_fusion.4
  464.0 5.4 convert_reduce_fusion.3
  473.0 2.4 copy.288
  478.9 2.5 pad_maximum_fusion.2
  481.5 4.1 convolution_bitcast_fusion
  487.7 6.7 pad_maximum_fusion.1
  499.0 6.7 pad_maximum_fusion
  509.5 4.3 fusion
  513.8 4.8 add_convert_fusion
  520.1 3.3 all-to-all-start.18
  528.2 3.3 all-to-all-start.20
  536.9 4.0 all-to-all-start.22
  551.1 4.1 all-to-all-start.19
  567.4 3.3 all-to-all-start.21
  571.7 3.6 all-to-all-done.21
  575.4 4.3 all-to-all-start.26
  579.9 6.6 all-to-all-done.26
  586.5 3.4 all-to-all-start.23
  591.5 3.6 all-to-all-done.23
  595.2 3.4 all-to-all-start.24
  602.0 5.3 all-to-all-done.24
  607.3 3.6 all-to-all-start.25
  611.1 5.1 fusion.82
  632.5 56.9 %all-reduce.8 = (f32[2,2,768]{2,1,0:T(2,128)}, f32[2,2,768]{2,1,0:T(2,128)}, f32[2,2,768]{2,1,0:T(2,128)}) all-reduce(f32[2,2,768]{2,1,0:T(2,128)S(1)} %pad_maximum_fusion.14, f32[2,2,768]{2,1,0:T(2,128)S(1)} %pad_maximum_fusion.15, f32[2,2,768]{2,1,0:T(2,128)S(1)} %pad_maximum_fusion.16), channel_id=1, replica_groups=mesh['wide'=8,'head'=4] {'wide','head'}, use_global_device_ids=true, to_apply=%region_35.36 | all-reduce | flops 9216 | bytes 73728 | tf_op jit(solution)/shard_map/psum | solution.py:339
  694.3 7.5 reduce-scatter.7.cloned.1.call-done
  701.9 212.3 %reduce-scatter.11.cloned.1.call-done = f32[2,96,768]{2,1,0:T(8,128)} async-done(((f32[2,3072,768]{2,1,0:T(8,128)}), f32[2,96,768]{2,1,0:T(8,128)}) %reduce-scatter.11.cloned.1.call-update) | async-done | bytes 589840 | tf_op jit(solution)/shard_map/reduce_scatter | solution.py:337
  914.2 212.0 %reduce-scatter.9.cloned.1.call-done = f32[2,96,768]{2,1,0:T(8,128)} async-done(((f32[2,3072,768]{2,1,0:T(8,128)}), f32[2,96,768]{2,1,0:T(8,128)}) %reduce-scatter.9.cloned.1.call-update) | async-done | bytes 589840 | tf_op jit(solution)/shard_map/reduce_scatter | solution.py:335
  (693 shorter events, 176.3 us)
Async XLA Ops:
  7.2 31.3 %copy-start = (bf16[3,64,64]{2,1,0:T(8,128)(2,1)S(1)}, bf16[3,64,64]{2,1,0:T(8,128)(2,1)}, u32[]{:S(2)}) copy-start(bf16[3,64,64]{2,1,0:T(8,128)(2,1)} %param.38) | copy-start | bytes 73732
  7.2 19.0 %copy-start.172 = (bf16[3,512,512]{2,1,0:T(8,128)(2,1)S(1)}, bf16[3,512,512]{2,1,0:T(8,128)(2,1)}, u32[]{:S(2)}) copy-start(bf16[3,512,512]{2,1,0:T(8,128)(2,1)} %param.42) | copy-start | bytes 4718596
  7.2 114.2 %all-gather.15.cloned.1.call-start = ((), (), s32[]{:S(2)}) async-start(), calls=%async_computation.34 | async-start | bytes 1216512 | tf_op jit(solution)/shard_map/all_gather | solution.py:214
  8.8 125.9 %all-gather.17.cloned.1.call-start = ((), (), s32[]{:S(2)}) async-start(), calls=%async_computation.35 | async-start | bytes 4866048 | tf_op jit(solution)/shard_map/all_gather | solution.py:215
  10.6 189.6 %all-gather.19.cloned.1.call-start = ((), (), s32[]{:S(2)}) async-start(), calls=%async_computation.36 | async-start | bytes 4866048 | tf_op jit(solution)/shard_map/all_gather | solution.py:219
  12.4 244.2 %all-gather.21.cloned.1.call-start = ((), (), s32[]{:S(2)}) async-start(), calls=%async_computation.37 | async-start | bytes 1216512 | tf_op jit(solution)/shard_map/all_gather | solution.py:214
  13.0 308.9 %all-gather.23.cloned.1.call-start = ((), (), s32[]{:S(2)}) async-start(), calls=%async_computation.38 | async-start | bytes 4866048 | tf_op jit(solution)/shard_map/all_gather | solution.py:215
  19.4 15.3 %all-to-all-start = ((bf16[32,4,192]{2,0,1:T(8,128)(2,1)}), bf16[32,4,192]{2,0,1:T(8,128)(2,1)S(1)}, u32[]{:S(2)}, u32[]{:S(2)}) async-start(bf16[32,4,192]{2,0,1:T(8,128)(2,1)} %copy.167), calls=%async_computation | async-start | bytes 131072 | tf_op jit(solution)/shard_map/all_to_all | solution.py:61
  23.7 364.0 %all-gather.25.cloned.1.call-start = ((), (), s32[]{:S(2)}) async-start(), calls=%async_computation.39 | async-start | bytes 4866048 | tf_op jit(solution)/shard_map/all_gather | solution.py:219
  26.2 20.8 %copy-start.177 = (pred[256]{0:T(512)(128)(4,1)}, pred[256]{0:T(512)(128)(4,1)S(1)}, u32[]{:S(2)}) copy-start(pred[256]{0:T(512)(128)(4,1)S(1)} %iota_compare_fusion.1) | copy-start | bytes 772
  34.7 8.3 all-to-all-start.2
  43.0 8.7 all-to-all-start.4
  51.7 9.9 all-to-all-start.1
  62.3 9.9 all-to-all-start.3
  66.2 55.2 %copy-start.18 = (bf16[64,768]{1,0:T(8,128)(2,1)S(1)}, bf16[64,768]{1,0:T(8,128)(2,1)}, u32[]{:S(2)}) copy-start(bf16[64,768]{1,0:T(8,128)(2,1)} %param.23) | copy-start | bytes 294916
  66.2 55.2 %copy-start.42 = (bf16[32,768]{1,0:T(8,128)(2,1)S(1)}, bf16[32,768]{1,0:T(8,128)(2,1)}, u32[]{:S(2)}) copy-start(bf16[32,768]{1,0:T(8,128)(2,1)} %param.22) | copy-start | bytes 147460
  72.2 62.6 %copy-start.112 = (f32[768]{0:T(1024)S(1)}, f32[768]{0:T(1024)}, u32[]{:S(2)}) copy-start(f32[768]{0:T(1024)} %get-tuple-element.111) | copy-start | bytes 9220
  72.2 62.6 %copy-start.132 = (f32[768]{0:T(1024)S(1)}, f32[768]{0:T(1024)}, u32[]{:S(2)}) copy-start(f32[768]{0:T(1024)} %get-tuple-element.36) | copy-start | bytes 9220
  72.2 49.2 %all-to-all-start.5 = ((bf16[4,128,192]{1,2,0:T(8,128)(2,1)}), bf16[4,128,192]{1,2,0:T(8,128)(2,1)S(1)}, u32[]{:S(2)}, u32[]{:S(2)}) async-start(bf16[4,128,192]{1,2,0:T(8,128)(2,1)} %copy.185), calls=%async_computation.5 | async-start | bytes 393216 | tf_op jit(solution)/shard_map/all_to_all | solution.py:68
  120.2 20.0 %copy-start.58 = (bf16[32,4,192]{0,2,1:T(8,128)(2,1)}, bf16[32,4,192]{0,2,1:T(8,128)(2,1)S(1)}, u32[]{:S(2)}) copy-start(bf16[32,4,192]{0,2,1:T(8,128)(2,1)S(1)} %copy.283) | copy-start | bytes 147460
  121.4 18.9 %copy-start.57 = (bf16[64,4,192]{0,2,1:T(8,128)(2,1)}, bf16[64,4,192]{0,2,1:T(8,128)(2,1)S(1)}, u32[]{:S(2)}) copy-start(bf16[64,4,192]{0,2,1:T(8,128)(2,1)S(1)} %copy.284) | copy-start | bytes 294916
  121.4 18.8 %copy-start.56 = (bf16[4,128,192]{1,2,0:T(8,128)(2,1)}, bf16[4,128,192]{1,2,0:T(8,128)(2,1)S(1)}, u32[]{:S(2)}) copy-start(bf16[4,128,192]{1,2,0:T(8,128)(2,1)S(1)} %all-to-all-done.5) | copy-start | bytes 589828
  123.7 76.6 %copy-start.10 = (f32[224,768]{1,0:T(8,128)}, f32[224,768]{1,0:T(8,128)S(1)}, u32[]{:S(2)}) copy-start(f32[224,768]{1,0:T(8,128)S(1)} %get-tuple-element.80) | copy-start | bytes 2064388
  205.6 20.0 %copy-start.127 = (f32[224]{0:T(256)}, f32[224]{0:T(256)S(1)}, u32[]{:S(2)}) copy-start(f32[224]{0:T(256)S(1)} %fusion.300) | copy-start | bytes 2692
  205.8 20.8 %copy-start.178 = (pred[256]{0:T(512)(128)(4,1)S(1)}, pred[256]{0:T(512)(128)(4,1)}, u32[]{:S(2)}) copy-start(pred[256]{0:T(512)(128)(4,1)} %copy-done.177) | copy-start | bytes 772
  205.8 20.8 %copy-start.185 = (f32[3,256]{1,0:T(4,128)S(1)}, f32[3,256]{1,0:T(4,128)}, u32[]{:S(2)}) copy-start(f32[3,256]{1,0:T(4,128)} %get-tuple-element.85) | copy-start | bytes 9220
  206.6 7.4 all-to-all-start.6
  214.1 7.9 all-to-all-start.8
  222.0 9.2 all-to-all-start.10
  231.2 7.4 all-to-all-start.7
  238.6 9.3 all-to-all-start.9
  245.5 76.4 %copy-start.113 = (f32[768]{0:T(1024)S(1)}, f32[768]{0:T(1024)}, u32[]{:S(2)}) copy-start(f32[768]{0:T(1024)} %get-tuple-element.112) | copy-start | bytes 9220
  245.5 76.4 %copy-start.134 = (f32[768]{0:T(1024)S(1)}, f32[768]{0:T(1024)}, u32[]{:S(2)}) copy-start(f32[768]{0:T(1024)} %get-tuple-element.35) | copy-start | bytes 9220
  247.8 9.1 all-to-all-start.11
  251.9 75.5 %copy-start.41 = (bf16[32,4,192]{0,2,1:T(8,128)(2,1)}, bf16[32,4,192]{0,2,1:T(8,128)(2,1)S(1)}, u32[]{:S(2)}) copy-start(bf16[32,4,192]{0,2,1:T(8,128)(2,1)S(1)} %copy.285) | copy-start | bytes 147460
  252.0 75.3 %copy-start.38 = (bf16[64,4,192]{0,2,1:T(8,128)(2,1)}, bf16[64,4,192]{0,2,1:T(8,128)(2,1)S(1)}, u32[]{:S(2)}) copy-start(bf16[64,4,192]{0,2,1:T(8,128)(2,1)S(1)} %copy.286) | copy-start | bytes 294916
  256.9 70.5 %copy-start.36 = (bf16[4,128,192]{1,2,0:T(8,128)(2,1)}, bf16[4,128,192]{1,2,0:T(8,128)(2,1)S(1)}, u32[]{:S(2)}) copy-start(bf16[4,128,192]{1,2,0:T(8,128)(2,1)S(1)} %all-to-all-done.11) | copy-start | bytes 589828
  259.1 235.6 %copy-start.3 = (f32[224,768]{1,0:T(8,128)}, f32[224,768]{1,0:T(8,128)S(1)}, u32[]{:S(2)}) copy-start(f32[224,768]{1,0:T(8,128)S(1)} %get-tuple-element.90) | copy-start | bytes 2064388
  259.1 68.2 %copy-start.129 = (f32[224]{0:T(256)}, f32[224]{0:T(256)S(1)}, u32[]{:S(2)}) copy-start(f32[224]{0:T(256)S(1)} %broadcast_multiply_fusion) | copy-start | bytes 2692
  259.4 68.0 %copy-start.157 = (f32[224]{0:T(256)}, f32[224]{0:T(256)S(1)}, u32[]{:S(2)}) copy-start(f32[224]{0:T(256)S(1)} %multiply_reduce_fusion.5) | copy-start | bytes 2692
  259.4 68.0 %copy-start.149 = (f32[224]{0:T(256)}, f32[224]{0:T(256)S(1)}, u32[]{:S(2)}) copy-start(f32[224]{0:T(256)S(1)} %fusion.301) | copy-start | bytes 2692
  402.2 8.7 all-to-all-start.12
  407.5 17.8 %copy-start.186 = (f32[3,256]{1,0:T(4,128)S(1)}, f32[3,256]{1,0:T(4,128)}, u32[]{:S(2)}) copy-start(f32[3,256]{1,0:T(4,128)} %get-tuple-element.85) | copy-start | bytes 9220
  410.9 8.3 all-to-all-start.14
  419.3 12.8 %all-to-all-start.16 = ((bf16[128,4,192]{0,2,1:T(8,128)(2,1)}), bf16[128,4,192]{0,2,1:T(8,128)(2,1)S(1)}, u32[]{:S(2)}, u32[]{:S(2)}) async-start(bf16[128,4,192]{0,2,1:T(8,128)(2,1)} %bitcast.109), calls=%async_computation.16 | async-start | bytes 393216 | tf_op jit(solution)/shard_map/all_to_all | solution.py:61
  432.0 9.6 all-to-all-start.13
  441.7 8.4 all-to-all-start.15
  450.1 9.4 all-to-all-start.17
  454.1 166.6 %reduce-scatter.13.cloned.1.call-start = ((), (), s32[]{:S(2)}) async-start(), calls=%async_computation.40 | async-start | bytes 1622016
  463.9 21.6 %copy-start.5 = (f32[224,768]{1,0:T(8,128)}, f32[224,768]{1,0:T(8,128)S(1)}, u32[]{:S(2)}) copy-start(f32[224,768]{1,0:T(8,128)S(1)} %get-tuple-element.57) | copy-start | bytes 2064388
  475.3 226.5 %reduce-scatter.7.cloned.1.call-start = ((), (), s32[]{:S(2)}) async-start(), calls=%async_computation.31 | async-start | bytes 4866048 | tf_op jit(solution)/shard_map/reduce_scatter | solution.py:334
  481.4 432.7 %reduce-scatter.11.cloned.1.call-start = ((), (), s32[]{:S(2)}) async-start(), calls=%async_computation.33 | async-start | bytes 19464192 | tf_op jit(solution)/shard_map/reduce_scatter | solution.py:337
  494.5 631.7 %reduce-scatter.9.cloned.1.call-start = ((), (), s32[]{:S(2)}) async-start(), calls=%async_computation.32 | async-start | bytes 19464192 | tf_op jit(solution)/shard_map/reduce_scatter | solution.py:335
  520.1 8.1 all-to-all-start.18
  528.2 8.7 all-to-all-start.20
  536.9 14.2 %all-to-all-start.22 = ((bf16[128,4,192]{0,2,1:T(8,128)(2,1)}), bf16[128,4,192]{0,2,1:T(8,128)(2,1)}, u32[]{:S(2)}, u32[]{:S(2)}) async-start(bf16[128,4,192]{0,2,1:T(8,128)(2,1)} %bitcast.159), calls=%async_computation.22 | async-start | bytes 393216 | tf_op jit(solution)/shard_map/all_to_all | solution.py:61
  551.1 16.3 %all-to-all-start.19 = ((bf16[4,32,192]{2,1,0:T(8,128)(2,1)}), bf16[4,32,192]{2,1,0:T(8,128)(2,1)}, u32[]{:S(2)}, u32[]{:S(2)}) async-start(bf16[4,32,192]{2,1,0:T(8,128)(2,1)} %all_to_all.387), calls=%async_computation.19 | async-start | bytes 131072 | tf_op jit(solution)/shard_map/all_to_all | solution.py:68
  565.5 34.2 %copy-start.47 = (bf16[3,512,512]{2,1,0:T(8,128)(2,1)S(1)}, bf16[3,512,512]{2,1,0:T(8,128)(2,1)}, u32[]{:S(2)}) copy-start(bf16[3,512,512]{2,1,0:T(8,128)(2,1)} %add_convert_fusion) | copy-start | bytes 4718596
  567.4 7.9 all-to-all-start.21
  575.4 19.8 %copy-start.67 = (bf16[4,64,192]{2,1,0:T(8,128)(2,1)}, bf16[4,64,192]{2,1,0:T(8,128)(2,1)S(1)}, u32[]{:S(2)}) copy-start(bf16[4,64,192]{2,1,0:T(8,128)(2,1)S(1)} %all-to-all-done.21) | copy-start | bytes 294916
  575.4 11.1 all-to-all-start.26
  586.5 8.7 all-to-all-start.23
  595.2 12.1 %all-to-all-start.24 = ((bf16[8,3,8,577]{3,2,1,0:T(8,128)(2,1)}), bf16[8,3,8,577]{3,2,1,0:T(8,128)(2,1)S(1)}, u32[]{:S(2)}, u32[]{:S(2)}) async-start(bf16[8,3,8,577]{3,2,1,0:T(8,128)(2,1)} %maximum_bitcast_fusion.1), calls=%async_computation.27 | async-start | bytes 491520 | tf_op jit(solution)/shard_map/all_to_all | solution.py:27
  607.3 85.1 %all-to-all-start.25 = ((bf16[8,3,64,513]{3,2,1,0:T(8,128)(2,1)}), bf16[8,3,64,513]{3,2,1,0:T(8,128)(2,1)S(1)}, u32[]{:S(2)}, u32[]{:S(2)}) async-start(bf16[8,3,64,513]{3,2,1,0:T(8,128)(2,1)} %maximum_bitcast_fusion), calls=%async_computation.28 | async-start | bytes 3932160 | tf_op jit(solution)/shard_map/all_to_all | solution.py:27
  (168 other events, 1031.5 us)
Sparse Core Ops, SparseCore 0:
  11.5 56.8 all-gather.14
  71.4 63.3 all-gather.16
  138.2 62.0 all-gather.18
  203.6 52.9 all-gather.20
  259.4 62.4 all-gather.22
  325.2 62.3 all-gather.24
  475.5 97.2 reduce-scatter.12
  578.8 123.0 reduce-scatter.6
  710.0 204.1 reduce-scatter.10
  922.1 203.9 reduce-scatter.8
where the time goes:
time: 1150 us; the launch traced here: 1130 us
  waiting for transfers between devices  668 us (58%)
  matrix products  109 us (9%)
  blocking collectives  98.6 us (9%)
  starting transfers between devices  97.3 us (8%)
  local copies, waits for them, and re-layouts  90.2 us (8%)
  other arithmetic  51.1 us (4%)
  between operations  19.8 us (2%)
    reduce_scatter x1, waiting for transfers between devices, per_device(): lax.psum_scatter(stacked_down, ('wide', 'head'), scatter_dimension=1, til...  212 us
    reduce_scatter x1, waiting for transfers between devices, per_device(): lax.psum_scatter(stacked_up, ('wide', 'head'), scatter_dimension=1, tiled...  212 us
    all_gather x2, waiting for transfers between devices, per_device(): lax.all_gather(down_weight[level_index], ('wide', 'head'), axis=0, tiled=...  120 us
    all_gather x2, waiting for transfers between devices, per_device(): lax.all_gather(up_weight[level_index], ('wide', 'head'), axis=0, tiled=True)  73.2 us
    psum x1, blocking collectives, per_device(): lax.psum((jnp.stack(gain_grads), jnp.stack(shift_grads), jnp.stack(bias_g...  56.9 us
    all_to_all x12, starting transfers between devices, to_tokens(): lax.all_to_all(segment, 'head', split_axis=0, concat_axis=1, tiled=True)  43 us
    all_to_all x12, starting transfers between devices, to_heads(): lax.all_to_all(segment, 'head', split_axis=1, concat_axis=0, tiled=True)  42.1 us
    unnamed x1, blocking collectives  41.7 us
  transfers between devices with their start and end apart: 37, of which 22 were waited for; matrix products, arithmetic and copies ran while one was open for 17% of the time, Pallas kernels for 0%

commit v1 on v0

v1 whole, which is shorter than its diff:
```python
from functools import partial

import jax
import jax.numpy as jnp
import numpy as np
from jax import lax
from jax.sharding import PartitionSpec as P

HD = 64
LC = 512
LA = 128
LB = 256
LAYERS = 2
D = 768

EPSILON = 1e-05
MASKED_SCORE = -1e30
AXES = ("wide", "head")
f32 = jnp.float32
bf16 = jnp.bfloat16


class Links:
    def __init__(self, n_wide, n_head):
        self.nx, self.nc = 2, 2
        self.nz, self.ny = n_wide // 2, n_head // 2
        self.n_head = n_head
        self.n_wide = n_wide
        self.digits = []
        stride, left = 1, self.nz
        while left > 1:
            count = 4 if left % 4 == 0 else 2 if left % 2 == 0 else left
            self.digits.append((stride, count))
            stride, left = stride * count, left // count

    def number(self, z, x, y, c):
        return ((z * self.nx + x) * self.ny + y) * self.nc + c

    def places(self):
        wide, head = lax.axis_index("wide"), lax.axis_index("head")
        return wide // self.nx, wide % self.nx, head // self.nc, head % self.nc

    def grid(self):
        return np.ndindex(self.nz, self.nx, self.ny, self.nc)

    def take(self, v, z=0, x=0, y=0, c=0):
        pairs = [
            (
                self.number(
                    (i + z) % self.nz, (j + x) % self.nx, (k + y) % self.ny, (m + c) % self.nc
                ),
                self.number(i, j, k, m),
            )
            for i, j, k, m in self.grid()
        ]
        return lax.ppermute(v, AXES, pairs)

    def give(self, v, z=0, x=0, y=0, c=0):
        return self.take(v, -z, -x, -y, -c)

    def take_bit(self, v, bit):
        pairs = [
            (self.number(i ^ bit, j, k, m), self.number(i, j, k, m)) for i, j, k, m in self.grid()
        ]
        return lax.ppermute(v, AXES, pairs)

    def total(self, v):
        v = v + self.take(v, x=1)
        v = v + self.take(v, y=1)
        bit = 1
        while bit < self.nz:
            v = v + self.take_bit(v, bit)
            bit = bit * 2
        return 0.5 * (v + self.take(v, c=1))

    def spread_z(self, v):
        v = v[None]
        for stride, count in self.digits:
            v = jnp.concatenate([v] + [self.take(v, z=stride * k) for k in range(1, count)], axis=0)
        return v

    def gather_z(self, v):
        for stride, count in reversed(self.digits):
            parts = v.reshape(count, v.shape[0] // count, *v.shape[1:])
            total = parts[0].astype(f32)
            for k in range(1, count):
                total = total + self.give(parts[k], z=stride * k).astype(f32)
            v = total if stride == 1 else total.astype(bf16)
        return v.reshape(v.shape[1:])

    def spread(self, v):
        half = v.shape[0] // 2
        zs = self.spread_z(v)
        a, b = zs[:, :half], zs[:, half:]
        a = jnp.stack([a, self.take(a, x=1)])
        b = jnp.stack([b, self.take(b, y=1)])
        return [a, self.take(a, y=1), b, self.take(b, x=1)]

    def fold(self, own, other, **step):
        return (own.astype(f32) + self.give(other, **step).astype(f32)).astype(bf16)

    def collect(self, blocks):
        a = self.fold(blocks[0], blocks[1], y=1)
        b = self.fold(blocks[2], blocks[3], x=1)
        a = self.fold(a[0], a[1], x=1)
        b = self.fold(b[0], b[1], y=1)
        return jnp.concatenate([self.gather_z(a), self.gather_z(b)], axis=0)

    def spread_one(self, v):
        v = self.spread_z(v)
        v = jnp.stack([v, self.take(v, x=1)])
        return jnp.stack([v, self.take(v, y=1)])

    def collect_one(self, v):
        v = self.fold(v[0], v[1], y=1)
        v = self.fold(v[0], v[1], x=1)
        return self.gather_z(v)

    def collect_wide(self, v, z, x):
        v = v.reshape(self.nz, self.nx, *v.shape[1:])
        own = lax.dynamic_index_in_dim(v, x, 1, keepdims=False)
        other = lax.dynamic_index_in_dim(v, 1 - x, 1, keepdims=False)
        v = self.fold(own, other, x=1)
        v = lax.dynamic_slice_in_dim(jnp.concatenate([v, v], axis=0), z, self.nz, axis=0)
        return self.gather_z(v)


def normalize(token_rows, gain_row, shift_row):
    middle = jnp.mean(token_rows, axis=-1, keepdims=True)
    centred = token_rows - middle
    spread = jnp.mean(centred * centred, axis=-1, keepdims=True)
    return centred * lax.rsqrt(spread + EPSILON) * gain_row + shift_row


def score_parts(level_index, head_block, span_len, item_lengths, head_weights):
    first, first_bias, second, second_bias, random_scores, value_weight = head_weights
    item_count = head_block.shape[0] // span_len
    head_grid = head_block.reshape(item_count, span_len, first.shape[0], HD)
    if level_index == 0:
        pre_act = (
            jnp.einsum("ilhd,hde->ilhe", head_grid, first, preferred_element_type=jnp.float32)
            + first_bias[None, None]
        )
        activated = jax.nn.gelu(pre_act).astype(jnp.bfloat16)
        raw_scores = (
            jnp.einsum(
                "ilhe,hej->ihlj",
                activated,
                second[:, :, :span_len],
                preferred_element_type=jnp.float32,
            )
            + second_bias[None, :, None, :span_len]
        )
    else:
        pre_act = None
        activated = None
        raw_scores = random_scores[None, :, :span_len, :span_len].astype(jnp.float32)
    key_mask = (jnp.arange(span_len)[None, :] < item_lengths[:, None])[:, None, None, :]
    masked = jnp.where(key_mask, raw_scores, MASKED_SCORE)
    highest = jnp.max(masked, axis=-1, keepdims=True)
    expanded = jnp.exp(masked - highest)
    softened = expanded / jnp.sum(expanded, axis=-1, keepdims=True)
    values_low = jnp.einsum(
        "ilhd,hde->ilhe", head_grid, value_weight[level_index], preferred_element_type=jnp.float32
    ).astype(jnp.bfloat16)
    return (head_grid, pre_act, activated, softened, values_low)


def synth_forward(level_index, head_block, span_len, item_lengths, head_weights):
    head_grid, pre_act, activated, softened, values_low = score_parts(
        level_index, head_block, span_len, item_lengths, head_weights
    )
    mixed = jnp.einsum(
        "ihlj,ijhe->ilhe",
        softened.astype(jnp.bfloat16),
        values_low,
        preferred_element_type=jnp.float32,
    )
    return mixed.astype(jnp.bfloat16).reshape(head_block.shape[0], -1)


def synth_backward(level_index, head_block, d_mixed, span_len, item_lengths, head_weights):
    first, first_bias, second, second_bias, random_scores, value_weight = head_weights
    head_grid, pre_act, activated, softened, values_low = score_parts(
        level_index, head_block, span_len, item_lengths, head_weights
    )
    d_grid_out = d_mixed.reshape(head_grid.shape)
    d_soft = jnp.einsum(
        "ilhe,ijhe->ihlj", d_grid_out, values_low, preferred_element_type=jnp.float32
    )
    d_values = jnp.einsum(
        "ihlj,ilhe->ijhe",
        softened.astype(jnp.bfloat16),
        d_grid_out,
        preferred_element_type=jnp.float32,
    ).astype(jnp.bfloat16)
    d_scores = softened * (d_soft - jnp.sum(softened * d_soft, axis=-1, keepdims=True))
    grad_value = jnp.einsum(
        "ilhd,ilhe->hde", head_grid, d_values, preferred_element_type=jnp.float32
    )
    d_grid = jnp.einsum(
        "ilhe,hde->ilhd", d_values, value_weight[level_index], preferred_element_type=jnp.float32
    )
    pad_cols = second.shape[2] - span_len
    if level_index == 0:
        d_scores_low = d_scores.astype(jnp.bfloat16)
        grad_second_bias = jnp.pad(
            jnp.einsum("ihlj->hj", d_scores_low, preferred_element_type=jnp.float32),
            ((0, 0), (0, pad_cols)),
        )
        grad_second = jnp.pad(
            jnp.einsum(
                "ilhe,ihlj->hej", activated, d_scores_low, preferred_element_type=jnp.float32
            ),
            ((0, 0), (0, 0), (0, pad_cols)),
        )
        d_activated = jnp.einsum(
            "ihlj,hej->ilhe",
            d_scores_low,
            second[:, :, :span_len],
            preferred_element_type=jnp.float32,
        )
        d_pre = jax.vjp(jax.nn.gelu, pre_act)[1](d_activated)[0].astype(jnp.bfloat16)
        grad_first_bias = jnp.einsum("ilhe->he", d_pre, preferred_element_type=jnp.float32)
        grad_first = jnp.einsum(
            "ilhd,ilhe->hde", head_grid, d_pre, preferred_element_type=jnp.float32
        )
        d_grid = d_grid + jnp.einsum(
            "ilhe,hde->ilhd", d_pre, first, preferred_element_type=jnp.float32
        )
        dense_grads = (grad_first, grad_first_bias, grad_second, grad_second_bias)
        return (d_grid.astype(jnp.bfloat16).reshape(head_block.shape), dense_grads, grad_value)
    grad_random = jnp.pad(jnp.sum(d_scores, axis=0), ((0, 0), (0, pad_cols), (0, pad_cols)))
    return (d_grid.astype(jnp.bfloat16).reshape(head_block.shape), grad_random, grad_value)


def per_device(
    links,
    tokens_a,
    tokens_b,
    tokens_c,
    lengths_a,
    lengths_b,
    lengths_c,
    cotan_a,
    cotan_b,
    cotan_c,
    ln_gain,
    ln_bias,
    row_bias,
    out_weight,
    up_weight,
    up_bias,
    down_weight,
    synth_first,
    synth_first_bias,
    synth_second,
    synth_second_bias,
    random_scores,
    value_weight,
):
    spans = (LA, LB, LC)
    bucket_lengths = (lengths_a, lengths_b, lengths_c)
    counts = [tokens_a.shape[0], tokens_b.shape[0], tokens_c.shape[0]]
    starts = [0, counts[0], counts[0] + counts[1]]
    rows = sum(counts)
    head_weights = (
        synth_first,
        synth_first_bias,
        synth_second,
        synth_second_bias,
        random_scores,
        value_weight,
    )
    z, x, y, c = links.places()
    nz = links.nz
    cols = synth_first.shape[0] * HD
    own_block = links.nc * y + c
    far_block = links.nc * (1 - y) + c

    own_rows = jnp.concatenate([tokens_a, tokens_b, tokens_c, cotan_a, cotan_b, cotan_c], axis=0)
    peer_rows = links.take(own_rows, c=1)
    both = jnp.where(
        c == 0, jnp.stack([own_rows, peer_rows]), jnp.stack([peer_rows, own_rows])
    )
    token_rows = both[:, :rows].reshape(2 * rows, D).astype(f32)
    grad_rows = both[:, rows:].reshape(2 * rows, D).astype(f32)

    out_rows, ff_rows = out_weight.shape[1], up_weight.shape[1]
    half_ff = ff_rows // 2
    misc_rows = -(-(out_rows + 1) // 16) * 16

    def misc_pack(level):
        high = up_bias[level].astype(bf16)
        low = (up_bias[level] - high.astype(f32)).astype(bf16)
        line = jnp.pad(jnp.concatenate([high, low])[None], ((0, 0), (0, D - 2 * ff_rows)))
        return jnp.pad(
            jnp.concatenate([out_weight[level], line], axis=0),
            ((0, misc_rows - out_rows - 1), (0, 0)),
        )

    def chip_numbers(core):
        iy = (y + jnp.arange(2)) % 2
        ix = (x + jnp.arange(2)) % 2
        iz = (z + jnp.arange(nz)) % nz
        device = links.number(
            iz[None, None, :], ix[None, :, None], iy[:, None, None], core
        )
        return (device[..., None] * out_rows + jnp.arange(out_rows)).reshape(-1)

    row_numbers = jnp.concatenate([chip_numbers(c), chip_numbers(1 - c)])
    wanted = jnp.concatenate(
        [own_block * cols + jnp.arange(cols), far_block * cols + jnp.arange(cols)]
    )
    pick_rows = (wanted[:, None] == row_numbers[None, :]).astype(bf16)
    pick_cols = (jnp.arange(D)[:, None] == wanted[None, :]).astype(bf16)

    weights = []
    for level in range(LAYERS):
        misc = links.spread_one(misc_pack(level))
        up_blocks = links.spread(up_weight[level])
        down_blocks = links.spread(down_weight[level])
        w_own = misc[:, :, :, :out_rows].reshape(-1, D)
        w_peer = links.take(w_own, c=1)
        w_out = jnp.dot(
            pick_rows, jnp.concatenate([w_own, w_peer]), preferred_element_type=f32
        ).astype(bf16)
        lines = misc[:, :, :, out_rows, : 2 * ff_rows].astype(f32)
        bias = lines[..., :ff_rows] + lines[..., ff_rows:]
        bias_blocks = [
            bias[0, :, :, :half_ff],
            bias[1, :, :, :half_ff],
            bias[:, 0, :, half_ff:],
            bias[:, 1, :, half_ff:],
        ]
        weights.append(
            (
                w_out,
                [w.reshape(-1, D) for w in up_blocks],
                [b.reshape(-1) for b in bias_blocks],
                [w.reshape(-1, D) for w in down_blocks],
            )
        )

    def to_heads(own, far):
        got = links.take(far, y=1)
        whole = jnp.where(y == 0, jnp.stack([own, got]), jnp.stack([got, own]))
        whole = whole.reshape(2, 2, rows, cols)
        return [
            whole[:, :, s : s + n].reshape(4 * n, cols) for s, n in zip(starts, counts)
        ]

    def to_tokens(parts):
        whole = jnp.concatenate(
            [p.reshape(2, 2, n, cols) for p, n in zip(parts, counts)], axis=2
        ).reshape(2, 2 * rows, cols)
        own = lax.dynamic_index_in_dim(whole, y, 0, keepdims=False)
        far = lax.dynamic_index_in_dim(whole, 1 - y, 0, keepdims=False)
        return own, links.take(far, y=1)

    def core_sum(part):
        return part + links.take(part.astype(bf16), c=1).astype(f32)

    stored = []
    for level in range(LAYERS):
        w_out, up_blocks, bias_blocks, down_blocks = weights[level]
        normed = normalize(token_rows, ln_gain[level, 0], ln_bias[level, 0]).astype(bf16)
        picked = jnp.dot(normed, pick_cols, preferred_element_type=f32).astype(bf16)
        head_parts = to_heads(picked[:, :cols], picked[:, cols:])
        mixed_parts = [
            synth_forward(level, head_parts[k], spans[k], bucket_lengths[k], head_weights)
            for k in range(3)
        ]
        mixed = jnp.concatenate(to_tokens(mixed_parts), axis=1)
        joined = core_sum(jnp.dot(mixed, w_out, preferred_element_type=f32)) + row_bias[level, 0]
        resid = token_rows + joined
        normed2 = normalize(resid, ln_gain[level, 1], ln_bias[level, 1]).astype(bf16)
        pre_blocks = [
            jnp.einsum("rd,fd->rf", normed2, w, preferred_element_type=f32) + b
            for w, b in zip(up_blocks, bias_blocks)
        ]
        hidden_blocks = [jax.nn.gelu(p).astype(bf16) for p in pre_blocks]
        ffn = sum(
            jnp.dot(h, w, preferred_element_type=f32) for h, w in zip(hidden_blocks, down_blocks)
        )
        stored.append((token_rows, head_parts, mixed, resid, normed2, pre_blocks, hidden_blocks))
        token_rows = resid + core_sum(ffn) + row_bias[level, 1]

    def own_parts(whole):
        mine = lax.dynamic_index_in_dim(whole.reshape(2, rows, D), c, 0, keepdims=False)
        return [mine[s : s + n] for s, n in zip(starts, counts)]

    out_parts = own_parts(token_rows.astype(bf16))

    stats = [None] * LAYERS
    out_grads, up_grads, bias_grads, down_grads = [], [], [], []
    head_grads = [None] * LAYERS
    for level in (1, 0):
        w_out, up_blocks, bias_blocks, down_blocks = weights[level]
        rows_in, head_parts, mixed, resid, normed2, pre_blocks, hidden_blocks = stored[level]
        d_ffn = grad_rows.astype(bf16)
        ffn_bias_grad = jnp.sum(d_ffn.astype(f32), axis=0)
        down_terms, up_terms, bias_terms = [], [], []
        d_normed2 = None
        for w_up, w_down, pre, hidden in zip(up_blocks, down_blocks, pre_blocks, hidden_blocks):
            shape = (2, nz, half_ff, D)
            down_terms.append(
                jnp.einsum("rf,rd->fd", hidden, d_ffn, preferred_element_type=f32)
                .astype(bf16)
                .reshape(shape)
            )
            d_hidden = jnp.einsum("rd,fd->rf", d_ffn, w_down, preferred_element_type=f32)
            d_pre = jax.vjp(jax.nn.gelu, pre)[1](d_hidden)[0].astype(bf16)
            bias_terms.append(jnp.sum(d_pre.astype(f32), axis=0).reshape(2, nz, half_ff))
            up_terms.append(
                jnp.einsum("rf,rd->fd", d_pre, normed2, preferred_element_type=f32)
                .astype(bf16)
                .reshape(shape)
            )
            term = jnp.dot(d_pre, w_up, preferred_element_type=f32)
            d_normed2 = term if d_normed2 is None else d_normed2 + term
        d_normed2 = core_sum(d_normed2)
        down_grads.insert(0, links.collect(down_terms))
        up_grads.insert(0, links.collect(up_terms))
        norm_pull = jax.vjp(normalize, resid, ln_gain[level, 1], ln_bias[level, 1])[1]
        d_resid_norm, gain_second, shift_second = norm_pull(d_normed2)
        d_resid = grad_rows + d_resid_norm
        d_join = d_resid.astype(bf16)
        join_bias_grad = jnp.sum(d_join.astype(f32), axis=0)
        d_mixed = jnp.einsum("re,de->rd", d_join, w_out, preferred_element_type=f32).astype(bf16)
        d_parts = to_heads(d_mixed[:, :cols], d_mixed[:, cols:])

        grad_out = jnp.einsum("rd,re->de", mixed, d_join, preferred_element_type=f32).astype(bf16)
        grad_out = jnp.einsum("wk,wd->kd", pick_rows, grad_out, preferred_element_type=f32)
        grad_out = grad_out.astype(bf16)
        near, far = grad_out[: grad_out.shape[0] // 2], grad_out[grad_out.shape[0] // 2 :]
        near = near + links.give(far, c=1)
        first = jnp.stack([bias_terms[0], bias_terms[1]])
        second = jnp.stack([bias_terms[2], bias_terms[3]], axis=1)
        line = jnp.pad(
            jnp.concatenate([first, second], axis=-1).astype(bf16)[..., None, :],
            ((0, 0),) * 4 + ((0, D - ff_rows),),
        )
        misc = jnp.concatenate([near.reshape(2, 2, nz, out_rows, D), line], axis=3)
        misc = jnp.pad(misc, ((0, 0),) * 3 + ((0, misc_rows - out_rows - 1), (0, 0)))
        misc = links.collect_one(misc)
        out_grads.insert(0, misc[:out_rows])
        bias_grads.insert(0, misc[out_rows, :ff_rows])

        d_head_parts = []
        totals = None
        for k in range(3):
            d_block, level_grads, grad_value = synth_backward(
                level, head_parts[k], d_parts[k], spans[k], bucket_lengths[k], head_weights
            )
            d_head_parts.append(d_block)
            found = (level_grads, grad_value)
            totals = found if totals is None else jax.tree.map(jnp.add, totals, found)
        n_wide = links.n_wide

        def by_wide(v, dim):
            shape = v.shape
            v = v.reshape(*shape[:dim], n_wide, shape[dim] // n_wide, *shape[dim + 1 :])
            return jnp.moveaxis(v, dim, 0).reshape(n_wide, -1)

        if level == 1:
            parts = [by_wide(totals[0], 1), by_wide(totals[1], 1)]
        else:
            parts = [by_wide(v, 1) for v in (*totals[0], totals[1])]
        widths = [p.shape[1] for p in parts]
        padded = -(-sum(widths) // LC) * LC
        packed = jnp.pad(
            jnp.concatenate(parts, axis=1).astype(bf16), ((0, 0), (0, padded - sum(widths)))
        ).reshape(n_wide, -1, LC)
        summed = links.collect_wide(packed, z, x).reshape(-1)
        head_grads[level] = [
            summed[sum(widths[:k]) : sum(widths[: k + 1])] for k in range(len(widths))
        ]

        own, far = to_tokens(d_head_parts)
        ours = jnp.concatenate([own, far], axis=1)
        theirs = links.take(ours, c=1)
        other_cols = jnp.concatenate(
            [
                (links.nc * y + 1 - c) * cols + jnp.arange(cols),
                (links.nc * (1 - y) + 1 - c) * cols + jnp.arange(cols),
            ]
        )
        places = jnp.concatenate([wanted, other_cols])
        place_cols = (places[:, None] == jnp.arange(D)[None, :]).astype(bf16)
        d_normed = jnp.dot(
            jnp.concatenate([ours, theirs], axis=1), place_cols, preferred_element_type=f32
        )
        norm_pull = jax.vjp(normalize, rows_in, ln_gain[level, 0], ln_bias[level, 0])[1]
        d_rows_norm, gain_first, shift_first = norm_pull(d_normed)
        grad_rows = d_resid + d_rows_norm
        stats[level] = jnp.stack(
            [gain_first, gain_second, shift_first, shift_second, join_bias_grad, ffn_bias_grad]
        )
    summed = links.total(jnp.stack(stats))
    grad_parts = own_parts(grad_rows)
    heads = synth_first.shape[0]
    first, first_bias, second, second_bias, value_low = head_grads[0]
    random, value_high = head_grads[1]
    return (
        *out_parts,
        *grad_parts,
        summed[:, 0:2],
        summed[:, 2:4],
        summed[:, 4:6],
        jnp.stack(out_grads),
        jnp.stack(up_grads),
        jnp.stack(bias_grads),
        jnp.stack(down_grads),
        first.reshape(heads, -1, HD),
        first_bias.reshape(heads, -1),
        second.reshape(heads, -1, LC),
        second_bias.reshape(heads, -1),
        random.reshape(heads, -1, LC),
        jnp.stack([value_low.reshape(heads, -1, HD), value_high.reshape(heads, -1, HD)]),
    )


def solution(mesh):
    placed = (
        P(("wide", "head"), None),
        P(("wide", "head"), None),
        P(("wide", "head"), None),
        P("wide"),
        P("wide"),
        P("wide"),
        P(("wide", "head"), None),
        P(("wide", "head"), None),
        P(("wide", "head"), None),
        P(),
        P(),
        P(),
        P(None, ("wide", "head"), None),
        P(None, ("wide", "head"), None),
        P(None, ("wide", "head")),
        P(None, ("wide", "head"), None),
        P("head", None, None),
        P("head", None),
        P("head", None, None),
        P("head", None),
        P("head", None, None),
        P(None, "head", None, None),
    )
    return jax.shard_map(
        partial(per_device, Links(mesh.shape["wide"], mesh.shape["head"])),
        mesh=mesh,
        in_specs=placed,
        out_specs=(
            P(("wide", "head"), None),
            P(("wide", "head"), None),
            P(("wide", "head"), None),
            P(("wide", "head"), None),
            P(("wide", "head"), None),
            P(("wide", "head"), None),
            P(),
            P(),
            P(),
            P(None, ("wide", "head"), None),
            P(None, ("wide", "head"), None),
            P(None, ("wide", "head")),
            P(None, ("wide", "head"), None),
            P("head", "wide", None),
            P("head", "wide"),
            P("head", "wide", None),
            P("head", "wide"),
            P("head", "wide", None),
            P(None, "head", "wide", None),
        ),
        check_vma=False,
    )
```

time: 1150 us -> 696 us (0.61)
  waiting for transfers between devices: 668 us -> 170 us
  blocking collectives: 98.6 us -> 0 us
  starting transfers between devices: 97.3 us -> 148 us
  matrix products: 109 us -> 159 us
  other arithmetic: 51.1 us -> 95 us
  local copies, waits for them, and re-layouts: 90.2 us -> 108 us
  between operations: 19.8 us -> 7.34 us
    reduce_scatter x3 -> x0, waiting for transfers between devices: 432 us -> none  [the longest x1 212 us: per_device(): lax.psum_scatter(stacked_down, ('wide', 'head'), scatter_dimension=1, til...]
    all_gather x6 -> x0, waiting for transfers between devices: 198 us -> none  [the longest x2 120 us: per_device(): lax.all_gather(down_weight[level_index], ('wide', 'head'), axis=0, tiled=...]
    ppermute x0 -> x122, waiting for transfers between devices: none -> 170 us  [the longest x120 165 us: take(): return lax.ppermute(v, AXES, pairs)]
    ppermute x0 -> x122, starting transfers between devices: none -> 148 us  [the longest x120 145 us: take(): return lax.ppermute(v, AXES, pairs)]
    all_to_all x27 -> x0, starting transfers between devices: 96.5 us -> none  [the longest x12 43 us: to_tokens(): lax.all_to_all(segment, 'head', split_axis=0, concat_axis=1, tiled=True)]
    psum x1 -> x0, blocking collectives: 56.9 us -> none  [per_device(): lax.psum((jnp.stack(gain_grads), jnp.stack(shift_grads), jnp.stack(bias_g...]
    unnamed x1 -> x0, blocking collectives: 41.7 us -> none
    dot_general x18 -> x60, matrix products: 57.1 us -> 98.7 us  [the longest x8 17 us: per_device(): jnp.einsum('rd,fd->rf', d_ffn, w_down, preferred_element_type=f32)]
  transfers between devices with their start and end apart: 37 -> 122, of which waited for: 22 -> 54; matrix products, arithmetic and copies ran while one was open for 17% -> 49% of each run, Pallas kernels for 0% -> 0%
where the time goes in v1:
time: 696 us; the launch traced here: 688 us
  waiting for transfers between devices  170 us (24%)
  matrix products  159 us (23%)
  starting transfers between devices  148 us (21%)
  local copies, waits for them, and re-layouts  108 us (16%)
  other arithmetic  95 us (14%)
  between operations  7.34 us (1%)
    ppermute x120, waiting for transfers between devices, take(): return lax.ppermute(v, AXES, pairs)  165 us
    ppermute x120, starting transfers between devices, take(): return lax.ppermute(v, AXES, pairs)  145 us
    unnamed x580, local copies, waits for them, and re-layouts  22.6 us
    dot_general x8, matrix products, per_device(): jnp.einsum('rd,fd->rf', d_ffn, w_down, preferred_element_type=f32)  17 us
    convert_element_type x22, other arithmetic, fold(): return (own.astype(f32) + self.give(other, **step).astype(f32)).astype(bf16)  15.7 us
    dot_general x8, matrix products, per_device(): term = jnp.dot(d_pre, w_up, preferred_element_type=f32)  14.3 us
  transfers between devices with their start and end apart: 122, of which 54 were waited for; matrix products, arithmetic and copies ran while one was open for 49% of the time, Pallas kernels for 0%

profile of v1, /device:TPU:0, one launch (start us, length us, event | category | flops | bytes accessed | tf_op | source)
XLA Modules:
  0.0 687.8 jit_solution(15852816944206920577)
XLA Ops:
  3.1 5.1 collective-permute-start.3
  10.2 2.9 collective-permute-start.10
  20.6 5.1 fusion.489
  25.7 2.7 fusion.490
  28.4 2.3 fusion.491
  37.2 10.3 %collective-permute-done.28 = bf16[1,32,768]{2,1,0:T(8,128)(2,1)S(1)} collective-permute-done((bf16[1,32,768]{2,1,0:T(8,128)(2,1)S(1)}, bf16[1,32,768]{2,1,0:T(8,128)(2,1)S(1)}, u32[]{:S(2)}, u32[]{:S(2)}) %collective-permute-start.28) | collective-permute-done | bytes 49184 | tf_op jit(solution)/shard_map/ppermute | solution.py:56
  50.3 2.4 collective-permute-start.34
  53.9 2.9 collective-permute-done.14
  56.8 8.7 %collective-permute-done.15 = bf16[1,96,768]{2,1,0:T(8,128)(2,1)S(1)} collective-permute-done((bf16[1,96,768]{2,1,0:T(8,128)(2,1)S(1)}, bf16[1,96,768]{2,1,0:T(8,128)(2,1)S(1)}, u32[]{:S(2)}, u32[]{:S(2)}) %collective-permute-start.15) | collective-permute-done | bytes 147488 | tf_op jit(solution)/shard_map/ppermute | solution.py:56
  65.5 4.9 collective-permute-start.39
  71.6 8.4 %collective-permute-done.35 = bf16[1,96,768]{2,1,0:T(8,128)(2,1)S(1)} collective-permute-done((bf16[1,96,768]{2,1,0:T(8,128)(2,1)S(1)}, bf16[1,96,768]{2,1,0:T(8,128)(2,1)S(1)}, u32[]{:S(2)}, u32[]{:S(2)}) %collective-permute-start.35) | collective-permute-done | bytes 147488 | tf_op jit(solution)/shard_map/ppermute | solution.py:56
  92.4 6.8 collective-permute-done.13
  101.6 4.0 collective-permute-done.17
  118.7 3.7 collective-permute-done.1
  147.7 5.0 collective-permute-done.2
  168.6 4.3 collective-permute-done.19
  201.7 5.1 collective-permute-done.31
  208.9 27.4 %collective-permute-done.25 = bf16[448,192]{1,0:T(8,128)(2,1)S(1)} collective-permute-done((bf16[448,192]{1,0:T(8,128)(2,1)S(1)}, bf16[448,192]{1,0:T(8,128)(2,1)S(1)}, u32[]{:S(2)}, u32[]{:S(2)}) %collective-permute-start.25) | collective-permute-done | bytes 172064 | tf_op jit(solution)/shard_map/ppermute | solution.py:56
  238.7 2.6 fusion.93
  243.0 2.5 fusion.120
  254.3 3.6 collective-permute-done.26
  275.6 2.5 fusion.448
  281.1 2.5 fusion.446
  293.0 2.7 fusion.450
  298.8 2.5 fusion.452
  301.3 3.0 fusion.494
  310.6 3.0 fusion.493
  326.5 3.5 collective-permute-done.104
  336.1 6.1 collective-permute-done.84
  349.3 2.4 multiply_reduce_fusion.1
  358.5 3.0 fusion.39
  372.8 4.4 fusion
  377.2 2.4 fusion.94
  380.3 2.5 fusion.121
  382.8 4.0 subtract_multiply_fusion
  390.5 3.8 add_convert_fusion
  397.2 2.7 pad_maximum_fusion
  399.8 3.4 convert_element_type.1423
  411.2 2.5 collective-permute-start.106
  416.0 2.5 collective-permute-start.108
  422.1 3.2 collective-permute-start.113
  426.1 2.3 collective-permute-done.112
  428.5 3.1 collective-permute-start.88
  432.4 3.2 collective-permute-done.87
  459.2 2.5 fusion.440
  472.2 2.9 fusion.495
  484.1 2.4 convolution_convert_fusion.13
  496.8 3.2 collective-permute-done.70
  503.9 7.6 %collective-permute-start.71 = (bf16[1,32,768]{2,1,0:T(8,128)(2,1)}, bf16[1,32,768]{2,1,0:T(8,128)(2,1)S(1)}, u32[]{:S(2)}, u32[]{:S(2)}) collective-permute-start(bf16[1,32,768]{2,1,0:T(8,128)(2,1)} %get-tuple-element.233), channel_id=1, source_target_pairs={{24,0},{25,1},{26,2},{27,3},{28,4},{29,5},{30,6},{31,7},{0,8},{1,9... | collective-permute-start | bytes 147464 | tf_op jit(solution)/shard_map/ppermute | solution.py:56
  513.5 5.2 collective-permute-start.73
  529.9 6.8 collective-permute-done.99
  542.0 7.3 %collective-permute-done.79 = bf16[2,4,48,768]{3,2,1,0:T(8,128)(2,1)S(1)} collective-permute-done((bf16[2,4,48,768]{3,2,1,0:T(8,128)(2,1)}, bf16[2,4,48,768]{3,2,1,0:T(8,128)(2,1)S(1)}, u32[]{:S(2)}, u32[]{:S(2)}) %collective-permute-start.79) | collective-permute-done | bytes 589856 | tf_op jit(solution)/shard_map/ppermute | solution.py:56
  552.1 2.4 multiply_reduce_fusion.3
  559.0 2.5 fusion.36
  570.6 2.8 fusion.156
  583.1 2.4 convert_reduce_fusion
  606.0 2.9 collective-permute-start.98
  611.6 4.2 collective-permute-start.103
  618.6 3.4 collective-permute-start.78
  623.0 3.1 collective-permute-done.77
  649.9 2.3 multiply_reduce_fusion.4
  658.8 2.7 collective-permute-done.58
  667.7 3.1 collective-permute-done.60
  672.8 5.6 collective-permute-done.64
  (1227 shorter events, 413.5 us)
Async XLA Ops:
  3.1 29.0 %collective-permute-start.3 = (bf16[1,32,768]{2,1,0:T(8,128)(2,1)S(1)}, bf16[1,32,768]{2,1,0:T(8,128)(2,1)S(1)}, u32[]{:S(2)}, u32[]{:S(2)}) collective-permute-start(bf16[1,32,768]{2,1,0:T(8,128)(2,1)S(1)} %pad_bitcast_fusion.1), channel_id=1, source_target_pairs={{8,0},{9,1},{10,2},{11,3},{12,4},{13,5},{14,6},{15,7},{16,8},{17,9... | collective-permute-start | bytes 147464 | tf_op jit(solution)/shard_map/ppermute | solution.py:56
  8.2 24.5 %collective-permute-start.4 = (bf16[1,32,768]{2,1,0:T(8,128)(2,1)S(1)}, bf16[1,32,768]{2,1,0:T(8,128)(2,1)S(1)}, u32[]{:S(2)}, u32[]{:S(2)}) collective-permute-start(bf16[1,32,768]{2,1,0:T(8,128)(2,1)S(1)} %pad_bitcast_fusion.1), channel_id=1, source_target_pairs={{16,0},{17,1},{18,2},{19,3},{20,4},{21,5},{22,6},{23,7},{24,8},{25... | collective-permute-start | bytes 147464 | tf_op jit(solution)/shard_map/ppermute | solution.py:56
  8.2 26.5 %collective-permute-start.5 = (bf16[1,32,768]{2,1,0:T(8,128)(2,1)S(1)}, bf16[1,32,768]{2,1,0:T(8,128)(2,1)S(1)}, u32[]{:S(2)}, u32[]{:S(2)}) collective-permute-start(bf16[1,32,768]{2,1,0:T(8,128)(2,1)S(1)} %pad_bitcast_fusion.1), channel_id=1, source_target_pairs={{24,0},{25,1},{26,2},{27,3},{28,4},{29,5},{30,6},{31,7},{0,8},{1,9... | collective-permute-start | bytes 147464 | tf_op jit(solution)/shard_map/ppermute | solution.py:56
  10.2 38.5 %collective-permute-start.10 = (bf16[1,96,768]{2,1,0:T(8,128)(2,1)S(1)}, bf16[1,96,768]{2,1,0:T(8,128)(2,1)S(1)}, u32[]{:S(2)}, u32[]{:S(2)}) collective-permute-start(bf16[1,96,768]{2,1,0:T(8,128)(2,1)S(1)} %get-tuple-element.227), channel_id=1, source_target_pairs={{8,0},{9,1},{10,2},{11,3},{12,4},{13,5},{14,6},{15,7},{16,8},{17,9... | collective-permute-start | bytes 442376 | tf_op jit(solution)/shard_map/ppermute | solution.py:56
  13.1 23.4 %collective-permute-start.27 = (bf16[1,32,768]{2,1,0:T(8,128)(2,1)S(1)}, bf16[1,32,768]{2,1,0:T(8,128)(2,1)S(1)}, u32[]{:S(2)}, u32[]{:S(2)}) collective-permute-start(bf16[1,32,768]{2,1,0:T(8,128)(2,1)S(1)} %pad_bitcast_fusion), channel_id=1, source_target_pairs={{8,0},{9,1},{10,2},{11,3},{12,4},{13,5},{14,6},{15,7},{16,8},{17,9... | collective-permute-start | bytes 147464 | tf_op jit(solution)/shard_map/ppermute | solution.py:56
  32.1 18.2 %collective-permute-start.11 = (bf16[1,96,768]{2,1,0:T(8,128)(2,1)S(1)}, bf16[1,96,768]{2,1,0:T(8,128)(2,1)S(1)}, u32[]{:S(2)}, u32[]{:S(2)}) collective-permute-start(bf16[1,96,768]{2,1,0:T(8,128)(2,1)S(1)} %get-tuple-element.227), channel_id=1, source_target_pairs={{16,0},{17,1},{18,2},{19,3},{20,4},{21,5},{22,6},{23,7},{24,8},{25... | collective-permute-start | bytes 442376 | tf_op jit(solution)/shard_map/ppermute | solution.py:56
  32.7 20.0 %collective-permute-start.12 = (bf16[1,96,768]{2,1,0:T(8,128)(2,1)S(1)}, bf16[1,96,768]{2,1,0:T(8,128)(2,1)S(1)}, u32[]{:S(2)}, u32[]{:S(2)}) collective-permute-start(bf16[1,96,768]{2,1,0:T(8,128)(2,1)S(1)} %get-tuple-element.227), channel_id=1, source_target_pairs={{24,0},{25,1},{26,2},{27,3},{28,4},{29,5},{30,6},{31,7},{0,8},{1,9... | collective-permute-start | bytes 442376 | tf_op jit(solution)/shard_map/ppermute | solution.py:56
  47.9 17.6 %collective-permute-start.15 = (bf16[1,96,768]{2,1,0:T(8,128)(2,1)S(1)}, bf16[1,96,768]{2,1,0:T(8,128)(2,1)S(1)}, u32[]{:S(2)}, u32[]{:S(2)}) collective-permute-start(bf16[1,96,768]{2,1,0:T(8,128)(2,1)S(1)} %get-tuple-element.229), channel_id=1, source_target_pairs={{16,0},{17,1},{18,2},{19,3},{20,4},{21,5},{22,6},{23,7},{24,8},{25... | collective-permute-start | bytes 442376 | tf_op jit(solution)/shard_map/ppermute | solution.py:56
  48.8 16.8 %collective-permute-start.16 = (bf16[1,96,768]{2,1,0:T(8,128)(2,1)S(1)}, bf16[1,96,768]{2,1,0:T(8,128)(2,1)S(1)}, u32[]{:S(2)}, u32[]{:S(2)}) collective-permute-start(bf16[1,96,768]{2,1,0:T(8,128)(2,1)S(1)} %get-tuple-element.229), channel_id=1, source_target_pairs={{24,0},{25,1},{26,2},{27,3},{28,4},{29,5},{30,6},{31,7},{0,8},{1,9... | collective-permute-start | bytes 442376 | tf_op jit(solution)/shard_map/ppermute | solution.py:56
  50.3 21.1 %collective-permute-start.34 = (bf16[1,96,768]{2,1,0:T(8,128)(2,1)S(1)}, bf16[1,96,768]{2,1,0:T(8,128)(2,1)S(1)}, u32[]{:S(2)}, u32[]{:S(2)}) collective-permute-start(bf16[1,96,768]{2,1,0:T(8,128)(2,1)S(1)} %get-tuple-element.226), channel_id=1, source_target_pairs={{8,0},{9,1},{10,2},{11,3},{12,4},{13,5},{14,6},{15,7},{16,8},{17,9... | collective-permute-start | bytes 442376 | tf_op jit(solution)/shard_map/ppermute | solution.py:56
  52.7 27.3 %collective-permute-start.35 = (bf16[1,96,768]{2,1,0:T(8,128)(2,1)S(1)}, bf16[1,96,768]{2,1,0:T(8,128)(2,1)S(1)}, u32[]{:S(2)}, u32[]{:S(2)}) collective-permute-start(bf16[1,96,768]{2,1,0:T(8,128)(2,1)S(1)} %get-tuple-element.226), channel_id=1, source_target_pairs={{16,0},{17,1},{18,2},{19,3},{20,4},{21,5},{22,6},{23,7},{24,8},{25... | collective-permute-start | bytes 442376 | tf_op jit(solution)/shard_map/ppermute | solution.py:56
  56.8 23.2 %collective-permute-start.36 = (bf16[1,96,768]{2,1,0:T(8,128)(2,1)S(1)}, bf16[1,96,768]{2,1,0:T(8,128)(2,1)S(1)}, u32[]{:S(2)}, u32[]{:S(2)}) collective-permute-start(bf16[1,96,768]{2,1,0:T(8,128)(2,1)S(1)} %get-tuple-element.226), channel_id=1, source_target_pairs={{24,0},{25,1},{26,2},{27,3},{28,4},{29,5},{30,6},{31,7},{0,8},{1,9... | collective-permute-start | bytes 442376 | tf_op jit(solution)/shard_map/ppermute | solution.py:56
  65.5 16.1 %collective-permute-start.38 = (bf16[1,96,768]{2,1,0:T(8,128)(2,1)S(1)}, bf16[1,96,768]{2,1,0:T(8,128)(2,1)S(1)}, u32[]{:S(2)}, u32[]{:S(2)}) collective-permute-start(bf16[1,96,768]{2,1,0:T(8,128)(2,1)S(1)} %get-tuple-element.228), channel_id=1, source_target_pairs={{8,0},{9,1},{10,2},{11,3},{12,4},{13,5},{14,6},{15,7},{16,8},{17,9... | collective-permute-start | bytes 442376 | tf_op jit(solution)/shard_map/ppermute | solution.py:56
  65.5 19.3 %collective-permute-start.39 = (bf16[1,96,768]{2,1,0:T(8,128)(2,1)S(1)}, bf16[1,96,768]{2,1,0:T(8,128)(2,1)S(1)}, u32[]{:S(2)}, u32[]{:S(2)}) collective-permute-start(bf16[1,96,768]{2,1,0:T(8,128)(2,1)S(1)} %get-tuple-element.228), channel_id=1, source_target_pairs={{16,0},{17,1},{18,2},{19,3},{20,4},{21,5},{22,6},{23,7},{24,8},{25... | collective-permute-start | bytes 442376 | tf_op jit(solution)/shard_map/ppermute | solution.py:56
  71.4 15.0 %collective-permute-start.40 = (bf16[1,96,768]{2,1,0:T(8,128)(2,1)S(1)}, bf16[1,96,768]{2,1,0:T(8,128)(2,1)S(1)}, u32[]{:S(2)}, u32[]{:S(2)}) collective-permute-start(bf16[1,96,768]{2,1,0:T(8,128)(2,1)S(1)} %get-tuple-element.228), channel_id=1, source_target_pairs={{24,0},{25,1},{26,2},{27,3},{28,4},{29,5},{30,6},{31,7},{0,8},{1,9... | collective-permute-start | bytes 442376 | tf_op jit(solution)/shard_map/ppermute | solution.py:56
  80.0 27.9 %collective-permute-start = (bf16[448,768]{1,0:T(8,128)(2,1)S(1)}, bf16[448,768]{1,0:T(8,128)(2,1)S(1)}, u32[]{:S(2)}, u32[]{:S(2)}) collective-permute-start(bf16[448,768]{1,0:T(8,128)(2,1)S(1)} %constant_dynamic-update-slice_fusion), channel_id=1, source_target_pairs={{1,0},{0,1},{3,2},{2,3},{5,4},{4,5},{7,6},{6,7},{9,8},{8,9},{11,10... | collective-permute-start | bytes 2064392 | tf_op jit(solution)/shard_map/ppermute | solution.py:56
  84.9 98.8 %collective-permute-start.30 = (bf16[4,32,768]{2,1,0:T(8,128)(2,1)}, bf16[4,32,768]{2,1,0:T(8,128)(2,1)}, u32[]{:S(2)}, u32[]{:S(2)}) collective-permute-start(bf16[4,32,768]{2,1,0:T(8,128)(2,1)} %get-tuple-element.237), channel_id=1, source_target_pairs={{4,0},{5,1},{6,2},{7,3},{0,4},{1,5},{2,6},{3,7},{12,8},{13,9},{14,... | collective-permute-start | bytes 589832 | tf_op jit(solution)/shard_map/ppermute | solution.py:56
  86.4 12.9 %collective-permute-start.13 = (bf16[4,48,768]{2,1,0:T(8,128)(2,1)S(1)}, bf16[4,48,768]{2,1,0:T(8,128)(2,1)S(1)}, u32[]{:S(2)}, u32[]{:S(2)}) collective-permute-start(bf16[4,48,768]{2,1,0:T(8,128)(2,1)S(1)} %get-tuple-element.177), channel_id=1, source_target_pairs={{4,0},{5,1},{6,2},{7,3},{0,4},{1,5},{2,6},{3,7},{12,8},{13,9},{14,... | collective-permute-start | bytes 884744 | tf_op jit(solution)/shard_map/ppermute | solution.py:56
  87.8 17.7 %collective-permute-start.17 = (bf16[4,48,768]{2,1,0:T(8,128)(2,1)S(1)}, bf16[4,48,768]{2,1,0:T(8,128)(2,1)S(1)}, u32[]{:S(2)}, u32[]{:S(2)}) collective-permute-start(bf16[4,48,768]{2,1,0:T(8,128)(2,1)S(1)} %get-tuple-element.181), channel_id=1, source_target_pairs={{4,0},{5,1},{6,2},{7,3},{0,4},{1,5},{2,6},{3,7},{12,8},{13,9},{14,... | collective-permute-start | bytes 884744 | tf_op jit(solution)/shard_map/ppermute | solution.py:56
  90.8 22.7 %collective-permute-start.21 = (bf16[4,48,768]{2,1,0:T(8,128)(2,1)}, bf16[4,48,768]{2,1,0:T(8,128)(2,1)}, u32[]{:S(2)}, u32[]{:S(2)}) collective-permute-start(bf16[4,48,768]{2,1,0:T(8,128)(2,1)} %get-tuple-element.180), channel_id=1, source_target_pairs={{2,0},{3,1},{0,2},{1,3},{6,4},{7,5},{4,6},{5,7},{10,8},{11,9},{8,1... | collective-permute-start | bytes 884744 | tf_op jit(solution)/shard_map/ppermute | solution.py:56
  99.2 85.8 %collective-permute-start.37 = (bf16[4,48,768]{2,1,0:T(8,128)(2,1)}, bf16[4,48,768]{2,1,0:T(8,128)(2,1)}, u32[]{:S(2)}, u32[]{:S(2)}) collective-permute-start(bf16[4,48,768]{2,1,0:T(8,128)(2,1)} %get-tuple-element.169), channel_id=1, source_target_pairs={{4,0},{5,1},{6,2},{7,3},{0,4},{1,5},{2,6},{3,7},{12,8},{13,9},{14,... | collective-permute-start | bytes 884744 | tf_op jit(solution)/shard_map/ppermute | solution.py:56
  108.0 52.4 %collective-permute-start.22 = (bf16[2,4,48,768]{3,2,1,0:T(8,128)(2,1)S(1)}, bf16[2,4,48,768]{3,2,1,0:T(8,128)(2,1)}, u32[]{:S(2)}, u32[]{:S(2)}) collective-permute-start(bf16[2,4,48,768]{3,2,1,0:T(8,128)(2,1)S(1)} %pad_maximum_fusion.5), channel_id=1, source_target_pairs={{4,0},{5,1},{6,2},{7,3},{0,4},{1,5},{2,6},{3,7},{12,8},{13,9},{14,... | collective-permute-start | bytes 1769480 | tf_op jit(solution)/shard_map/ppermute | solution.py:56
  115.9 50.8 %collective-permute-start.18 = (bf16[2,4,48,768]{3,2,1,0:T(8,128)(2,1)}, bf16[2,4,48,768]{3,2,1,0:T(8,128)(2,1)}, u32[]{:S(2)}, u32[]{:S(2)}) collective-permute-start(bf16[2,4,48,768]{3,2,1,0:T(8,128)(2,1)} %pad_maximum_fusion.2), channel_id=1, source_target_pairs={{2,0},{3,1},{0,2},{1,3},{6,4},{7,5},{4,6},{5,7},{10,8},{11,9},{8,1... | collective-permute-start | bytes 1769480 | tf_op jit(solution)/shard_map/ppermute | solution.py:56
  122.4 23.0 %collective-permute-start.8 = (bf16[384,768]{1,0:T(8,128)(2,1)}, bf16[384,768]{1,0:T(8,128)(2,1)}, u32[]{:S(2)}, u32[]{:S(2)}) collective-permute-start(bf16[384,768]{1,0:T(8,128)(2,1)} %bitcast.1058), channel_id=1, source_target_pairs={{1,0},{0,1},{3,2},{2,3},{5,4},{4,5},{7,6},{6,7},{9,8},{8,9},{11,10... | collective-permute-start | bytes 1769480 | tf_op jit(solution)/shard_map/ppermute | solution.py:56
  157.2 15.7 %collective-permute-start.19 = (bf16[2,4,48,768]{3,2,1,0:T(8,128)(2,1)}, bf16[2,4,48,768]{3,2,1,0:T(8,128)(2,1)}, u32[]{:S(2)}, u32[]{:S(2)}) collective-permute-start(bf16[2,4,48,768]{3,2,1,0:T(8,128)(2,1)} %pad_maximum_fusion.4), channel_id=1, source_target_pairs={{2,0},{3,1},{0,2},{1,3},{6,4},{7,5},{4,6},{5,7},{10,8},{11,9},{8,1... | collective-permute-start | bytes 1769480 | tf_op jit(solution)/shard_map/ppermute | solution.py:56
  160.9 16.7 %collective-permute-start.23 = (bf16[2,4,48,768]{3,2,1,0:T(8,128)(2,1)S(1)}, bf16[2,4,48,768]{3,2,1,0:T(8,128)(2,1)S(1)}, u32[]{:S(2)}, u32[]{:S(2)}) collective-permute-start(bf16[2,4,48,768]{3,2,1,0:T(8,128)(2,1)S(1)} %copy-done.73), channel_id=1, source_target_pairs={{4,0},{5,1},{6,2},{7,3},{0,4},{1,5},{2,6},{3,7},{12,8},{13,9},{14,... | collective-permute-start | bytes 1769480 | tf_op jit(solution)/shard_map/ppermute | solution.py:56
  179.1 15.6 %collective-permute-start.24 = (bf16[448,768]{1,0:T(8,128)(2,1)}, bf16[448,768]{1,0:T(8,128)(2,1)}, u32[]{:S(2)}, u32[]{:S(2)}) collective-permute-start(bf16[448,768]{1,0:T(8,128)(2,1)} %get-tuple-element.270), channel_id=1, source_target_pairs={{1,0},{0,1},{3,2},{2,3},{5,4},{4,5},{7,6},{6,7},{9,8},{8,9},{11,10... | collective-permute-start | bytes 2064392 | tf_op jit(solution)/shard_map/ppermute | solution.py:56
  183.7 15.3 %collective-permute-start.45 = (bf16[4,48,768]{2,1,0:T(8,128)(2,1)}, bf16[4,48,768]{2,1,0:T(8,128)(2,1)S(1)}, u32[]{:S(2)}, u32[]{:S(2)}) collective-permute-start(bf16[4,48,768]{2,1,0:T(8,128)(2,1)} %get-tuple-element.172), channel_id=1, source_target_pairs={{2,0},{3,1},{0,2},{1,3},{6,4},{7,5},{4,6},{5,7},{10,8},{11,9},{8,1... | collective-permute-start | bytes 884744 | tf_op jit(solution)/shard_map/ppermute | solution.py:56
  185.1 21.7 %collective-permute-start.31 = (bf16[2,4,32,768]{3,2,1,0:T(8,128)(2,1)S(1)}, bf16[2,4,32,768]{3,2,1,0:T(8,128)(2,1)S(1)}, u32[]{:S(2)}, u32[]{:S(2)}) collective-permute-start(bf16[2,4,32,768]{3,2,1,0:T(8,128)(2,1)S(1)} %get-tuple-element.188), channel_id=1, source_target_pairs={{2,0},{3,1},{0,2},{1,3},{6,4},{7,5},{4,6},{5,7},{10,8},{11,9},{8,1... | collective-permute-start | bytes 1179656 | tf_op jit(solution)/shard_map/ppermute | solution.py:56
  190.0 82.0 %collective-permute-start.42 = (bf16[2,4,48,768]{3,2,1,0:T(8,128)(2,1)}, bf16[2,4,48,768]{3,2,1,0:T(8,128)(2,1)}, u32[]{:S(2)}, u32[]{:S(2)}) collective-permute-start(bf16[2,4,48,768]{3,2,1,0:T(8,128)(2,1)} %pad_maximum_fusion.8), channel_id=1, source_target_pairs={{2,0},{3,1},{0,2},{1,3},{6,4},{7,5},{4,6},{5,7},{10,8},{11,9},{8,1... | collective-permute-start | bytes 1769480 | tf_op jit(solution)/shard_map/ppermute | solution.py:56
  192.8 81.0 %collective-permute-start.43 = (bf16[2,4,48,768]{3,2,1,0:T(8,128)(2,1)}, bf16[2,4,48,768]{3,2,1,0:T(8,128)(2,1)}, u32[]{:S(2)}, u32[]{:S(2)}) collective-permute-start(bf16[2,4,48,768]{3,2,1,0:T(8,128)(2,1)} %pad_maximum_fusion.10), channel_id=1, source_target_pairs={{2,0},{3,1},{0,2},{1,3},{6,4},{7,5},{4,6},{5,7},{10,8},{11,9},{8,1... | collective-permute-start | bytes 1769480 | tf_op jit(solution)/shard_map/ppermute | solution.py:56
  194.8 93.4 %collective-permute-start.46 = (bf16[2,4,48,768]{3,2,1,0:T(8,128)(2,1)}, bf16[2,4,48,768]{3,2,1,0:T(8,128)(2,1)}, u32[]{:S(2)}, u32[]{:S(2)}) collective-permute-start(bf16[2,4,48,768]{3,2,1,0:T(8,128)(2,1)} %pad_maximum_fusion.11), channel_id=1, source_target_pairs={{4,0},{5,1},{6,2},{7,3},{0,4},{1,5},{2,6},{3,7},{12,8},{13,9},{14,... | collective-permute-start | bytes 1769480 | tf_op jit(solution)/shard_map/ppermute | solution.py:56
  199.0 37.2 %collective-permute-start.25 = (bf16[448,192]{1,0:T(8,128)(2,1)S(1)}, bf16[448,192]{1,0:T(8,128)(2,1)S(1)}, u32[]{:S(2)}, u32[]{:S(2)}) collective-permute-start(bf16[448,192]{1,0:T(8,128)(2,1)S(1)} %get-tuple-element.199), channel_id=1, source_target_pairs={{2,0},{3,1},{0,2},{1,3},{6,4},{7,5},{4,6},{5,7},{10,8},{11,9},{8,1... | collective-permute-start | bytes 516104 | tf_op jit(solution)/shard_map/ppermute | solution.py:56
  206.8 92.0 %collective-permute-start.47 = (bf16[2,4,48,768]{3,2,1,0:T(8,128)(2,1)}, bf16[2,4,48,768]{3,2,1,0:T(8,128)(2,1)}, u32[]{:S(2)}, u32[]{:S(2)}) collective-permute-start(bf16[2,4,48,768]{3,2,1,0:T(8,128)(2,1)} %pad_maximum_fusion.12), channel_id=1, source_target_pairs={{4,0},{5,1},{6,2},{7,3},{0,4},{1,5},{2,6},{3,7},{12,8},{13,9},{14,... | collective-permute-start | bytes 1769480 | tf_op jit(solution)/shard_map/ppermute | solution.py:56
  236.2 14.3 %collective-permute-start.32 = (bf16[384,768]{1,0:T(8,128)(2,1)}, bf16[384,768]{1,0:T(8,128)(2,1)}, u32[]{:S(2)}, u32[]{:S(2)}) collective-permute-start(bf16[384,768]{1,0:T(8,128)(2,1)} %bitcast.107), channel_id=1, source_target_pairs={{1,0},{0,1},{3,2},{2,3},{5,4},{4,5},{7,6},{6,7},{9,8},{8,9},{11,10... | collective-permute-start | bytes 1769480 | tf_op jit(solution)/shard_map/ppermute | solution.py:56
  304.2 47.5 %collective-permute-start.48 = (bf16[448,768]{1,0:T(8,128)(2,1)}, bf16[448,768]{1,0:T(8,128)(2,1)}, u32[]{:S(2)}, u32[]{:S(2)}) collective-permute-start(bf16[448,768]{1,0:T(8,128)(2,1)} %get-tuple-element.282), channel_id=1, source_target_pairs={{1,0},{0,1},{3,2},{2,3},{5,4},{4,5},{7,6},{6,7},{9,8},{8,9},{11,10... | collective-permute-start | bytes 2064392 | tf_op jit(solution)/shard_map/ppermute | solution.py:56
  313.6 34.8 %collective-permute-start.49 = (bf16[448,768]{1,0:T(8,128)(2,1)}, bf16[448,768]{1,0:T(8,128)(2,1)}, u32[]{:S(2)}, u32[]{:S(2)}) collective-permute-start(bf16[448,768]{1,0:T(8,128)(2,1)} %get-tuple-element.280), channel_id=1, source_target_pairs={{1,0},{0,1},{3,2},{2,3},{5,4},{4,5},{7,6},{6,7},{9,8},{8,9},{11,10... | collective-permute-start | bytes 2064392 | tf_op jit(solution)/shard_map/ppermute | solution.py:56
  313.6 16.4 %collective-permute-start.104 = (bf16[2,4,48,768]{3,2,1,0:T(8,128)(2,1)}, bf16[2,4,48,768]{3,2,1,0:T(8,128)(2,1)}, u32[]{:S(2)}, u32[]{:S(2)}) collective-permute-start(bf16[2,4,48,768]{3,2,1,0:T(8,128)(2,1)} %bitcast.265), channel_id=1, source_target_pairs={{2,0},{3,1},{0,2},{1,3},{6,4},{7,5},{4,6},{5,7},{10,8},{11,9},{8,1... | collective-permute-start | bytes 1769480 | tf_op jit(solution)/shard_map/ppermute | solution.py:56
  315.3 17.7 %collective-permute-start.109 = (bf16[2,4,48,768]{3,2,1,0:T(8,128)(2,1)}, bf16[2,4,48,768]{3,2,1,0:T(8,128)(2,1)}, u32[]{:S(2)}, u32[]{:S(2)}) collective-permute-start(bf16[2,4,48,768]{3,2,1,0:T(8,128)(2,1)} %bitcast.270), channel_id=1, source_target_pairs={{4,0},{5,1},{6,2},{7,3},{0,4},{1,5},{2,6},{3,7},{12,8},{13,9},{14,... | collective-permute-start | bytes 1769480 | tf_op jit(solution)/shard_map/ppermute | solution.py:56
  325.5 16.7 %collective-permute-start.84 = (bf16[2,4,48,768]{3,2,1,0:T(8,128)(2,1)S(1)}, bf16[2,4,48,768]{3,2,1,0:T(8,128)(2,1)S(1)}, u32[]{:S(2)}, u32[]{:S(2)}) collective-permute-start(bf16[2,4,48,768]{3,2,1,0:T(8,128)(2,1)S(1)} %bitcast.1091), channel_id=1, source_target_pairs={{2,0},{3,1},{0,2},{1,3},{6,4},{7,5},{4,6},{5,7},{10,8},{11,9},{8,1... | collective-permute-start | bytes 1769480 | tf_op jit(solution)/shard_map/ppermute | solution.py:56
  330.0 16.3 %collective-permute-start.89 = (bf16[2,4,48,768]{3,2,1,0:T(8,128)(2,1)S(1)}, bf16[2,4,48,768]{3,2,1,0:T(8,128)(2,1)S(1)}, u32[]{:S(2)}, u32[]{:S(2)}) collective-permute-start(bf16[2,4,48,768]{3,2,1,0:T(8,128)(2,1)S(1)} %bitcast.1092), channel_id=1, source_target_pairs={{4,0},{5,1},{6,2},{7,3},{0,4},{1,5},{2,6},{3,7},{12,8},{13,9},{14,... | collective-permute-start | bytes 1769480 | tf_op jit(solution)/shard_map/ppermute | solution.py:56
  333.1 76.0 %collective-permute-start.105 = (bf16[4,48,768]{2,1,0:T(8,128)(2,1)}, bf16[4,48,768]{2,1,0:T(8,128)(2,1)}, u32[]{:S(2)}, u32[]{:S(2)}) collective-permute-start(bf16[4,48,768]{2,1,0:T(8,128)(2,1)} %slice_bitcast_fusion.2), channel_id=1, source_target_pairs={{4,0},{5,1},{6,2},{7,3},{0,4},{1,5},{2,6},{3,7},{12,8},{13,9},{14,... | collective-permute-start | bytes 884744 | tf_op jit(solution)/shard_map/ppermute | solution.py:56
  342.2 69.0 %collective-permute-start.110 = (bf16[4,48,768]{2,1,0:T(8,128)(2,1)}, bf16[4,48,768]{2,1,0:T(8,128)(2,1)}, u32[]{:S(2)}, u32[]{:S(2)}) collective-permute-start(bf16[4,48,768]{2,1,0:T(8,128)(2,1)} %slice_bitcast_fusion), channel_id=1, source_target_pairs={{2,0},{3,1},{0,2},{1,3},{6,4},{7,5},{4,6},{5,7},{10,8},{11,9},{8,1... | collective-permute-start | bytes 884744 | tf_op jit(solution)/shard_map/ppermute | solution.py:56
  346.3 68.5 %collective-permute-start.85 = (bf16[4,48,768]{2,1,0:T(8,128)(2,1)}, bf16[4,48,768]{2,1,0:T(8,128)(2,1)}, u32[]{:S(2)}, u32[]{:S(2)}) collective-permute-start(bf16[4,48,768]{2,1,0:T(8,128)(2,1)} %slice_bitcast_fusion.10), channel_id=1, source_target_pairs={{4,0},{5,1},{6,2},{7,3},{0,4},{1,5},{2,6},{3,7},{12,8},{13,9},{14,... | collective-permute-start | bytes 884744 | tf_op jit(solution)/shard_map/ppermute | solution.py:56
  348.3 67.7 %collective-permute-start.90 = (bf16[4,48,768]{2,1,0:T(8,128)(2,1)}, bf16[4,48,768]{2,1,0:T(8,128)(2,1)}, u32[]{:S(2)}, u32[]{:S(2)}) collective-permute-start(bf16[4,48,768]{2,1,0:T(8,128)(2,1)} %slice_bitcast_fusion.8), channel_id=1, source_target_pairs={{2,0},{3,1},{0,2},{1,3},{6,4},{7,5},{4,6},{5,7},{10,8},{11,9},{8,1... | collective-permute-start | bytes 884744 | tf_op jit(solution)/shard_map/ppermute | solution.py:56
  368.4 76.4 %collective-permute-start.68 = (bf16[384,768]{1,0:T(8,128)(2,1)}, bf16[384,768]{1,0:T(8,128)(2,1)}, u32[]{:S(2)}, u32[]{:S(2)}) collective-permute-start(bf16[384,768]{1,0:T(8,128)(2,1)} %slice.850), channel_id=1, source_target_pairs={{1,0},{0,1},{3,2},{2,3},{5,4},{4,5},{7,6},{6,7},{9,8},{8,9},{11,10... | collective-permute-start | bytes 1769480 | tf_op jit(solution)/shard_map/ppermute | solution.py:56
  409.1 80.2 %collective-permute-start.118 = (bf16[4,195,512]{2,0,1:T(4,128)(2,1)}, bf16[4,195,512]{2,0,1:T(4,128)(2,1)}, u32[]{:S(2)}, u32[]{:S(2)}) collective-permute-start(bf16[4,195,512]{2,0,1:T(4,128)(2,1)} %copy.405), channel_id=1, source_target_pairs={{4,0},{5,1},{6,2},{7,3},{0,4},{1,5},{2,6},{3,7},{12,8},{13,9},{14,... | collective-permute-start | bytes 2396168 | tf_op jit(solution)/shard_map/ppermute | solution.py:56
  447.9 43.1 %collective-permute-start.69 = (bf16[2,4,32,768]{3,2,1,0:T(8,128)(2,1)}, bf16[2,4,32,768]{3,2,1,0:T(8,128)(2,1)}, u32[]{:S(2)}, u32[]{:S(2)}) collective-permute-start(bf16[2,4,32,768]{3,2,1,0:T(8,128)(2,1)} %fusion.260), channel_id=1, source_target_pairs={{2,0},{3,1},{0,2},{1,3},{6,4},{7,5},{4,6},{5,7},{10,8},{11,9},{8,1... | collective-permute-start | bytes 1179656 | tf_op jit(solution)/shard_map/ppermute | solution.py:56
  475.1 77.0 %collective-permute-start.53 = (bf16[448,768]{1,0:T(8,128)(2,1)}, bf16[448,768]{1,0:T(8,128)(2,1)}, u32[]{:S(2)}, u32[]{:S(2)}) collective-permute-start(bf16[448,768]{1,0:T(8,128)(2,1)} %get-tuple-element.285), channel_id=1, source_target_pairs={{1,0},{0,1},{3,2},{2,3},{5,4},{4,5},{7,6},{6,7},{9,8},{8,9},{11,10... | collective-permute-start | bytes 2064392 | tf_op jit(solution)/shard_map/ppermute | solution.py:56
  475.3 50.7 %collective-permute-start.94 = (bf16[2,4,48,768]{3,2,1,0:T(8,128)(2,1)}, bf16[2,4,48,768]{3,2,1,0:T(8,128)(2,1)}, u32[]{:S(2)}, u32[]{:S(2)}) collective-permute-start(bf16[2,4,48,768]{3,2,1,0:T(8,128)(2,1)} %bitcast.254), channel_id=1, source_target_pairs={{2,0},{3,1},{0,2},{1,3},{6,4},{7,5},{4,6},{5,7},{10,8},{11,9},{8,1... | collective-permute-start | bytes 1769480 | tf_op jit(solution)/shard_map/ppermute | solution.py:56
  494.7 18.0 %collective-permute-start.120 = (bf16[1,195,512]{2,1,0:T(8,128)(2,1)S(1)}, bf16[1,195,512]{2,1,0:T(8,128)(2,1)S(1)}, u32[]{:S(2)}, u32[]{:S(2)}) collective-permute-start(bf16[1,195,512]{2,1,0:T(8,128)(2,1)S(1)} %get-tuple-element.164), channel_id=1, source_target_pairs={{16,0},{17,1},{18,2},{19,3},{20,4},{21,5},{22,6},{23,7},{24,8},{25... | collective-permute-start | bytes 599048 | tf_op jit(solution)/shard_map/ppermute | solution.py:56
  500.0 13.4 %collective-permute-start.121 = (bf16[1,195,512]{2,1,0:T(8,128)(2,1)S(1)}, bf16[1,195,512]{2,1,0:T(8,128)(2,1)S(1)}, u32[]{:S(2)}, u32[]{:S(2)}) collective-permute-start(bf16[1,195,512]{2,1,0:T(8,128)(2,1)S(1)} %get-tuple-element.165), channel_id=1, source_target_pairs={{8,0},{9,1},{10,2},{11,3},{12,4},{13,5},{14,6},{15,7},{16,8},{17,9... | collective-permute-start | bytes 599048 | tf_op jit(solution)/shard_map/ppermute | solution.py:56
  503.9 16.2 %collective-permute-start.71 = (bf16[1,32,768]{2,1,0:T(8,128)(2,1)}, bf16[1,32,768]{2,1,0:T(8,128)(2,1)S(1)}, u32[]{:S(2)}, u32[]{:S(2)}) collective-permute-start(bf16[1,32,768]{2,1,0:T(8,128)(2,1)} %get-tuple-element.233), channel_id=1, source_target_pairs={{24,0},{25,1},{26,2},{27,3},{28,4},{29,5},{30,6},{31,7},{0,8},{1,9... | collective-permute-start | bytes 147464 | tf_op jit(solution)/shard_map/ppermute | solution.py:56
  520.2 16.5 %collective-permute-start.99 = (bf16[2,4,48,768]{3,2,1,0:T(8,128)(2,1)}, bf16[2,4,48,768]{3,2,1,0:T(8,128)(2,1)S(1)}, u32[]{:S(2)}, u32[]{:S(2)}) collective-permute-start(bf16[2,4,48,768]{3,2,1,0:T(8,128)(2,1)} %bitcast.1090), channel_id=1, source_target_pairs={{4,0},{5,1},{6,2},{7,3},{0,4},{1,5},{2,6},{3,7},{12,8},{13,9},{14,... | collective-permute-start | bytes 1769480 | tf_op jit(solution)/shard_map/ppermute | solution.py:56
  521.9 17.4 %collective-permute-start.74 = (bf16[2,4,48,768]{3,2,1,0:T(8,128)(2,1)}, bf16[2,4,48,768]{3,2,1,0:T(8,128)(2,1)S(1)}, u32[]{:S(2)}, u32[]{:S(2)}) collective-permute-start(bf16[2,4,48,768]{3,2,1,0:T(8,128)(2,1)} %bitcast.1089), channel_id=1, source_target_pairs={{2,0},{3,1},{0,2},{1,3},{6,4},{7,5},{4,6},{5,7},{10,8},{11,9},{8,1... | collective-permute-start | bytes 1769480 | tf_op jit(solution)/shard_map/ppermute | solution.py:56
  523.7 25.6 %collective-permute-start.79 = (bf16[2,4,48,768]{3,2,1,0:T(8,128)(2,1)}, bf16[2,4,48,768]{3,2,1,0:T(8,128)(2,1)S(1)}, u32[]{:S(2)}, u32[]{:S(2)}) collective-permute-start(bf16[2,4,48,768]{3,2,1,0:T(8,128)(2,1)} %bitcast.1088), channel_id=1, source_target_pairs={{4,0},{5,1},{6,2},{7,3},{0,4},{1,5},{2,6},{3,7},{12,8},{13,9},{14,... | collective-permute-start | bytes 1769480 | tf_op jit(solution)/shard_map/ppermute | solution.py:56
  528.1 70.6 %collective-permute-start.95 = (bf16[4,48,768]{2,1,0:T(8,128)(2,1)}, bf16[4,48,768]{2,1,0:T(8,128)(2,1)}, u32[]{:S(2)}, u32[]{:S(2)}) collective-permute-start(bf16[4,48,768]{2,1,0:T(8,128)(2,1)} %slice_bitcast_fusion.6), channel_id=1, source_target_pairs={{4,0},{5,1},{6,2},{7,3},{0,4},{1,5},{2,6},{3,7},{12,8},{13,9},{14,... | collective-permute-start | bytes 884744 | tf_op jit(solution)/shard_map/ppermute | solution.py:56
  537.6 64.0 %collective-permute-start.100 = (bf16[4,48,768]{2,1,0:T(8,128)(2,1)}, bf16[4,48,768]{2,1,0:T(8,128)(2,1)}, u32[]{:S(2)}, u32[]{:S(2)}) collective-permute-start(bf16[4,48,768]{2,1,0:T(8,128)(2,1)} %slice_bitcast_fusion.4), channel_id=1, source_target_pairs={{2,0},{3,1},{0,2},{1,3},{6,4},{7,5},{4,6},{5,7},{10,8},{11,9},{8,1... | collective-permute-start | bytes 884744 | tf_op jit(solution)/shard_map/ppermute | solution.py:56
  540.3 63.0 %collective-permute-start.75 = (bf16[4,48,768]{2,1,0:T(8,128)(2,1)}, bf16[4,48,768]{2,1,0:T(8,128)(2,1)}, u32[]{:S(2)}, u32[]{:S(2)}) collective-permute-start(bf16[4,48,768]{2,1,0:T(8,128)(2,1)} %slice_bitcast_fusion.14), channel_id=1, source_target_pairs={{4,0},{5,1},{6,2},{7,3},{0,4},{1,5},{2,6},{3,7},{12,8},{13,9},{14,... | collective-permute-start | bytes 884744 | tf_op jit(solution)/shard_map/ppermute | solution.py:56
  550.3 55.7 %collective-permute-start.80 = (bf16[4,48,768]{2,1,0:T(8,128)(2,1)}, bf16[4,48,768]{2,1,0:T(8,128)(2,1)}, u32[]{:S(2)}, u32[]{:S(2)}) collective-permute-start(bf16[4,48,768]{2,1,0:T(8,128)(2,1)} %slice_bitcast_fusion.12), channel_id=1, source_target_pairs={{2,0},{3,1},{0,2},{1,3},{6,4},{7,5},{4,6},{5,7},{10,8},{11,9},{8,1... | collective-permute-start | bytes 884744 | tf_op jit(solution)/shard_map/ppermute | solution.py:56
  564.5 80.9 %collective-permute-start.62 = (bf16[384,768]{1,0:T(8,128)(2,1)}, bf16[384,768]{1,0:T(8,128)(2,1)}, u32[]{:S(2)}, u32[]{:S(2)}) collective-permute-start(bf16[384,768]{1,0:T(8,128)(2,1)} %slice.841), channel_id=1, source_target_pairs={{1,0},{0,1},{3,2},{2,3},{5,4},{4,5},{7,6},{6,7},{9,8},{8,9},{11,10... | collective-permute-start | bytes 1769480 | tf_op jit(solution)/shard_map/ppermute | solution.py:56
  598.7 35.0 %collective-permute-start.114 = (bf16[4,31,512]{2,1,0:T(8,128)(2,1)S(1)}, bf16[4,31,512]{2,1,0:T(8,128)(2,1)S(1)}, u32[]{:S(2)}, u32[]{:S(2)}) collective-permute-start(bf16[4,31,512]{2,1,0:T(8,128)(2,1)S(1)} %dynamic-slice_bitcast_fusion.4), channel_id=1, source_target_pairs={{4,0},{5,1},{6,2},{7,3},{0,4},{1,5},{2,6},{3,7},{12,8},{13,9},{14,... | collective-permute-start | bytes 380936 | tf_op jit(solution)/shard_map/ppermute | solution.py:56
  629.9 15.4 %collective-permute-start.55 = (bf16[448,192]{0,1:T(8,128)(2,1)S(1)}, bf16[448,192]{0,1:T(8,128)(2,1)S(1)}, u32[]{:S(2)}, u32[]{:S(2)}) collective-permute-start(bf16[448,192]{0,1:T(8,128)(2,1)S(1)} %bitcast.1080), channel_id=1, source_target_pairs={{2,0},{3,1},{0,2},{1,3},{6,4},{7,5},{4,6},{5,7},{10,8},{11,9},{8,1... | collective-permute-start | bytes 516104 | tf_op jit(solution)/shard_map/ppermute | solution.py:56
  648.4 22.5 %collective-permute-start.63 = (bf16[2,4,32,768]{3,2,1,0:T(8,128)(2,1)}, bf16[2,4,32,768]{3,2,1,0:T(8,128)(2,1)S(1)}, u32[]{:S(2)}, u32[]{:S(2)}) collective-permute-start(bf16[2,4,32,768]{3,2,1,0:T(8,128)(2,1)} %fusion.258), channel_id=1, source_target_pairs={{2,0},{3,1},{0,2},{1,3},{6,4},{7,5},{4,6},{5,7},{10,8},{11,9},{8,1... | collective-permute-start | bytes 1179656 | tf_op jit(solution)/shard_map/ppermute | solution.py:56
  (342 other events, 2081.9 us)

commit v2 on v1

v2 whole, which is shorter than its diff:
```python
import math
from functools import partial

import jax
import jax.numpy as jnp
import numpy as np
from jax import lax
from jax.experimental import pallas as pl
from jax.experimental.pallas import tpu as pltpu
from jax.sharding import PartitionSpec as P

HD = 64
LC = 512
LA = 128
LB = 256
LAYERS = 2
D = 768

EPSILON = 1e-05
MASKED_SCORE = -1e30
AXES = ("wide", "head")
ROW_TILE = 112
SCORE_TILE = 256
VMEM_LIMIT = 56 * 1024 * 1024
f32 = jnp.float32
bf16 = jnp.bfloat16


class Links:
    def __init__(self, n_wide, n_head):
        self.nx, self.nc = 2, 2
        self.nz, self.ny = n_wide // 2, n_head // 2
        self.n_head = n_head
        self.n_wide = n_wide
        self.digits = []
        stride, left = 1, self.nz
        while left > 1:
            count = 4 if left % 4 == 0 else 2 if left % 2 == 0 else left
            self.digits.append((stride, count))
            stride, left = stride * count, left // count

    def number(self, z, x, y, c):
        return ((z * self.nx + x) * self.ny + y) * self.nc + c

    def places(self):
        wide, head = lax.axis_index("wide"), lax.axis_index("head")
        return wide // self.nx, wide % self.nx, head // self.nc, head % self.nc

    def grid(self):
        return np.ndindex(self.nz, self.nx, self.ny, self.nc)

    def take(self, v, z=0, x=0, y=0, c=0):
        pairs = [
            (
                self.number(
                    (i + z) % self.nz, (j + x) % self.nx, (k + y) % self.ny, (m + c) % self.nc
                ),
                self.number(i, j, k, m),
            )
            for i, j, k, m in self.grid()
        ]
        return lax.ppermute(v, AXES, pairs)

    def give(self, v, z=0, x=0, y=0, c=0):
        return self.take(v, -z, -x, -y, -c)

    def take_bit(self, v, bit):
        pairs = [
            (self.number(i ^ bit, j, k, m), self.number(i, j, k, m)) for i, j, k, m in self.grid()
        ]
        return lax.ppermute(v, AXES, pairs)

    def total(self, v):
        v = v + self.take(v, x=1)
        v = v + self.take(v, y=1)
        bit = 1
        while bit < self.nz:
            v = v + self.take_bit(v, bit)
            bit = bit * 2
        return 0.5 * (v + self.take(v, c=1))

    def spread_z(self, v):
        v = v[None]
        for stride, count in self.digits:
            v = jnp.concatenate([v] + [self.take(v, z=stride * k) for k in range(1, count)], axis=0)
        return v

    def gather_z(self, v):
        for stride, count in reversed(self.digits):
            parts = v.reshape(count, v.shape[0] // count, *v.shape[1:])
            total = parts[0].astype(f32)
            for k in range(1, count):
                total = total + self.give(parts[k], z=stride * k).astype(f32)
            v = total if stride == 1 else total.astype(bf16)
        return v.reshape(v.shape[1:])

    def spread(self, v):
        half = v.shape[0] // 2
        zs = self.spread_z(v)
        a, b = zs[:, :half], zs[:, half:]
        a = jnp.stack([a, self.take(a, x=1)])
        b = jnp.stack([b, self.take(b, y=1)])
        return [a, self.take(a, y=1), b, self.take(b, x=1)]

    def fold(self, own, other, **step):
        return (own.astype(f32) + self.give(other, **step).astype(f32)).astype(bf16)

    def collect(self, blocks):
        a = self.fold(blocks[0], blocks[1], y=1)
        b = self.fold(blocks[2], blocks[3], x=1)
        a = self.fold(a[0], a[1], x=1)
        b = self.fold(b[0], b[1], y=1)
        return jnp.concatenate([self.gather_z(a), self.gather_z(b)], axis=0)

    def spread_one(self, v):
        v = self.spread_z(v)
        v = jnp.stack([v, self.take(v, x=1)])
        return jnp.stack([v, self.take(v, y=1)])

    def collect_one(self, v):
        v = self.fold(v[0], v[1], y=1)
        v = self.fold(v[0], v[1], x=1)
        return self.gather_z(v)

    def collect_wide(self, v, z, x):
        v = v.reshape(self.nz, self.nx, *v.shape[1:])
        own = lax.dynamic_index_in_dim(v, x, 1, keepdims=False)
        other = lax.dynamic_index_in_dim(v, 1 - x, 1, keepdims=False)
        v = self.fold(own, other, x=1)
        v = lax.dynamic_slice_in_dim(jnp.concatenate([v, v], axis=0), z, self.nz, axis=0)
        return self.gather_z(v)


def stage(kernel, outs, args, scratch=(), smem=0, flops=0):
    spaces = [pltpu.SMEM] * smem + [pltpu.VMEM] * (len(args) - smem)
    size = sum(a.size * a.dtype.itemsize for a in args[smem:])
    size = size + sum(math.prod(s) * jnp.dtype(d).itemsize for s, d in outs)
    return pl.pallas_call(
        kernel,
        out_shape=[jax.ShapeDtypeStruct(s, d) for s, d in outs],
        in_specs=[pl.BlockSpec(memory_space=s) for s in spaces],
        out_specs=[pl.BlockSpec(memory_space=pltpu.VMEM) for _ in outs],
        scratch_shapes=list(scratch),
        compiler_params=pltpu.CompilerParams(vmem_limit_bytes=VMEM_LIMIT),
        cost_estimate=pl.CostEstimate(flops=flops, bytes_accessed=size, transcendentals=0),
    )(*args)


def mm(a, b):
    return lax.dot_general(a, b, (((1,), (0,)), ((), ())), preferred_element_type=f32)


def mm_nt(a, b):
    return lax.dot_general(a, b, (((1,), (1,)), ((), ())), preferred_element_type=f32)


def mm_tn(a, b):
    return lax.dot_general(a, b, (((0,), (0,)), ((), ())), preferred_element_type=f32)


def tiles(rows):
    return [pl.ds(i, ROW_TILE) for i in range(0, rows, ROW_TILE)]


def centre(v):
    middle = jnp.mean(v, axis=-1, keepdims=True)
    centred = v - middle
    scale = lax.rsqrt(jnp.mean(centred * centred, axis=-1, keepdims=True) + EPSILON)
    return centred * scale, scale


def norm_back(v, gain, d_out):
    unit, scale = centre(v)
    inner = d_out * gain
    flat = jnp.mean(inner, axis=-1, keepdims=True)
    along = jnp.mean(inner * unit, axis=-1, keepdims=True)
    d_rows = scale * (inner - flat - unit * along)
    return d_rows, jnp.sum(d_out * unit, axis=0, keepdims=True), jnp.sum(d_out, 0, keepdims=True)


def gelu_both(v):
    k = math.sqrt(2.0 / math.pi)
    square = v * v
    t = jnp.tanh(k * v * (1.0 + 0.044715 * square))
    half = 0.5 * (1.0 + t)
    slope = half + 0.5 * v * (1.0 - t * t) * (k * (1.0 + 3 * 0.044715 * square))
    return v * half, slope


def first_norm_kernel(tokens, gain, shift, pick, own, far):
    for t in tiles(tokens.shape[0]):
        unit, _ = centre(tokens[t, :].astype(f32))
        normed = (unit * gain[...] + shift[...]).astype(bf16)
        picked = mm(normed, pick[...]).astype(bf16)
        own[t, :] = picked[:, : own.shape[1]]
        far[t, :] = picked[:, own.shape[1] :]


def next_norm_kernel(resid, part, got, bias, gain, shift, pick, rows, own, far):
    for t in tiles(resid.shape[0]):
        v = resid[t, :] + part[t, :].astype(f32) + got[t, :].astype(f32) + bias[...]
        rows[t, :] = v
        unit, _ = centre(v)
        normed = (unit * gain[...] + shift[...]).astype(bf16)
        picked = mm(normed, pick[...]).astype(bf16)
        own[t, :] = picked[:, : own.shape[1]]
        far[t, :] = picked[:, own.shape[1] :]


def join_kernel(near, far, weight, part):
    cols = near.shape[1]
    total = mm(near[...], weight[:cols, :]) + mm(far[...], weight[cols:, :])
    part[...] = total.astype(bf16)


def ffn_kernel(n, rows, part, got, bias, gain, shift, *refs):
    ups, biases, downs = refs[:n], refs[n : 2 * n], refs[2 * n : 3 * n]
    resid, normed, ffn = refs[3 * n : 3 * n + 3]
    hiddens, slopes = refs[3 * n + 3 : 4 * n + 3], refs[4 * n + 3 :]
    for t in tiles(rows.shape[0]):
        v = rows[t, :].astype(f32) + part[t, :].astype(f32) + got[t, :].astype(f32) + bias[...]
        resid[t, :] = v
        unit, _ = centre(v)
        normed[t, :] = (unit * gain[...] + shift[...]).astype(bf16)
    total = None
    for up, b, down, hidden, slope in zip(ups, biases, downs, hiddens, slopes):
        value, grad = gelu_both(mm_nt(normed[...], up[...]) + b[...])
        hidden[...] = value.astype(bf16)
        slope[...] = grad.astype(bf16)
        term = mm(hidden[...], down[...])
        total = term if total is None else total + term
    ffn[...] = total.astype(bf16)


def ffn_back_kernel(n, grad_rows, normed, *refs):
    ups, downs, hiddens, slopes = (refs[i * n : (i + 1) * n] for i in range(4))
    d_normed, bias_grad = refs[4 * n : 4 * n + 2]
    down_grads, up_grads, hidden_bias = (
        refs[4 * n + 2 + i * n : 4 * n + 2 + (i + 1) * n] for i in range(3)
    )
    d_ffn = grad_rows[...].astype(bf16)
    bias_grad[...] = jnp.sum(d_ffn.astype(f32), axis=0, keepdims=True)
    total = None
    for k in range(n):
        d_pre = (mm_nt(d_ffn, downs[k][...]) * slopes[k][...].astype(f32)).astype(bf16)
        down_grads[k][...] = mm_tn(hiddens[k][...], d_ffn).astype(bf16)
        hidden_bias[k][...] = jnp.sum(d_pre.astype(f32), axis=0, keepdims=True)
        up_grads[k][...] = mm_tn(d_pre, normed[...]).astype(bf16)
        term = mm(d_pre, ups[k][...])
        total = term if total is None else total + term
    d_normed[...] = total.astype(bf16)


def join_back_kernel(
    grad_rows, part, got, resid, gain, weight, near, far, pick,
    d_resid, d_near, d_far, gain_grad, shift_grad, bias_grad, out_near, out_far, d_join,
):
    gain_grad[...] = jnp.zeros_like(gain_grad)
    shift_grad[...] = jnp.zeros_like(shift_grad)
    bias_grad[...] = jnp.zeros_like(bias_grad)
    for t in tiles(resid.shape[0]):
        d_out = part[t, :].astype(f32) + got[t, :].astype(f32)
        d_rows, d_gain, d_shift = norm_back(resid[t, :], gain[...], d_out)
        gain_grad[...] += d_gain
        shift_grad[...] += d_shift
        d_rows = d_rows + grad_rows[t, :].astype(f32)
        d_resid[t, :] = d_rows
        low = d_rows.astype(bf16)
        d_join[t, :] = low
        bias_grad[...] += jnp.sum(low.astype(f32), axis=0, keepdims=True)
    cols = near.shape[1]
    d_near[...] = mm_nt(d_join[...], weight[:cols, :]).astype(bf16)
    d_far[...] = mm_nt(d_join[...], weight[cols:, :]).astype(bf16)
    grad = mm_tn(pick[:cols, :], mm_tn(near[...], d_join[...]).astype(bf16))
    grad = grad + mm_tn(pick[cols:, :], mm_tn(far[...], d_join[...]).astype(bf16))
    half = out_near.shape[0]
    out_near[...] = grad[:half].astype(bf16)
    out_far[...] = grad[half:].astype(bf16)


def rows_back_kernel(
    d_resid, near, far, peer_near, peer_far, place, rows, gain, grad_rows, gain_grad, shift_grad
):
    cols = near.shape[1]
    gain_grad[...] = jnp.zeros_like(gain_grad)
    shift_grad[...] = jnp.zeros_like(shift_grad)
    for t in tiles(rows.shape[0]):
        d_out = mm(near[t, :], place[:cols, :]) + mm(far[t, :], place[cols : 2 * cols, :])
        d_out = d_out + mm(peer_near[t, :], place[2 * cols : 3 * cols, :])
        d_out = d_out + mm(peer_far[t, :], place[3 * cols :, :])
        d_rows, d_gain, d_shift = norm_back(rows[t, :].astype(f32), gain[...], d_out)
        gain_grad[...] += d_gain
        shift_grad[...] += d_shift
        grad_rows[t, :] = d_resid[t, :] + d_rows


def group_pieces(counts):
    total = sum(counts)
    start = 0
    found = []
    for bucket, n in enumerate(counts):
        for chip in range(2):
            for core in range(2):
                found.append((bucket, chip, core * total + start, (2 * chip + core) * n, n))
        start = start + n
    return found


def load_groups(counts, y, near, far, whole, buckets):
    whole[y] = near[...]
    whole[1 - y] = far[...]
    for bucket, chip, source, target, n in group_pieces(counts):
        buckets[bucket][target : target + n, :] = whole[chip, source : source + n, :]


def store_groups(counts, y, buckets, whole, near, far):
    for bucket, chip, source, target, n in group_pieces(counts):
        whole[chip, source : source + n, :] = buckets[bucket][target : target + n, :]
    near[...] = whole[y]
    far[...] = whole[1 - y]


def head_lanes(shape, h):
    return lax.broadcasted_iota(jnp.int32, shape, 1) // HD == h


def only_head(v, h):
    return jnp.where(head_lanes(v.shape, h), v, jnp.zeros_like(v))


def soft(level, h, act, length, span, second, second_bias, random, tile):
    if level == 0:
        scores = mm(only_head(act, h), second[:, :span]) + second_bias[h : h + 1, :span]
    else:
        scores = random[h, tile, :span].astype(f32)
    keys = lax.broadcasted_iota(jnp.int32, scores.shape, 1) < length
    scores = jnp.where(keys, scores, MASKED_SCORE)
    e = jnp.exp(scores - jnp.max(scores, axis=-1, keepdims=True))
    return e * (1.0 / jnp.sum(e, axis=-1, keepdims=True))


def score_tiles(span):
    size = min(span, SCORE_TILE)
    return [pl.ds(i, size) for i in range(0, span, size)]


def synth_kernel(level, counts, scalars, near, far, first, first_bias, second, second_bias,
                 random, value, mixed_near, mixed_far, whole, rows_a, rows_b, rows_c,
                 mixed_a, mixed_b, mixed_c):
    y = scalars[0]
    rows, mixed = (rows_a, rows_b, rows_c), (mixed_a, mixed_b, mixed_c)
    heads = near.shape[1] // HD
    load_groups(counts, y, near, far, whole, rows)
    for k, span in enumerate((LA, LB, LC)):
        values = mm(rows[k][...], value[...]).astype(bf16)
        by_head = [only_head(values, h) for h in range(heads)]
        for t in score_tiles(span):
            act = None
            if level == 0:
                act = gelu_both(mm(rows[k][t, :], first[...]) + first_bias[...])[0].astype(bf16)
            total = None
            for h in range(heads):
                p = soft(level, h, act, scalars[1 + k], span, second, second_bias, random, t)
                term = mm(p.astype(bf16), by_head[h])
                total = term if total is None else total + term
            mixed[k][t, :] = total.astype(bf16)
    store_groups(counts, y, mixed, whole, mixed_near, mixed_far)


def synth_back_kernel(level, counts, scalars, near, far, d_near, d_far, first, first_bias, second,
                      second_bias, random, value, *refs):
    y = scalars[0]
    if level == 0:
        (dx_near, dx_far, value_grad, second_grad, second_bias_grad, first_grad, first_bias_grad,
         *scratch) = refs
        sums = (value_grad, second_grad, second_bias_grad, first_grad, first_bias_grad)
    else:
        dx_near, dx_far, value_grad, random_out, *scratch = refs
        *scratch, random_grad = scratch
        sums = (value_grad, random_grad)
    whole, dx, *rest = scratch
    rows, d_mixed = rest[:3], rest[3:6]
    d_values = rest[6]
    heads = near.shape[1] // HD
    load_groups(counts, y, near, far, whole, rows)
    load_groups(counts, y, d_near, d_far, whole, d_mixed)
    for s in sums:
        s[...] = jnp.zeros_like(s)
    for k, span in enumerate((LA, LB, LC)):
        values = mm(rows[k][...], value[...]).astype(bf16)
        d_values[:span, :] = jnp.zeros((span, heads * HD), f32)
        for t in score_tiles(span):
            x = rows[k][t, :]
            act = None
            if level == 0:
                act, slope = gelu_both(mm(x, first[...]) + first_bias[...])
                act = act.astype(bf16)
                d_act = None
            dm = d_mixed[k][t, :]
            for h in range(heads):
                p = soft(level, h, act, scalars[1 + k], span, second, second_bias, random, t)
                dm_h = only_head(dm, h)
                dp = mm_nt(dm_h, values)
                d_values[:span, :] += mm_tn(p.astype(bf16), dm_h)
                ds = p * (dp - jnp.sum(p * dp, axis=-1, keepdims=True))
                if level == 0:
                    low = ds.astype(bf16)
                    second_bias_grad[h : h + 1, :span] += jnp.sum(
                        low.astype(f32), axis=0, keepdims=True
                    )
                    second_grad[:, :span] += mm_tn(only_head(act, h), low)
                    term = only_head(mm_nt(low, second[:, :span]), h)
                    d_act = term if d_act is None else d_act + term
                else:
                    random_grad[h, t, :span] += ds
            if level == 0:
                d_pre = (d_act * slope).astype(bf16)
                first_bias_grad[...] += jnp.sum(d_pre.astype(f32), axis=0, keepdims=True)
                first_grad[...] += mm_tn(x, d_pre)
                dx[t, :] = mm_nt(d_pre, first[...])
        d_low = d_values[:span, :].astype(bf16)
        value_grad[...] += mm_tn(rows[k][...], d_low)
        back = mm_nt(d_low, value[...])
        if level == 0:
            back = back + dx[:span, :]
        d_mixed[k][...] = back.astype(bf16)
    store_groups(counts, y, d_mixed, whole, dx_near, dx_far)
    if level == 1:
        random_out[...] = random_grad[...].astype(bf16)


def per_device(
    links,
    tokens_a,
    tokens_b,
    tokens_c,
    lengths_a,
    lengths_b,
    lengths_c,
    cotan_a,
    cotan_b,
    cotan_c,
    ln_gain,
    ln_bias,
    row_bias,
    out_weight,
    up_weight,
    up_bias,
    down_weight,
    synth_first,
    synth_first_bias,
    synth_second,
    synth_second_bias,
    random_scores,
    value_weight,
):
    counts = (tokens_a.shape[0], tokens_b.shape[0], tokens_c.shape[0])
    starts = (0, counts[0], counts[0] + counts[1])
    rows = sum(counts)
    heads = synth_first.shape[0]
    z, x, y, c = links.places()
    nz = links.nz
    n_wide = links.n_wide
    cols = heads * HD
    own_block = links.nc * y + c
    far_block = links.nc * (1 - y) + c
    scalars = jnp.stack([y, lengths_a[0], lengths_b[0], lengths_c[0]]).astype(jnp.int32)

    own_rows = jnp.concatenate([tokens_a, tokens_b, tokens_c, cotan_a, cotan_b, cotan_c], axis=0)
    peer_rows = links.take(own_rows, c=1)
    both = jnp.where(c == 0, jnp.stack([own_rows, peer_rows]), jnp.stack([peer_rows, own_rows]))
    token_rows = both[:, :rows].reshape(2 * rows, D)
    cotan_rows = both[:, rows:].reshape(2 * rows, D)

    def block_lines(block):
        return block * cols + jnp.arange(cols)

    wanted = jnp.concatenate([block_lines(own_block), block_lines(far_block)])
    their_cols = jnp.concatenate(
        [block_lines(links.nc * y + 1 - c), block_lines(links.nc * (1 - y) + 1 - c)]
    )
    out_rows, ff_rows = out_weight.shape[1], up_weight.shape[1]

    def chip_numbers(core):
        iy = (y + jnp.arange(2)) % 2
        ix = (x + jnp.arange(2)) % 2
        iz = (z + jnp.arange(nz)) % nz
        device = links.number(iz[None, None, :], ix[None, :, None], iy[:, None, None], core)
        return (device[..., None] * out_rows + jnp.arange(out_rows)).reshape(-1)

    row_numbers = jnp.concatenate([chip_numbers(c), chip_numbers(1 - c)])
    pick_rows = (wanted[:, None] == row_numbers[None, :]).astype(bf16)
    pick_cols = (jnp.arange(D)[:, None] == wanted[None, :]).astype(bf16)
    places = jnp.concatenate([wanted, their_cols])
    place_cols = (places[:, None] == jnp.arange(D)[None, :]).astype(bf16)

    half_ff = ff_rows // 2
    misc_rows = -(-(out_rows + 1) // 16) * 16

    def misc_pack(level):
        high = up_bias[level].astype(bf16)
        low = (up_bias[level] - high.astype(f32)).astype(bf16)
        line = jnp.pad(jnp.concatenate([high, low])[None], ((0, 0), (0, D - 2 * ff_rows)))
        return jnp.pad(
            jnp.concatenate([out_weight[level], line], axis=0),
            ((0, misc_rows - out_rows - 1), (0, 0)),
        )

    weights = []
    for level in range(LAYERS):
        misc = links.spread_one(misc_pack(level))
        up_blocks = links.spread(up_weight[level])
        down_blocks = links.spread(down_weight[level])
        w_own = misc[:, :, :, :out_rows].reshape(-1, D)
        w_peer = links.take(w_own, c=1)
        w_out = jnp.dot(
            pick_rows, jnp.concatenate([w_own, w_peer]), preferred_element_type=f32
        ).astype(bf16)
        lines = misc[:, :, :, out_rows, : 2 * ff_rows].astype(f32)
        bias = lines[..., :ff_rows] + lines[..., ff_rows:]
        bias_blocks = [
            bias[0, :, :, :half_ff],
            bias[1, :, :, :half_ff],
            bias[:, 0, :, half_ff:],
            bias[:, 1, :, half_ff:],
        ]
        weights.append(
            (
                w_out,
                [w.reshape(-1, D) for w in up_blocks],
                [b.reshape(1, -1) for b in bias_blocks],
                [w.reshape(-1, D) for w in down_blocks],
            )
        )

    same_head = (jnp.arange(cols)[:, None] // HD) == (jnp.arange(cols)[None, :] // HD)

    def diagonal(w):
        return jnp.where(same_head, jnp.tile(w.reshape(cols, HD), (1, heads)), 0).astype(bf16)

    first = diagonal(synth_first)
    first_bias = synth_first_bias.reshape(1, cols)
    second = synth_second.reshape(cols, LC)
    values = [diagonal(value_weight[level]) for level in range(LAYERS)]
    head_weights = [
        (first, first_bias, second, synth_second_bias, first_bias, values[0]),
        (first_bias, first_bias, first_bias, first_bias, random_scores, values[1]),
    ]

    def line(v, level, which):
        return v[level, which][None]

    n = 4
    chip_rows = 2 * rows
    ffn_cols = [w.shape[0] for w in weights[0][1]]
    row_low = ((chip_rows, D), bf16)
    row_high = ((chip_rows, D), f32)
    head_low = ((chip_rows, cols), bf16)
    vector = ((1, D), f32)
    groups = [pltpu.VMEM((4 * k, cols), bf16) for k in counts]
    group_pair = pltpu.VMEM((2, chip_rows, cols), bf16)

    stored = []
    for level in range(LAYERS):
        w_out, up_blocks, bias_blocks, down_blocks = weights[level]
        gain, shift = line(ln_gain, level, 0), line(ln_bias, level, 0)
        if level == 0:
            rows_in = token_rows
            own, far = stage(
                first_norm_kernel, [head_low] * 2, (token_rows, gain, shift, pick_cols)
            )
        else:
            rows_in, own, far = stage(
                next_norm_kernel,
                [row_high, head_low, head_low],
                (resid, ffn, ffn_got, line(row_bias, level - 1, 1), gain, shift, pick_cols),
            )
        got = links.take(far, y=1)
        mixed_own, mixed_far = stage(
            partial(synth_kernel, level, counts),
            [head_low] * 2,
            (scalars, own, got, *head_weights[level]),
            scratch=[group_pair, *groups, *groups],
            smem=1,
        )
        mixed_got = links.take(mixed_far, y=1)
        (part,) = stage(join_kernel, [row_low], (mixed_own, mixed_got, w_out))
        part_got = links.take(part, c=1)
        resid, normed2, ffn, *saved = stage(
            partial(ffn_kernel, n),
            [row_high, row_low, row_low] + [((chip_rows, k), bf16) for k in ffn_cols] * 2,
            (
                rows_in,
                part,
                part_got,
                line(row_bias, level, 0),
                line(ln_gain, level, 1),
                line(ln_bias, level, 1),
                *up_blocks,
                *bias_blocks,
                *down_blocks,
            ),
        )
        ffn_got = links.take(ffn, c=1)
        stored.append((rows_in, own, got, mixed_own, mixed_got, resid, normed2, saved))

    def own_half(whole):
        return lax.dynamic_index_in_dim(whole.reshape(2, rows, D), c, 0, keepdims=False)

    def buckets(mine):
        return [mine[s : s + k] for s, k in zip(starts, counts)]

    last = own_half(resid) + own_half(ffn).astype(f32) + own_half(ffn_got).astype(f32)
    out_parts = buckets((last + row_bias[LAYERS - 1, 1]).astype(bf16))

    stats = [None] * LAYERS
    out_grads, up_grads, bias_grads, down_grads = [], [], [], []
    head_grads = [None] * LAYERS
    grad_rows = cotan_rows
    for level in (1, 0):
        w_out, up_blocks, bias_blocks, down_blocks = weights[level]
        rows_in, own, got, mixed_own, mixed_got, resid, normed2, saved = stored[level]
        d_normed2, ffn_bias_grad, *terms = stage(
            partial(ffn_back_kernel, n),
            [row_low, vector]
            + [((k, D), bf16) for k in ffn_cols] * 2
            + [((1, k), f32) for k in ffn_cols],
            (grad_rows, normed2, *up_blocks, *down_blocks, *saved),
        )
        d_got = links.take(d_normed2, c=1)
        shape = (2, nz, half_ff, D)
        down_grads.insert(0, links.collect([t.reshape(shape) for t in terms[:n]]))
        up_grads.insert(0, links.collect([t.reshape(shape) for t in terms[n : 2 * n]]))
        bias_terms = [t.reshape(2, nz, half_ff) for t in terms[2 * n :]]
        (
            d_resid,
            d_own,
            d_far,
            gain_second,
            shift_second,
            join_bias_grad,
            out_near,
            out_peer,
        ) = stage(
            join_back_kernel,
            [row_high, head_low, head_low, vector, vector, vector]
            + [((D // 2, D), bf16)] * 2,
            (
                grad_rows,
                d_normed2,
                d_got,
                resid,
                line(ln_gain, level, 1),
                w_out,
                mixed_own,
                mixed_got,
                pick_rows,
            ),
            scratch=[pltpu.VMEM((chip_rows, D), bf16)],
        )
        d_mixed_got = links.take(d_far, y=1)

        near = out_near + links.give(out_peer, c=1)
        first_terms = jnp.stack([bias_terms[0], bias_terms[1]])
        second_terms = jnp.stack([bias_terms[2], bias_terms[3]], axis=1)
        bias_line = jnp.pad(
            jnp.concatenate([first_terms, second_terms], axis=-1).astype(bf16)[..., None, :],
            ((0, 0),) * 4 + ((0, D - ff_rows),),
        )
        misc = jnp.concatenate([near.reshape(2, 2, nz, out_rows, D), bias_line], axis=3)
        misc = jnp.pad(misc, ((0, 0),) * 3 + ((0, misc_rows - out_rows - 1), (0, 0)))
        misc = links.collect_one(misc)
        out_grads.insert(0, misc[:out_rows])
        bias_grads.insert(0, misc[out_rows, :ff_rows])

        square = ((cols, cols), f32)
        scratch = [group_pair, pltpu.VMEM((LC, cols), f32), *groups, *groups]
        scratch = scratch + [pltpu.VMEM((LC, cols), f32)]
        if level == 0:
            outs = [square, ((cols, LC), f32), ((heads, LC), f32), square, ((1, cols), f32)]
        else:
            outs = [square, ((heads, LC, LC), bf16)]
            scratch = scratch + [pltpu.VMEM((heads, LC, LC), f32)]
        dx_own, dx_far, *found = stage(
            partial(synth_back_kernel, level, counts),
            [head_low] * 2 + outs,
            (scalars, own, got, d_own, d_mixed_got, *head_weights[level]),
            scratch=scratch,
            smem=1,
        )
        dx_peer = links.take(dx_own, c=1)
        dx_got = links.take(dx_far, y=1)
        dx_peer_got = links.take(dx_got, c=1)
        head_grads[level] = found
        grad_rows, gain_first, shift_first = stage(
            rows_back_kernel,
            [row_high, vector, vector],
            (
                d_resid,
                dx_own,
                dx_got,
                dx_peer,
                dx_peer_got,
                place_cols,
                rows_in,
                line(ln_gain, level, 0),
            ),
        )
        stats[level] = jnp.concatenate(
            [gain_first, gain_second, shift_first, shift_second, join_bias_grad, ffn_bias_grad]
        )

    def blocks(v):
        kept = jnp.where(same_head, v, 0).reshape(cols, heads, HD)
        return jnp.sum(kept, axis=1)

    def by_wide(v):
        return jnp.moveaxis(v.reshape(heads, n_wide, -1, v.shape[-1]), 1, 0)

    value_high, random = head_grads[1]
    random = by_wide(random.reshape(cols * LC // HD, LC)).reshape(n_wide, -1, LC)
    random = links.collect_wide(random, z, x)
    value_low, second_grad, second_bias_grad, first_grad, first_bias_grad = head_grads[0]
    bias_lines = second_bias_grad.reshape(heads, n_wide, 1, -1)
    bias_lines = jnp.pad(
        bias_lines,
        ((0, 0), (0, 0), (0, HD // n_wide - 1), (0, LC - bias_lines.shape[-1])),
    ).reshape(cols, LC)
    pack = jnp.concatenate(
        [
            second_grad,
            bias_lines,
            blocks(first_grad),
            blocks(value_low),
            blocks(value_high),
            first_bias_grad.reshape(cols, 1),
        ],
        axis=1,
    ).astype(bf16)
    pack = jnp.pad(pack, ((0, 0), (0, -pack.shape[1] % 128)))
    pack = by_wide(pack).reshape(n_wide, cols // n_wide, -1)
    pack = links.collect_wide(pack, z, x).reshape(heads, HD // n_wide, -1)
    at = 2 * LC

    summed = links.total(jnp.stack(stats))
    return (
        *out_parts,
        *buckets(own_half(grad_rows)),
        summed[:, 0:2],
        summed[:, 2:4],
        summed[:, 4:6],
        jnp.stack(out_grads),
        jnp.stack(up_grads),
        jnp.stack(bias_grads),
        jnp.stack(down_grads),
        pack[:, :, at : at + HD],
        pack[:, :, at + 3 * HD],
        pack[:, :, :LC],
        pack[:, 0, LC : LC + LC // n_wide],
        random.reshape(heads, -1, LC),
        jnp.stack(
            [pack[:, :, at + HD : at + 2 * HD], pack[:, :, at + 2 * HD : at + 3 * HD]]
        ),
    )


def solution(mesh):
    placed = (
        P(("wide", "head"), None),
        P(("wide", "head"), None),
        P(("wide", "head"), None),
        P("wide"),
        P("wide"),
        P("wide"),
        P(("wide", "head"), None),
        P(("wide", "head"), None),
        P(("wide", "head"), None),
        P(),
        P(),
        P(),
        P(None, ("wide", "head"), None),
        P(None, ("wide", "head"), None),
        P(None, ("wide", "head")),
        P(None, ("wide", "head"), None),
        P("head", None, None),
        P("head", None),
        P("head", None, None),
        P("head", None),
        P("head", None, None),
        P(None, "head", None, None),
    )
    return jax.shard_map(
        partial(per_device, Links(mesh.shape["wide"], mesh.shape["head"])),
        mesh=mesh,
        in_specs=placed,
        out_specs=(
            P(("wide", "head"), None),
            P(("wide", "head"), None),
            P(("wide", "head"), None),
            P(("wide", "head"), None),
            P(("wide", "head"), None),
            P(("wide", "head"), None),
            P(),
            P(),
            P(),
            P(None, ("wide", "head"), None),
            P(None, ("wide", "head"), None),
            P(None, ("wide", "head")),
            P(None, ("wide", "head"), None),
            P("head", "wide", None),
            P("head", "wide"),
            P("head", "wide", None),
            P("head", "wide"),
            P("head", "wide", None),
            P(None, "head", "wide", None),
        ),
        check_vma=False,
    )
```

time: 696 us -> 544 us (0.78)
  matrix products: 159 us -> 5.27 us
  Pallas kernels: 0 us -> 101 us
  local copies, waits for them, and re-layouts: 108 us -> 55 us
  other arithmetic: 95 us -> 45.4 us
  waiting for transfers between devices: 170 us -> 184 us
    dot_general x110 -> x0, matrix products: 145 us -> none  [the longest x8 17 us: per_device(): jnp.einsum('rd,fd->rf', d_ffn, w_down, preferred_element_type=f32)]
    pallas_call x0 -> x16, Pallas kernels: none -> 101 us  [stage(): pl.pallas_call(kernel, out_shape=[jax.ShapeDtypeStruct(s, d) for s, d in...]
    reduce_sum x23 -> x3, other arithmetic: 21.7 us -> 1.9 us  [blocks(): return jnp.sum(kept, axis=1)]
    ppermute x120 -> x122, waiting for transfers between devices: 165 us -> 178 us  [take(): return lax.ppermute(v, AXES, pairs)]
    another operation x49 -> x31, local copies, waits for them, and re-layouts: 25.8 us -> 14.2 us  [the longest x8 7.95 us: per_device(): b.reshape(1, -1)]
    unnamed x580 -> x154, local copies, waits for them, and re-layouts: 22.6 us -> 11.3 us
    concatenate x17 -> x10, other arithmetic: 11.3 us -> 0.49 us  [the longest x6 0.2 us: per_device(): jnp.concatenate([first_terms, second_terms], axis=-1).astype(bf16)]
    sub x3 -> x0, matrix products: 10.3 us -> none  [synth_backward(): d_soft - jnp.sum(softened * d_soft, axis=-1, keepdims=True)]
  transfers between devices with their start and end apart: 122 -> 124, of which waited for: 54 -> 46; matrix products, arithmetic and copies ran while one was open for 49% -> 18% of each run, Pallas kernels for 0% -> 17%
where the time goes in v2:
time: 544 us; the launch traced here: 539 us
  waiting for transfers between devices  184 us (34%)
  starting transfers between devices  144 us (26%)
  Pallas kernels  101 us (19%)
  local copies, waits for them, and re-layouts  55 us (10%)
  other arithmetic  45.4 us (8%)
    ppermute x122, waiting for transfers between devices, take(): return lax.ppermute(v, AXES, pairs)  178 us
    ppermute x122, starting transfers between devices, take(): return lax.ppermute(v, AXES, pairs)  143 us
    pallas_call x16, Pallas kernels, stage(): pl.pallas_call(kernel, out_shape=[jax.ShapeDtypeStruct(s, d) for s, d in...  101 us
    unnamed x154, local copies, waits for them, and re-layouts  11.3 us
  transfers between devices with their start and end apart: 124, of which 46 were waited for; matrix products, arithmetic and copies ran while one was open for 18% of the time, Pallas kernels for 17%

profile of v2, /device:TPU:0, one launch (start us, length us, event | category | flops | bytes accessed | tf_op | source)
XLA Modules:
  0.0 538.7 jit_solution(8447805276767860597)
XLA Ops:
  3.1 3.1 collective-permute-start.5
  6.2 2.6 collective-permute-start.4
  25.8 3.6 collective-permute-start.11
  31.6 2.2 collective-permute-start.27
  33.9 7.0 %collective-permute-done.28 = bf16[1,32,768]{2,1,0:T(8,128)(2,1)S(1)} collective-permute-done((bf16[1,32,768]{2,1,0:T(8,128)(2,1)S(1)}, bf16[1,32,768]{2,1,0:T(8,128)(2,1)S(1)}, u32[]{:S(2)}, u32[]{:S(2)}) %collective-permute-start.28) | collective-permute-done | bytes 49184 | tf_op jit(solution)/shard_map/ppermute | solution.py:62
  41.7 3.4 collective-permute-start.18
  45.2 2.0 collective-permute-start.36
  47.4 2.2 collective-permute-done.19
  49.6 5.1 collective-permute-start.34
  54.7 3.4 collective-permute-done.18
  58.1 6.2 %collective-permute-start.42 = (bf16[1,96,768]{2,1,0:T(8,128)(2,1)S(1)}, bf16[1,96,768]{2,1,0:T(8,128)(2,1)S(1)}, u32[]{:S(2)}, u32[]{:S(2)}) collective-permute-start(bf16[1,96,768]{2,1,0:T(8,128)(2,1)S(1)} %get-tuple-element.252), channel_id=1, source_target_pairs={{16,0},{17,1},{18,2},{19,3},{20,4},{21,5},{22,6},{23,7},{24,8},{25... | collective-permute-start | bytes 442376 | tf_op jit(solution)/shard_map/ppermute | solution.py:62
  64.5 3.8 collective-permute-start.41
  68.3 4.4 collective-permute-done.35
  75.9 4.5 collective-permute-done.6
  87.0 4.0 collective-permute-done.13
  93.6 6.8 %collective-permute-done.7 = bf16[2,4,32,768]{3,2,1,0:T(8,128)(2,1)S(1)} collective-permute-done((bf16[2,4,32,768]{3,2,1,0:T(8,128)(2,1)S(1)}, bf16[2,4,32,768]{3,2,1,0:T(8,128)(2,1)S(1)}, u32[]{:S(2)}, u32[]{:S(2)}) %collective-permute-start.7) | collective-permute-done | bytes 393248 | tf_op jit(solution)/shard_map/ppermute | solution.py:62
  103.9 3.0 shard_map.357
  111.0 13.3 %collective-permute-done.1.far = bf16[448,192]{1,0:T(8,128)(2,1)S(1)} collective-permute-done((bf16[448,192]{1,0:T(8,128)(2,1)}, bf16[448,192]{1,0:T(8,128)(2,1)S(1)}, u32[]{:S(2)}, u32[]{:S(2)}) %collective-permute-start.1) | collective-permute-done | bytes 172064 | tf_op jit(solution)/shard_map/ppermute | solution.py:62
  125.0 6.0 %shard_map.358 = (bf16[448,192]{1,0:T(8,128)(2,1)}, bf16[448,192]{1,0:T(8,128)(2,1)}) custom-call(s32[4]{0:T(128)} %pad_add_fusion.3.scalars, bf16[448,192]{1,0:T(8,128)(2,1)} %get-tuple-element.111.near, bf16[448,192]{1,0:T(8,128)(2,1)} %copy-done.21, bf16[192,192]{1,0:T(8,128)(2,1)} %get-tuple-element.310.first, ...), custom_call_target="tpu_custom_call" | custom-call | bytes 1039872 | tf_op jit(solution)/shard_map/pallas_call | solution.py:138
  132.5 2.5 fusion.8.weight
  135.1 4.8 collective-permute-done.2.far
  140.6 2.7 shard_map.359.part
  148.6 8.8 %shard_map.360 = (f32[448,768]{1,0:T(8,128)}, bf16[448,768]{1,0:T(8,128)(2,1)}, bf16[448,768]{1,0:T(8,128)(2,1)}, bf16[448,384]{1,0:T(8,128)(2,1)}, bf16[448,384...) custom-call(bf16[448,768]{1,0:T(8,128)(2,1)} %bitcast.315, ...), custom_call_target="tpu_custom_call" | custom-call | bytes 12303360 | tf_op jit(solution)/shard_map/pallas_call | solution.py:138
  167.3 3.7 shard_map.361
  174.3 15.6 %collective-permute-done.25.far = bf16[448,192]{1,0:T(8,128)(2,1)S(1)} collective-permute-done((bf16[448,192]{1,0:T(8,128)(2,1)}, bf16[448,192]{1,0:T(8,128)(2,1)S(1)}, u32[]{:S(2)}, u32[]{:S(2)}) %collective-permute-start.25) | collective-permute-done | bytes 172064 | tf_op jit(solution)/shard_map/ppermute | solution.py:62
  190.6 4.2 shard_map.362
  196.4 2.7 fusion.11.weight
  199.2 7.7 %collective-permute-done.26.far = bf16[448,192]{1,0:T(8,128)(2,1)S(1)} collective-permute-done((bf16[448,192]{1,0:T(8,128)(2,1)}, bf16[448,192]{1,0:T(8,128)(2,1)S(1)}, u32[]{:S(2)}, u32[]{:S(2)}) %collective-permute-start.26) | collective-permute-done | bytes 172064 | tf_op jit(solution)/shard_map/ppermute | solution.py:62
  207.6 2.7 shard_map.363.part
  218.0 8.9 %shard_map.364 = (f32[448,768]{1,0:T(8,128)}, bf16[448,768]{1,0:T(8,128)(2,1)}, bf16[448,768]{1,0:T(8,128)(2,1)}, bf16[448,384]{1,0:T(8,128)(2,1)}, bf16[448,384...) custom-call(f32[448,768]{1,0:T(8,128)} %get-tuple-element.117.rows, ...), custom_call_target="tpu_custom_call" | custom-call | bytes 12991488 | tf_op jit(solution)/shard_map/pallas_call | solution.py:138
  227.4 10.5 %shard_map.365 = (bf16[448,768]{1,0:T(8,128)(2,1)}, f32[1,768]{1,0:T(1,128)}, bf16[384,768]{1,0:T(8,128)(2,1)}, bf16[384,768]{1,0:T(8,128)(2,1)}, bf16[384,768]{...) custom-call(bf16[448,768]{1,0:T(8,128)(2,1)} %bitcast.319, ...), custom_call_target="tpu_custom_call" | custom-call | bytes 14263296 | tf_op jit(solution)/shard_map/pallas_call | solution.py:138
  245.1 10.1 %collective-permute-done.91 = bf16[2,4,48,768]{3,2,1,0:T(8,128)(2,1)S(1)} collective-permute-done((bf16[2,4,48,768]{3,2,1,0:T(8,128)(2,1)}, bf16[2,4,48,768]{3,2,1,0:T(8,128)(2,1)S(1)}, u32[]{:S(2)}, u32[]{:S(2)}) %collective-permute-start.91) | collective-permute-done | bytes 589856 | tf_op jit(solution)/shard_map/ppermute | solution.py:62
  259.4 8.0 %collective-permute-done.111 = bf16[2,4,48,768]{3,2,1,0:T(8,128)(2,1)S(1)} collective-permute-done((bf16[2,4,48,768]{3,2,1,0:T(8,128)(2,1)}, bf16[2,4,48,768]{3,2,1,0:T(8,128)(2,1)S(1)}, u32[]{:S(2)}, u32[]{:S(2)}) %collective-permute-start.111) | collective-permute-done | bytes 589856 | tf_op jit(solution)/shard_map/ppermute | solution.py:62
  268.1 3.6 collective-permute-done.106
  274.3 6.0 %shard_map.366 = (f32[448,768]{1,0:T(8,128)}, bf16[448,192]{1,0:T(8,128)(2,1)}, bf16[448,192]{1,0:T(8,128)(2,1)}, f32[1,768]{1,0:T(1,128)}, f32[1,768]{1,0:T(1,1...) custom-call(bf16[448,768]{1,0:T(8,128)(2,1)} %bitcast.320, ...), custom_call_target="tpu_custom_call" | custom-call | bytes 7876608 | tf_op jit(solution)/shard_map/pallas_call | solution.py:138
  283.9 3.7 collective-permute-done.50.d_far
  288.4 7.0 %shard_map.367 = (bf16[448,192]{1,0:T(8,128)(2,1)}, bf16[448,192]{1,0:T(8,128)(2,1)}, f32[192,192]{1,0:T(8,128)}, bf16[3,512,512]{2,1,0:T(8,128)(2,1)}) custom-call(s32[4]{0:T(128)} %pad_add_fusion.3.scalars, bf16[448,192]{1,0:T(8,128)(2,1)} %get-tuple-element.118.near, bf16[448,192]{1,0:T(8,128)(2,1)} %copy-done.20, ...), custom_call_target="tpu_custom_call" | custom-call | bytes 4402176 | tf_op jit(solution)/shard_map/pallas_call | solution.py:138
  299.6 4.4 collective-permute-start.95
  306.7 4.3 collective-permute-start.90
  313.3 3.9 collective-permute-start.115
  317.2 2.5 collective-permute-done.89
  319.7 2.1 collective-permute-start.113
  323.9 3.5 collective-permute-done.114
  329.1 3.5 collective-permute-done.109
  336.4 5.0 shard_map.368
  341.4 10.6 %shard_map.369 = (bf16[448,768]{1,0:T(8,128)(2,1)}, f32[1,768]{1,0:T(1,128)}, bf16[384,768]{1,0:T(8,128)(2,1)}, bf16[384,768]{1,0:T(8,128)(2,1)}, bf16[384,768]{...) custom-call(f32[448,768]{1,0:T(8,128)} %get-tuple-element.139.grad_r, ...), custom_call_target="tpu_custom_call" | custom-call | bytes 14951424 | tf_op jit(solution)/shard_map/pallas_call | solution.py:138
  361.9 18.5 %collective-permute-done.71 = bf16[2,4,32,768]{3,2,1,0:T(8,128)(2,1)S(1)} collective-permute-done((bf16[2,4,32,768]{3,2,1,0:T(8,128)(2,1)S(1)}, bf16[2,4,32,768]{3,2,1,0:T(8,128)(2,1)S(1)}, u32[]{:S(2)}, u32[]{:S(2)}) %collective-permute-start.71) | collective-permute-done | bytes 393248 | tf_op jit(solution)/shard_map/ppermute | solution.py:62
  389.1 5.8 %collective-permute-done.96 = bf16[2,4,48,768]{3,2,1,0:T(8,128)(2,1)S(1)} collective-permute-done((bf16[2,4,48,768]{3,2,1,0:T(8,128)(2,1)S(1)}, bf16[2,4,48,768]{3,2,1,0:T(8,128)(2,1)S(1)}, u32[]{:S(2)}, u32[]{:S(2)}) %collective-permute-start.96) | collective-permute-done | bytes 589856 | tf_op jit(solution)/shard_map/ppermute | solution.py:62
  396.9 3.7 collective-permute-done.72
  402.6 2.1 collective-permute-start.73
  406.1 6.1 %shard_map.370 = (f32[448,768]{1,0:T(8,128)}, bf16[448,192]{1,0:T(8,128)(2,1)}, bf16[448,192]{1,0:T(8,128)(2,1)}, f32[1,768]{1,0:T(1,128)}, f32[1,768]{1,0:T(1,1...) custom-call(f32[448,768]{1,0:T(8,128)} %get-tuple-element.139.grad_rows, ...), custom_call_target="tpu_custom_call" | custom-call | bytes 8564736 | tf_op jit(solution)/shard_map/pallas_call | solution.py:138
  415.9 6.7 %collective-permute-done.55.d_far = bf16[448,192]{1,0:T(8,128)(2,1)S(1)} collective-permute-done((bf16[448,192]{1,0:T(8,128)(2,1)}, bf16[448,192]{1,0:T(8,128)(2,1)S(1)}, u32[]{:S(2)}, u32[]{:S(2)}) %collective-permute-start.55) | collective-permute-done | bytes 172064 | tf_op jit(solution)/shard_map/ppermute | solution.py:62
  423.2 11.1 %shard_map.371 = (bf16[448,192]{1,0:T(8,128)(2,1)}, bf16[448,192]{1,0:T(8,128)(2,1)}, f32[192,192]{1,0:T(8,128)}, f32[192,512]{1,0:T(8,128)}, f32[3,512]{1,0:T(4...) custom-call(s32[4]{0:T(128)} %pad_add_fusion.3.scalars, bf16[448,192]{1,0:T(8,128)(2,1)} %get-tuple-element.111.near, ...), custom_call_target="tpu_custom_call" | custom-call | bytes 2078976 | tf_op jit(solution)/shard_map/pallas_call | solution.py:138
  450.7 3.3 collective-permute-start.85
  458.5 3.6 collective-permute-start.80
  464.2 4.4 collective-permute-start.105
  471.3 3.5 collective-permute-start.100
  474.8 2.4 collective-permute-done.104
  480.0 2.5 collective-permute-done.99
  490.4 2.7 collective-permute-done.118
  499.0 4.8 shard_map.372
  514.7 2.5 collective-permute-done.61
  519.1 3.0 collective-permute-done.62
  523.5 6.3 %collective-permute-done.66 = bf16[4,32,768]{2,1,0:T(8,128)(2,1)S(1)} collective-permute-done((bf16[4,32,768]{2,1,0:T(8,128)(2,1)S(1)}, bf16[4,32,768]{2,1,0:T(8,128)(2,1)S(1)}, u32[]{:S(2)}, u32[]{:S(2)}) %collective-permute-start.66) | collective-permute-done | bytes 196640 | tf_op jit(solution)/shard_map/ppermute | solution.py:62
  (582 shorter events, 201.5 us)
Async XLA Ops:
  3.1 22.7 %collective-permute-start.5 = (bf16[1,32,768]{2,1,0:T(8,128)(2,1)S(1)}, bf16[1,32,768]{2,1,0:T(8,128)(2,1)S(1)}, u32[]{:S(2)}, u32[]{:S(2)}) collective-permute-start(bf16[1,32,768]{2,1,0:T(8,128)(2,1)S(1)} %pad_bitcast_fusion.1), channel_id=1, source_target_pairs={{24,0},{25,1},{26,2},{27,3},{28,4},{29,5},{30,6},{31,7},{0,8},{1,9... | collective-permute-start | bytes 147464 | tf_op jit(solution)/shard_map/ppermute | solution.py:62
  6.2 23.3 %collective-permute-start.4 = (bf16[1,32,768]{2,1,0:T(8,128)(2,1)S(1)}, bf16[1,32,768]{2,1,0:T(8,128)(2,1)S(1)}, u32[]{:S(2)}, u32[]{:S(2)}) collective-permute-start(bf16[1,32,768]{2,1,0:T(8,128)(2,1)S(1)} %pad_bitcast_fusion.1), channel_id=1, source_target_pairs={{16,0},{17,1},{18,2},{19,3},{20,4},{21,5},{22,6},{23,7},{24,8},{25... | collective-permute-start | bytes 147464 | tf_op jit(solution)/shard_map/ppermute | solution.py:62
  8.8 20.9 %collective-permute-start.3 = (bf16[1,32,768]{2,1,0:T(8,128)(2,1)S(1)}, bf16[1,32,768]{2,1,0:T(8,128)(2,1)S(1)}, u32[]{:S(2)}, u32[]{:S(2)}) collective-permute-start(bf16[1,32,768]{2,1,0:T(8,128)(2,1)S(1)} %pad_bitcast_fusion.1), channel_id=1, source_target_pairs={{8,0},{9,1},{10,2},{11,3},{12,4},{13,5},{14,6},{15,7},{16,8},{17,9... | collective-permute-start | bytes 147464 | tf_op jit(solution)/shard_map/ppermute | solution.py:62
  11.1 34.0 %collective-permute-start.12 = (bf16[1,96,768]{2,1,0:T(8,128)(2,1)S(1)}, bf16[1,96,768]{2,1,0:T(8,128)(2,1)S(1)}, u32[]{:S(2)}, u32[]{:S(2)}) collective-permute-start(bf16[1,96,768]{2,1,0:T(8,128)(2,1)S(1)} %get-tuple-element.255), channel_id=1, source_target_pairs={{24,0},{25,1},{26,2},{27,3},{28,4},{29,5},{30,6},{31,7},{0,8},{1,9... | collective-permute-start | bytes 442376 | tf_op jit(solution)/shard_map/ppermute | solution.py:62
  11.9 19.7 %collective-permute-start.29 = (bf16[1,32,768]{2,1,0:T(8,128)(2,1)S(1)}, bf16[1,32,768]{2,1,0:T(8,128)(2,1)S(1)}, u32[]{:S(2)}, u32[]{:S(2)}) collective-permute-start(bf16[1,32,768]{2,1,0:T(8,128)(2,1)S(1)} %pad_bitcast_fusion), channel_id=1, source_target_pairs={{24,0},{25,1},{26,2},{27,3},{28,4},{29,5},{30,6},{31,7},{0,8},{1,9... | collective-permute-start | bytes 147464 | tf_op jit(solution)/shard_map/ppermute | solution.py:62
  25.8 19.4 %collective-permute-start.11 = (bf16[1,96,768]{2,1,0:T(8,128)(2,1)S(1)}, bf16[1,96,768]{2,1,0:T(8,128)(2,1)S(1)}, u32[]{:S(2)}, u32[]{:S(2)}) collective-permute-start(bf16[1,96,768]{2,1,0:T(8,128)(2,1)S(1)} %get-tuple-element.255), channel_id=1, source_target_pairs={{16,0},{17,1},{18,2},{19,3},{20,4},{21,5},{22,6},{23,7},{24,8},{25... | collective-permute-start | bytes 442376 | tf_op jit(solution)/shard_map/ppermute | solution.py:62
  29.5 17.8 %collective-permute-start.10 = (bf16[1,96,768]{2,1,0:T(8,128)(2,1)S(1)}, bf16[1,96,768]{2,1,0:T(8,128)(2,1)S(1)}, u32[]{:S(2)}, u32[]{:S(2)}) collective-permute-start(bf16[1,96,768]{2,1,0:T(8,128)(2,1)S(1)} %get-tuple-element.255), channel_id=1, source_target_pairs={{8,0},{9,1},{10,2},{11,3},{12,4},{13,5},{14,6},{15,7},{16,8},{17,9... | collective-permute-start | bytes 442376 | tf_op jit(solution)/shard_map/ppermute | solution.py:62
  41.7 16.4 %collective-permute-start.18 = (bf16[1,96,768]{2,1,0:T(8,128)(2,1)S(1)}, bf16[1,96,768]{2,1,0:T(8,128)(2,1)S(1)}, u32[]{:S(2)}, u32[]{:S(2)}) collective-permute-start(bf16[1,96,768]{2,1,0:T(8,128)(2,1)S(1)} %get-tuple-element.253), channel_id=1, source_target_pairs={{16,0},{17,1},{18,2},{19,3},{20,4},{21,5},{22,6},{23,7},{24,8},{25... | collective-permute-start | bytes 442376 | tf_op jit(solution)/shard_map/ppermute | solution.py:62
  45.2 13.0 %collective-permute-start.17 = (bf16[1,96,768]{2,1,0:T(8,128)(2,1)S(1)}, bf16[1,96,768]{2,1,0:T(8,128)(2,1)S(1)}, u32[]{:S(2)}, u32[]{:S(2)}) collective-permute-start(bf16[1,96,768]{2,1,0:T(8,128)(2,1)S(1)} %get-tuple-element.253), channel_id=1, source_target_pairs={{8,0},{9,1},{10,2},{11,3},{12,4},{13,5},{14,6},{15,7},{16,8},{17,9... | collective-permute-start | bytes 442376 | tf_op jit(solution)/shard_map/ppermute | solution.py:62
  45.2 19.3 %collective-permute-start.36 = (bf16[1,96,768]{2,1,0:T(8,128)(2,1)S(1)}, bf16[1,96,768]{2,1,0:T(8,128)(2,1)S(1)}, u32[]{:S(2)}, u32[]{:S(2)}) collective-permute-start(bf16[1,96,768]{2,1,0:T(8,128)(2,1)S(1)} %get-tuple-element.254), channel_id=1, source_target_pairs={{24,0},{25,1},{26,2},{27,3},{28,4},{29,5},{30,6},{31,7},{0,8},{1,9... | collective-permute-start | bytes 442376 | tf_op jit(solution)/shard_map/ppermute | solution.py:62
  47.2 25.5 %collective-permute-start.35 = (bf16[1,96,768]{2,1,0:T(8,128)(2,1)S(1)}, bf16[1,96,768]{2,1,0:T(8,128)(2,1)S(1)}, u32[]{:S(2)}, u32[]{:S(2)}) collective-permute-start(bf16[1,96,768]{2,1,0:T(8,128)(2,1)S(1)} %get-tuple-element.254), channel_id=1, source_target_pairs={{16,0},{17,1},{18,2},{19,3},{20,4},{21,5},{22,6},{23,7},{24,8},{25... | collective-permute-start | bytes 442376 | tf_op jit(solution)/shard_map/ppermute | solution.py:62
  49.6 23.2 %collective-permute-start.34 = (bf16[1,96,768]{2,1,0:T(8,128)(2,1)S(1)}, bf16[1,96,768]{2,1,0:T(8,128)(2,1)S(1)}, u32[]{:S(2)}, u32[]{:S(2)}) collective-permute-start(bf16[1,96,768]{2,1,0:T(8,128)(2,1)S(1)} %get-tuple-element.254), channel_id=1, source_target_pairs={{8,0},{9,1},{10,2},{11,3},{12,4},{13,5},{14,6},{15,7},{16,8},{17,9... | collective-permute-start | bytes 442376 | tf_op jit(solution)/shard_map/ppermute | solution.py:62
  58.1 17.3 %collective-permute-start.43 = (bf16[1,96,768]{2,1,0:T(8,128)(2,1)S(1)}, bf16[1,96,768]{2,1,0:T(8,128)(2,1)S(1)}, u32[]{:S(2)}, u32[]{:S(2)}) collective-permute-start(bf16[1,96,768]{2,1,0:T(8,128)(2,1)S(1)} %get-tuple-element.252), channel_id=1, source_target_pairs={{24,0},{25,1},{26,2},{27,3},{28,4},{29,5},{30,6},{31,7},{0,8},{1,9... | collective-permute-start | bytes 442376 | tf_op jit(solution)/shard_map/ppermute | solution.py:62
  58.1 23.9 %collective-permute-start.42 = (bf16[1,96,768]{2,1,0:T(8,128)(2,1)S(1)}, bf16[1,96,768]{2,1,0:T(8,128)(2,1)S(1)}, u32[]{:S(2)}, u32[]{:S(2)}) collective-permute-start(bf16[1,96,768]{2,1,0:T(8,128)(2,1)S(1)} %get-tuple-element.252), channel_id=1, source_target_pairs={{16,0},{17,1},{18,2},{19,3},{20,4},{21,5},{22,6},{23,7},{24,8},{25... | collective-permute-start | bytes 442376 | tf_op jit(solution)/shard_map/ppermute | solution.py:62
  64.5 19.1 %collective-permute-start.41 = (bf16[1,96,768]{2,1,0:T(8,128)(2,1)S(1)}, bf16[1,96,768]{2,1,0:T(8,128)(2,1)S(1)}, u32[]{:S(2)}, u32[]{:S(2)}) collective-permute-start(bf16[1,96,768]{2,1,0:T(8,128)(2,1)S(1)} %get-tuple-element.252), channel_id=1, source_target_pairs={{8,0},{9,1},{10,2},{11,3},{12,4},{13,5},{14,6},{15,7},{16,8},{17,9... | collective-permute-start | bytes 442376 | tf_op jit(solution)/shard_map/ppermute | solution.py:62
  72.7 28.3 %collective-permute-start = (bf16[448,768]{1,0:T(8,128)(2,1)}, bf16[448,768]{1,0:T(8,128)(2,1)S(1)}, u32[]{:S(2)}, u32[]{:S(2)}) collective-permute-start(bf16[448,768]{1,0:T(8,128)(2,1)} %constant_dynamic-update-slice_fusion), channel_id=1, source_target_pairs={{1,0},{0,1},{3,2},{2,3},{5,4},{4,5},{7,6},{6,7},{9,8},{8,9},{11,10... | collective-permute-start | bytes 2064392 | tf_op jit(solution)/shard_map/ppermute | solution.py:62
  83.6 16.8 %collective-permute-start.7 = (bf16[2,4,32,768]{3,2,1,0:T(8,128)(2,1)S(1)}, bf16[2,4,32,768]{3,2,1,0:T(8,128)(2,1)S(1)}, u32[]{:S(2)}, u32[]{:S(2)}) collective-permute-start(bf16[2,4,32,768]{3,2,1,0:T(8,128)(2,1)S(1)} %get-tuple-element.226), channel_id=1, source_target_pairs={{2,0},{3,1},{0,2},{1,3},{6,4},{7,5},{4,6},{5,7},{10,8},{11,9},{8,1... | collective-permute-start | bytes 1179656 | tf_op jit(solution)/shard_map/ppermute | solution.py:62
  85.0 21.8 %collective-permute-start.20 = (bf16[4,48,768]{2,1,0:T(8,128)(2,1)S(1)}, bf16[4,48,768]{2,1,0:T(8,128)(2,1)}, u32[]{:S(2)}, u32[]{:S(2)}) collective-permute-start(bf16[4,48,768]{2,1,0:T(8,128)(2,1)S(1)} %get-tuple-element.219), channel_id=1, source_target_pairs={{4,0},{5,1},{6,2},{7,3},{0,4},{1,5},{2,6},{3,7},{12,8},{13,9},{14,... | collective-permute-start | bytes 884744 | tf_op jit(solution)/shard_map/ppermute | solution.py:62
  91.0 18.4 %collective-permute-start.22 = (bf16[4,48,768]{2,1,0:T(8,128)(2,1)S(1)}, bf16[4,48,768]{2,1,0:T(8,128)(2,1)}, u32[]{:S(2)}, u32[]{:S(2)}) collective-permute-start(bf16[4,48,768]{2,1,0:T(8,128)(2,1)S(1)} %get-tuple-element.218), channel_id=1, source_target_pairs={{2,0},{3,1},{0,2},{1,3},{6,4},{7,5},{4,6},{5,7},{10,8},{11,9},{8,1... | collective-permute-start | bytes 884744 | tf_op jit(solution)/shard_map/ppermute | solution.py:62
  92.6 52.1 %collective-permute-start.14 = (bf16[2,4,48,768]{3,2,1,0:T(8,128)(2,1)S(1)}, bf16[2,4,48,768]{3,2,1,0:T(8,128)(2,1)S(1)}, u32[]{:S(2)}, u32[]{:S(2)}) collective-permute-start(bf16[2,4,48,768]{3,2,1,0:T(8,128)(2,1)S(1)} %pad_maximum_fusion.1), channel_id=1, source_target_pairs={{2,0},{3,1},{0,2},{1,3},{6,4},{7,5},{4,6},{5,7},{10,8},{11,9},{8,1... | collective-permute-start | bytes 1769480 | tf_op jit(solution)/shard_map/ppermute | solution.py:62
  100.4 47.1 %collective-permute-start.16 = (bf16[2,4,48,768]{3,2,1,0:T(8,128)(2,1)S(1)}, bf16[2,4,48,768]{3,2,1,0:T(8,128)(2,1)}, u32[]{:S(2)}, u32[]{:S(2)}) collective-permute-start(bf16[2,4,48,768]{3,2,1,0:T(8,128)(2,1)S(1)} %pad_maximum_fusion.2), channel_id=1, source_target_pairs={{4,0},{5,1},{6,2},{7,3},{0,4},{1,5},{2,6},{3,7},{12,8},{13,9},{14,... | collective-permute-start | bytes 1769480 | tf_op jit(solution)/shard_map/ppermute | solution.py:62
  101.0 29.9 %collective-permute-start.8 = (bf16[384,768]{1,0:T(8,128)(2,1)S(1)}, bf16[384,768]{1,0:T(8,128)(2,1)}, u32[]{:S(2)}, u32[]{:S(2)}) collective-permute-start(bf16[384,768]{1,0:T(8,128)(2,1)S(1)} %bitcast.369), channel_id=1, source_target_pairs={{1,0},{0,1},{3,2},{2,3},{5,4},{4,5},{7,6},{6,7},{9,8},{8,9},{11,10... | collective-permute-start | bytes 1769480 | tf_op jit(solution)/shard_map/ppermute | solution.py:62
  106.8 17.5 %collective-permute-start.1 = (bf16[448,192]{1,0:T(8,128)(2,1)}, bf16[448,192]{1,0:T(8,128)(2,1)S(1)}, u32[]{:S(2)}, u32[]{:S(2)}) collective-permute-start(bf16[448,192]{1,0:T(8,128)(2,1)} %get-tuple-element.112), channel_id=1, source_target_pairs={{2,0},{3,1},{0,2},{1,3},{6,4},{7,5},{4,6},{5,7},{10,8},{11,9},{8,1... | collective-permute-start | bytes 516104 | tf_op jit(solution)/shard_map/ppermute | solution.py:62
  109.4 38.7 %collective-permute-start.21 = (bf16[2,4,48,768]{3,2,1,0:T(8,128)(2,1)S(1)}, bf16[2,4,48,768]{3,2,1,0:T(8,128)(2,1)}, u32[]{:S(2)}, u32[]{:S(2)}) collective-permute-start(bf16[2,4,48,768]{3,2,1,0:T(8,128)(2,1)S(1)} %pad_maximum_fusion.4), channel_id=1, source_target_pairs={{2,0},{3,1},{0,2},{1,3},{6,4},{7,5},{4,6},{5,7},{10,8},{11,9},{8,1... | collective-permute-start | bytes 1769480 | tf_op jit(solution)/shard_map/ppermute | solution.py:62
  124.3 24.3 %collective-permute-start.23 = (bf16[2,4,48,768]{3,2,1,0:T(8,128)(2,1)S(1)}, bf16[2,4,48,768]{3,2,1,0:T(8,128)(2,1)}, u32[]{:S(2)}, u32[]{:S(2)}) collective-permute-start(bf16[2,4,48,768]{3,2,1,0:T(8,128)(2,1)S(1)} %pad_maximum_fusion.5), channel_id=1, source_target_pairs={{4,0},{5,1},{6,2},{7,3},{0,4},{1,5},{2,6},{3,7},{12,8},{13,9},{14,... | collective-permute-start | bytes 1769480 | tf_op jit(solution)/shard_map/ppermute | solution.py:62
  144.7 15.8 %collective-permute-start.31 = (bf16[2,4,32,768]{3,2,1,0:T(8,128)(2,1)}, bf16[2,4,32,768]{3,2,1,0:T(8,128)(2,1)S(1)}, u32[]{:S(2)}, u32[]{:S(2)}) collective-permute-start(bf16[2,4,32,768]{3,2,1,0:T(8,128)(2,1)} %get-tuple-element.224), channel_id=1, source_target_pairs={{2,0},{3,1},{0,2},{1,3},{6,4},{7,5},{4,6},{5,7},{10,8},{11,9},{8,1... | collective-permute-start | bytes 1179656 | tf_op jit(solution)/shard_map/ppermute | solution.py:62
  147.6 15.0 %collective-permute-start.37 = (bf16[4,48,768]{2,1,0:T(8,128)(2,1)}, bf16[4,48,768]{2,1,0:T(8,128)(2,1)}, u32[]{:S(2)}, u32[]{:S(2)}) collective-permute-start(bf16[4,48,768]{2,1,0:T(8,128)(2,1)} %get-tuple-element.215), channel_id=1, source_target_pairs={{4,0},{5,1},{6,2},{7,3},{0,4},{1,5},{2,6},{3,7},{12,8},{13,9},{14,... | collective-permute-start | bytes 884744 | tf_op jit(solution)/shard_map/ppermute | solution.py:62
  148.1 17.0 %collective-permute-start.39 = (bf16[4,48,768]{2,1,0:T(8,128)(2,1)}, bf16[4,48,768]{2,1,0:T(8,128)(2,1)}, u32[]{:S(2)}, u32[]{:S(2)}) collective-permute-start(bf16[4,48,768]{2,1,0:T(8,128)(2,1)} %get-tuple-element.214), channel_id=1, source_target_pairs={{2,0},{3,1},{0,2},{1,3},{6,4},{7,5},{4,6},{5,7},{10,8},{11,9},{8,1... | collective-permute-start | bytes 884744 | tf_op jit(solution)/shard_map/ppermute | solution.py:62
  159.0 12.1 %collective-permute-start.44 = (bf16[4,48,768]{2,1,0:T(8,128)(2,1)}, bf16[4,48,768]{2,1,0:T(8,128)(2,1)}, u32[]{:S(2)}, u32[]{:S(2)}) collective-permute-start(bf16[4,48,768]{2,1,0:T(8,128)(2,1)} %get-tuple-element.211), channel_id=1, source_target_pairs={{4,0},{5,1},{6,2},{7,3},{0,4},{1,5},{2,6},{3,7},{12,8},{13,9},{14,... | collective-permute-start | bytes 884744 | tf_op jit(solution)/shard_map/ppermute | solution.py:62
  161.3 33.5 %collective-permute-start.32 = (bf16[384,768]{1,0:T(8,128)(2,1)}, bf16[384,768]{1,0:T(8,128)(2,1)}, u32[]{:S(2)}, u32[]{:S(2)}) collective-permute-start(bf16[384,768]{1,0:T(8,128)(2,1)} %bitcast.50), channel_id=1, source_target_pairs={{1,0},{0,1},{3,2},{2,3},{5,4},{4,5},{7,6},{6,7},{9,8},{8,9},{11,10... | collective-permute-start | bytes 1769480 | tf_op jit(solution)/shard_map/ppermute | solution.py:62
  165.1 51.8 %collective-permute-start.38 = (bf16[2,4,48,768]{3,2,1,0:T(8,128)(2,1)S(1)}, bf16[2,4,48,768]{3,2,1,0:T(8,128)(2,1)S(1)}, u32[]{:S(2)}, u32[]{:S(2)}) collective-permute-start(bf16[2,4,48,768]{3,2,1,0:T(8,128)(2,1)S(1)} %pad_maximum_fusion.7), channel_id=1, source_target_pairs={{2,0},{3,1},{0,2},{1,3},{6,4},{7,5},{4,6},{5,7},{10,8},{11,9},{8,1... | collective-permute-start | bytes 1769480 | tf_op jit(solution)/shard_map/ppermute | solution.py:62
  166.7 50.2 %collective-permute-start.40 = (bf16[2,4,48,768]{3,2,1,0:T(8,128)(2,1)S(1)}, bf16[2,4,48,768]{3,2,1,0:T(8,128)(2,1)S(1)}, u32[]{:S(2)}, u32[]{:S(2)}) collective-permute-start(bf16[2,4,48,768]{3,2,1,0:T(8,128)(2,1)S(1)} %pad_maximum_fusion.8), channel_id=1, source_target_pairs={{4,0},{5,1},{6,2},{7,3},{0,4},{1,5},{2,6},{3,7},{12,8},{13,9},{14,... | collective-permute-start | bytes 1769480 | tf_op jit(solution)/shard_map/ppermute | solution.py:62
  171.1 18.9 %collective-permute-start.25 = (bf16[448,192]{1,0:T(8,128)(2,1)}, bf16[448,192]{1,0:T(8,128)(2,1)S(1)}, u32[]{:S(2)}, u32[]{:S(2)}) collective-permute-start(bf16[448,192]{1,0:T(8,128)(2,1)} %get-tuple-element.119), channel_id=1, source_target_pairs={{2,0},{3,1},{0,2},{1,3},{6,4},{7,5},{4,6},{5,7},{10,8},{11,9},{8,1... | collective-permute-start | bytes 516104 | tf_op jit(solution)/shard_map/ppermute | solution.py:62
  173.7 43.3 %collective-permute-start.45 = (bf16[2,4,48,768]{3,2,1,0:T(8,128)(2,1)S(1)}, bf16[2,4,48,768]{3,2,1,0:T(8,128)(2,1)}, u32[]{:S(2)}, u32[]{:S(2)}) collective-permute-start(bf16[2,4,48,768]{3,2,1,0:T(8,128)(2,1)S(1)} %pad_maximum_fusion.10), channel_id=1, source_target_pairs={{2,0},{3,1},{0,2},{1,3},{6,4},{7,5},{4,6},{5,7},{10,8},{11,9},{8,1... | collective-permute-start | bytes 1769480 | tf_op jit(solution)/shard_map/ppermute | solution.py:62
  189.9 27.1 %collective-permute-start.47 = (bf16[2,4,48,768]{3,2,1,0:T(8,128)(2,1)S(1)}, bf16[2,4,48,768]{3,2,1,0:T(8,128)(2,1)}, u32[]{:S(2)}, u32[]{:S(2)}) collective-permute-start(bf16[2,4,48,768]{3,2,1,0:T(8,128)(2,1)S(1)} %pad_maximum_fusion.11), channel_id=1, source_target_pairs={{4,0},{5,1},{6,2},{7,3},{0,4},{1,5},{2,6},{3,7},{12,8},{13,9},{14,... | collective-permute-start | bytes 1769480 | tf_op jit(solution)/shard_map/ppermute | solution.py:62
  226.9 53.4 %collective-permute-start.48 = (bf16[448,768]{1,0:T(8,128)(2,1)}, bf16[448,768]{1,0:T(8,128)(2,1)}, u32[]{:S(2)}, u32[]{:S(2)}) collective-permute-start(bf16[448,768]{1,0:T(8,128)(2,1)} %get-tuple-element.123), channel_id=1, source_target_pairs={{1,0},{0,1},{3,2},{2,3},{5,4},{4,5},{7,6},{6,7},{9,8},{8,9},{11,10... | collective-permute-start | bytes 2064392 | tf_op jit(solution)/shard_map/ppermute | solution.py:62
  238.0 35.4 %collective-permute-start.49 = (bf16[448,768]{1,0:T(8,128)(2,1)}, bf16[448,768]{1,0:T(8,128)(2,1)S(1)}, u32[]{:S(2)}, u32[]{:S(2)}) collective-permute-start(bf16[448,768]{1,0:T(8,128)(2,1)} %get-tuple-element.133.part), channel_id=1, source_target_pairs={{1,0},{0,1},{3,2},{2,3},{5,4},{4,5},{7,6},{6,7},{9,8},{8,9},{11,10... | collective-permute-start | bytes 2064392 | tf_op jit(solution)/shard_map/ppermute | solution.py:62
  238.8 16.4 %collective-permute-start.91 = (bf16[2,4,48,768]{3,2,1,0:T(8,128)(2,1)}, bf16[2,4,48,768]{3,2,1,0:T(8,128)(2,1)S(1)}, u32[]{:S(2)}, u32[]{:S(2)}) collective-permute-start(bf16[2,4,48,768]{3,2,1,0:T(8,128)(2,1)} %bitcast.409), channel_id=1, source_target_pairs={{4,0},{5,1},{6,2},{7,3},{0,4},{1,5},{2,6},{3,7},{12,8},{13,9},{14,... | collective-permute-start | bytes 1769480 | tf_op jit(solution)/shard_map/ppermute | solution.py:62
  241.9 16.1 %collective-permute-start.86 = (bf16[2,4,48,768]{3,2,1,0:T(8,128)(2,1)}, bf16[2,4,48,768]{3,2,1,0:T(8,128)(2,1)S(1)}, u32[]{:S(2)}, u32[]{:S(2)}) collective-permute-start(bf16[2,4,48,768]{3,2,1,0:T(8,128)(2,1)} %bitcast.408), channel_id=1, source_target_pairs={{2,0},{3,1},{0,2},{1,3},{6,4},{7,5},{4,6},{5,7},{10,8},{11,9},{8,1... | collective-permute-start | bytes 1769480 | tf_op jit(solution)/shard_map/ppermute | solution.py:62
  243.5 23.9 %collective-permute-start.111 = (bf16[2,4,48,768]{3,2,1,0:T(8,128)(2,1)}, bf16[2,4,48,768]{3,2,1,0:T(8,128)(2,1)S(1)}, u32[]{:S(2)}, u32[]{:S(2)}) collective-permute-start(bf16[2,4,48,768]{3,2,1,0:T(8,128)(2,1)} %bitcast.407), channel_id=1, source_target_pairs={{4,0},{5,1},{6,2},{7,3},{0,4},{1,5},{2,6},{3,7},{12,8},{13,9},{14,... | collective-permute-start | bytes 1769480 | tf_op jit(solution)/shard_map/ppermute | solution.py:62
  255.2 16.5 %collective-permute-start.106 = (bf16[2,4,48,768]{3,2,1,0:T(8,128)(2,1)}, bf16[2,4,48,768]{3,2,1,0:T(8,128)(2,1)S(1)}, u32[]{:S(2)}, u32[]{:S(2)}) collective-permute-start(bf16[2,4,48,768]{3,2,1,0:T(8,128)(2,1)} %bitcast.406), channel_id=1, source_target_pairs={{2,0},{3,1},{0,2},{1,3},{6,4},{7,5},{4,6},{5,7},{10,8},{11,9},{8,1... | collective-permute-start | bytes 1769480 | tf_op jit(solution)/shard_map/ppermute | solution.py:62
  258.0 39.9 %collective-permute-start.92 = (bf16[4,48,768]{2,1,0:T(8,128)(2,1)S(1)}, bf16[4,48,768]{2,1,0:T(8,128)(2,1)S(1)}, u32[]{:S(2)}, u32[]{:S(2)}) collective-permute-start(bf16[4,48,768]{2,1,0:T(8,128)(2,1)S(1)} %slice_bitcast_fusion.8), channel_id=1, source_target_pairs={{2,0},{3,1},{0,2},{1,3},{6,4},{7,5},{4,6},{5,7},{10,8},{11,9},{8,1... | collective-permute-start | bytes 884744 | tf_op jit(solution)/shard_map/ppermute | solution.py:62
  267.4 32.2 %collective-permute-start.87 = (bf16[4,48,768]{2,1,0:T(8,128)(2,1)S(1)}, bf16[4,48,768]{2,1,0:T(8,128)(2,1)S(1)}, u32[]{:S(2)}, u32[]{:S(2)}) collective-permute-start(bf16[4,48,768]{2,1,0:T(8,128)(2,1)S(1)} %slice_bitcast_fusion.10), channel_id=1, source_target_pairs={{4,0},{5,1},{6,2},{7,3},{0,4},{1,5},{2,6},{3,7},{12,8},{13,9},{14,... | collective-permute-start | bytes 884744 | tf_op jit(solution)/shard_map/ppermute | solution.py:62
  271.7 32.3 %collective-permute-start.112 = (bf16[4,48,768]{2,1,0:T(8,128)(2,1)S(1)}, bf16[4,48,768]{2,1,0:T(8,128)(2,1)S(1)}, u32[]{:S(2)}, u32[]{:S(2)}) collective-permute-start(bf16[4,48,768]{2,1,0:T(8,128)(2,1)S(1)} %slice_bitcast_fusion), channel_id=1, source_target_pairs={{2,0},{3,1},{0,2},{1,3},{6,4},{7,5},{4,6},{5,7},{10,8},{11,9},{8,1... | collective-permute-start | bytes 884744 | tf_op jit(solution)/shard_map/ppermute | solution.py:62
  273.4 30.8 %collective-permute-start.107 = (bf16[4,48,768]{2,1,0:T(8,128)(2,1)S(1)}, bf16[4,48,768]{2,1,0:T(8,128)(2,1)S(1)}, u32[]{:S(2)}, u32[]{:S(2)}) collective-permute-start(bf16[4,48,768]{2,1,0:T(8,128)(2,1)S(1)} %slice_bitcast_fusion.2), channel_id=1, source_target_pairs={{4,0},{5,1},{6,2},{7,3},{0,4},{1,5},{2,6},{3,7},{12,8},{13,9},{14,... | collective-permute-start | bytes 884744 | tf_op jit(solution)/shard_map/ppermute | solution.py:62
  287.7 69.4 %collective-permute-start.70 = (bf16[384,768]{1,0:T(8,128)(2,1)}, bf16[384,768]{1,0:T(8,128)(2,1)}, u32[]{:S(2)}, u32[]{:S(2)}) collective-permute-start(bf16[384,768]{1,0:T(8,128)(2,1)} %get-tuple-element.175), channel_id=1, source_target_pairs={{1,0},{0,1},{3,2},{2,3},{5,4},{4,5},{7,6},{6,7},{9,8},{8,9},{11,10... | collective-permute-start | bytes 1769480 | tf_op jit(solution)/shard_map/ppermute | solution.py:62
  297.9 36.2 %collective-permute-start.51 = (bf16[448,192]{1,0:T(8,128)(2,1)S(1)}, bf16[448,192]{1,0:T(8,128)(2,1)S(1)}, u32[]{:S(2)}, u32[]{:S(2)}) collective-permute-start(bf16[448,192]{1,0:T(8,128)(2,1)S(1)} %copy-done.71), channel_id=1, source_target_pairs={{2,0},{3,1},{0,2},{1,3},{6,4},{7,5},{4,6},{5,7},{10,8},{11,9},{8,1... | collective-permute-start | bytes 516104 | tf_op jit(solution)/shard_map/ppermute | solution.py:62
  332.6 27.2 %collective-permute-start.120 = (bf16[4,192,512]{2,1,0:T(8,128)(2,1)}, bf16[4,192,512]{2,1,0:T(8,128)(2,1)S(1)}, u32[]{:S(2)}, u32[]{:S(2)}) collective-permute-start(bf16[4,192,512]{2,1,0:T(8,128)(2,1)} %dynamic-slice_bitcast_fusion), channel_id=1, source_target_pairs={{4,0},{5,1},{6,2},{7,3},{0,4},{1,5},{2,6},{3,7},{12,8},{13,9},{14,... | collective-permute-start | bytes 2359304 | tf_op jit(solution)/shard_map/ppermute | solution.py:62
  352.0 53.6 %collective-permute-start.54 = (bf16[448,768]{1,0:T(8,128)(2,1)}, bf16[448,768]{1,0:T(8,128)(2,1)}, u32[]{:S(2)}, u32[]{:S(2)}) collective-permute-start(bf16[448,768]{1,0:T(8,128)(2,1)} %get-tuple-element.149.part), channel_id=1, source_target_pairs={{1,0},{0,1},{3,2},{2,3},{5,4},{4,5},{7,6},{6,7},{9,8},{8,9},{11,10... | collective-permute-start | bytes 2064392 | tf_op jit(solution)/shard_map/ppermute | solution.py:62
  355.5 25.6 %collective-permute-start.81 = (bf16[2,4,48,768]{3,2,1,0:T(8,128)(2,1)}, bf16[2,4,48,768]{3,2,1,0:T(8,128)(2,1)}, u32[]{:S(2)}, u32[]{:S(2)}) collective-permute-start(bf16[2,4,48,768]{3,2,1,0:T(8,128)(2,1)} %bitcast.405), channel_id=1, source_target_pairs={{4,0},{5,1},{6,2},{7,3},{0,4},{1,5},{2,6},{3,7},{12,8},{13,9},{14,... | collective-permute-start | bytes 1769480 | tf_op jit(solution)/shard_map/ppermute | solution.py:62
  356.4 28.1 %collective-permute-start.76 = (bf16[2,4,48,768]{3,2,1,0:T(8,128)(2,1)}, bf16[2,4,48,768]{3,2,1,0:T(8,128)(2,1)}, u32[]{:S(2)}, u32[]{:S(2)}) collective-permute-start(bf16[2,4,48,768]{3,2,1,0:T(8,128)(2,1)} %bitcast.404), channel_id=1, source_target_pairs={{2,0},{3,1},{0,2},{1,3},{6,4},{7,5},{4,6},{5,7},{10,8},{11,9},{8,1... | collective-permute-start | bytes 1769480 | tf_op jit(solution)/shard_map/ppermute | solution.py:62
  357.1 29.4 %collective-permute-start.101 = (bf16[2,4,48,768]{3,2,1,0:T(8,128)(2,1)}, bf16[2,4,48,768]{3,2,1,0:T(8,128)(2,1)S(1)}, u32[]{:S(2)}, u32[]{:S(2)}) collective-permute-start(bf16[2,4,48,768]{3,2,1,0:T(8,128)(2,1)} %bitcast.403), channel_id=1, source_target_pairs={{4,0},{5,1},{6,2},{7,3},{0,4},{1,5},{2,6},{3,7},{12,8},{13,9},{14,... | collective-permute-start | bytes 1769480 | tf_op jit(solution)/shard_map/ppermute | solution.py:62
  359.7 20.6 %collective-permute-start.71 = (bf16[2,4,32,768]{3,2,1,0:T(8,128)(2,1)S(1)}, bf16[2,4,32,768]{3,2,1,0:T(8,128)(2,1)S(1)}, u32[]{:S(2)}, u32[]{:S(2)}) collective-permute-start(bf16[2,4,32,768]{3,2,1,0:T(8,128)(2,1)S(1)} %fusion.53), channel_id=1, source_target_pairs={{2,0},{3,1},{0,2},{1,3},{6,4},{7,5},{4,6},{5,7},{10,8},{11,9},{8,1... | collective-permute-start | bytes 1179656 | tf_op jit(solution)/shard_map/ppermute | solution.py:62
  380.4 14.5 %collective-permute-start.96 = (bf16[2,4,48,768]{3,2,1,0:T(8,128)(2,1)S(1)}, bf16[2,4,48,768]{3,2,1,0:T(8,128)(2,1)S(1)}, u32[]{:S(2)}, u32[]{:S(2)}) collective-permute-start(bf16[2,4,48,768]{3,2,1,0:T(8,128)(2,1)S(1)} %bitcast.402), channel_id=1, source_target_pairs={{2,0},{3,1},{0,2},{1,3},{6,4},{7,5},{4,6},{5,7},{10,8},{11,9},{8,1... | collective-permute-start | bytes 1769480 | tf_op jit(solution)/shard_map/ppermute | solution.py:62
  381.1 20.1 %collective-permute-start.123 = (bf16[1,192,512]{2,1,0:T(8,128)(2,1)S(1)}, bf16[1,192,512]{2,1,0:T(8,128)(2,1)S(1)}, u32[]{:S(2)}, u32[]{:S(2)}) collective-permute-start(bf16[1,192,512]{2,1,0:T(8,128)(2,1)S(1)} %get-tuple-element.207), channel_id=1, source_target_pairs={{8,0},{9,1},{10,2},{11,3},{12,4},{13,5},{14,6},{15,7},{16,8},{17,9... | collective-permute-start | bytes 589832 | tf_op jit(solution)/shard_map/ppermute | solution.py:62
  384.5 18.1 %collective-permute-start.122 = (bf16[1,192,512]{2,1,0:T(8,128)(2,1)S(1)}, bf16[1,192,512]{2,1,0:T(8,128)(2,1)S(1)}, u32[]{:S(2)}, u32[]{:S(2)}) collective-permute-start(bf16[1,192,512]{2,1,0:T(8,128)(2,1)S(1)} %get-tuple-element.206), channel_id=1, source_target_pairs={{16,0},{17,1},{18,2},{19,3},{20,4},{21,5},{22,6},{23,7},{24,8},{25... | collective-permute-start | bytes 589832 | tf_op jit(solution)/shard_map/ppermute | solution.py:62
  386.5 16.2 %collective-permute-start.121 = (bf16[1,192,512]{2,1,0:T(8,128)(2,1)S(1)}, bf16[1,192,512]{2,1,0:T(8,128)(2,1)S(1)}, u32[]{:S(2)}, u32[]{:S(2)}) collective-permute-start(bf16[1,192,512]{2,1,0:T(8,128)(2,1)S(1)} %get-tuple-element.205), channel_id=1, source_target_pairs={{24,0},{25,1},{26,2},{27,3},{28,4},{29,5},{30,6},{31,7},{0,8},{1,9... | collective-permute-start | bytes 589832 | tf_op jit(solution)/shard_map/ppermute | solution.py:62
  400.5 46.7 %collective-permute-start.82 = (bf16[4,48,768]{2,1,0:T(8,128)(2,1)}, bf16[4,48,768]{2,1,0:T(8,128)(2,1)}, u32[]{:S(2)}, u32[]{:S(2)}) collective-permute-start(bf16[4,48,768]{2,1,0:T(8,128)(2,1)} %slice_bitcast_fusion.12), channel_id=1, source_target_pairs={{2,0},{3,1},{0,2},{1,3},{6,4},{7,5},{4,6},{5,7},{10,8},{11,9},{8,1... | collective-permute-start | bytes 884744 | tf_op jit(solution)/shard_map/ppermute | solution.py:62
  402.6 12.7 %collective-permute-start.73 = (bf16[1,32,768]{2,1,0:T(8,128)(2,1)S(1)}, bf16[1,32,768]{2,1,0:T(8,128)(2,1)S(1)}, u32[]{:S(2)}, u32[]{:S(2)}) collective-permute-start(bf16[1,32,768]{2,1,0:T(8,128)(2,1)S(1)} %get-tuple-element.262), channel_id=1, source_target_pairs={{24,0},{25,1},{26,2},{27,3},{28,4},{29,5},{30,6},{31,7},{0,8},{1,9... | collective-permute-start | bytes 147464 | tf_op jit(solution)/shard_map/ppermute | solution.py:62
  405.6 45.1 %collective-permute-start.77 = (bf16[4,48,768]{2,1,0:T(8,128)(2,1)}, bf16[4,48,768]{2,1,0:T(8,128)(2,1)}, u32[]{:S(2)}, u32[]{:S(2)}) collective-permute-start(bf16[4,48,768]{2,1,0:T(8,128)(2,1)} %slice_bitcast_fusion.14), channel_id=1, source_target_pairs={{4,0},{5,1},{6,2},{7,3},{0,4},{1,5},{2,6},{3,7},{12,8},{13,9},{14,... | collective-permute-start | bytes 884744 | tf_op jit(solution)/shard_map/ppermute | solution.py:62
  412.2 42.8 %collective-permute-start.102 = (bf16[4,48,768]{2,1,0:T(8,128)(2,1)}, bf16[4,48,768]{2,1,0:T(8,128)(2,1)}, u32[]{:S(2)}, u32[]{:S(2)}) collective-permute-start(bf16[4,48,768]{2,1,0:T(8,128)(2,1)} %slice_bitcast_fusion.4), channel_id=1, source_target_pairs={{2,0},{3,1},{0,2},{1,3},{6,4},{7,5},{4,6},{5,7},{10,8},{11,9},{8,1... | collective-permute-start | bytes 884744 | tf_op jit(solution)/shard_map/ppermute | solution.py:62
  413.8 43.1 %collective-permute-start.97 = (bf16[4,48,768]{2,1,0:T(8,128)(2,1)}, bf16[4,48,768]{2,1,0:T(8,128)(2,1)}, u32[]{:S(2)}, u32[]{:S(2)}) collective-permute-start(bf16[4,48,768]{2,1,0:T(8,128)(2,1)} %slice_bitcast_fusion.6), channel_id=1, source_target_pairs={{4,0},{5,1},{6,2},{7,3},{0,4},{1,5},{2,6},{3,7},{12,8},{13,9},{14,... | collective-permute-start | bytes 884744 | tf_op jit(solution)/shard_map/ppermute | solution.py:62
  422.5 86.8 %collective-permute-start.64 = (bf16[384,768]{1,0:T(8,128)(2,1)}, bf16[384,768]{1,0:T(8,128)(2,1)}, u32[]{:S(2)}, u32[]{:S(2)}) collective-permute-start(bf16[384,768]{1,0:T(8,128)(2,1)} %get-tuple-element.169), channel_id=1, source_target_pairs={{1,0},{0,1},{3,2},{2,3},{5,4},{4,5},{7,6},{6,7},{9,8},{8,9},{11,10... | collective-permute-start | bytes 1769480 | tf_op jit(solution)/shard_map/ppermute | solution.py:62
  448.1 41.8 %collective-permute-start.56 = (bf16[448,192]{1,0:T(8,128)(2,1)S(1)}, bf16[448,192]{1,0:T(8,128)(2,1)S(1)}, u32[]{:S(2)}, u32[]{:S(2)}) collective-permute-start(bf16[448,192]{1,0:T(8,128)(2,1)S(1)} %copy-done.70), channel_id=1, source_target_pairs={{2,0},{3,1},{0,2},{1,3},{6,4},{7,5},{4,6},{5,7},{10,8},{11,9},{8,1... | collective-permute-start | bytes 516104 | tf_op jit(solution)/shard_map/ppermute | solution.py:62
  (132 other events, 1081.5 us)
